TPU v7x, 32 devices: a whole 2x2x4 slice. The times are simulated.
32 devices in a mesh: groups: 2 (over x), chan: 8 (over z, y), tm: 2 (over core).
Axes of the slice: x: 2, y: 2, z: 4, core: 2. Of those that a mesh axis runs over, the one named last changes fastest.
Arguments:
- traces: bfloat16 [2048, 2, 1024], P(('groups', 'chan'), 'tm'), parts along dimension 0, may hold values from -6 to 6
- fir_taps: bfloat16 [64], replicated, may hold values from -0.75 to 0.75
- pair_blocks: int32 [64, 2], P(('groups', 'chan')), parts along dimension 0, may hold values from 0 to 7, as said below
- pair_count: int32 [16], P(('groups', 'chan')), parts along dimension 0, may hold values from 1 to 4, as said below
Outputs:
- stacks: float32 [64, 128, 65, 128], P(('groups', 'chan'), 'tm'), parts along dimension 0
There are 2 independent parts, one for each index of `groups`. A program takes and returns all parts, laid end to end along the dimension named above; an argument that names none is the same for every part. Nothing has to cross between parts.
Inputs may be any that keep to these rules, and one draw needn't show every extreme that they name: `pair_blocks`: both blocks of a slot of owner o lie within 2 blocks of o; the first slot of every owner has source max(o - 2, 0) and partner min(o + 2, 7). `pair_count`: some owner uses all its slots.
All inputs are finite; a program needn't handle non-finite values.
Results may differ from a plain program's by a relative error of at most 0.0027.
Values may be sent and summed in bfloat16 or wider, within the bound.
No kernel may reach another device: no remote copies, remote signals or barrier semaphores. Data moves between devices by JAX's collectives and lax.ppermute only.
A program may use at most 128 MiB of HBM per device.

v0:
```python
import jax
import jax.numpy as jnp
from jax import lax
from jax.sharding import PartitionSpec as P

LAG = 32
REACH = 2


def passed_along(block, axis, distance):
    devices = range(lax.axis_size(axis))
    route = [(i - distance, i) for i in devices if i - distance in devices]
    return lax.ppermute(block, axis, route)


def fir_matrix(fir_taps, length):
    first = jnp.arange(length, dtype=jnp.int32)[:, None]
    second = jnp.arange(length, dtype=jnp.int32)[None, :]
    offset = second - first
    picked = fir_taps[jnp.clip(offset, 0, fir_taps.shape[0] - 1)]
    inside = (offset >= 0) & (offset < fir_taps.shape[0])
    return jnp.where(inside, picked, jnp.zeros_like(picked))


def correlate(source_rows, partner_rows, lag):
    padded = jnp.pad(partner_rows, ((0, 0), (0, 0), (lag, lag)))
    result = lax.conv_general_dilated(
        padded,
        source_rows,
        (1,),
        "VALID",
        dimension_numbers=("NCH", "OIH", "NCH"),
        preferred_element_type=jnp.float32,
    )
    return jnp.transpose(result, (1, 2, 0))


def body(traces, fir_taps, pair_blocks, pair_count):
    rows, windows, length = traces.shape
    matrix = fir_matrix(fir_taps, length)
    filtered = jnp.dot(
        traces.reshape(rows * windows, length), matrix, preferred_element_type=jnp.float32
    )
    meansq = jnp.mean(filtered * filtered, axis=-1, keepdims=True)
    unit = (
        (filtered * lax.rsqrt(meansq + 1e-06)).astype(jnp.bfloat16).reshape(rows, windows, length)
    )
    near_list = []
    for offset in range(-REACH, REACH + 1):
        if offset == 0:
            near_list.append(unit)
        else:
            near_list.append(passed_along(unit, "chan", -offset))
    nearby = jnp.stack(near_list, axis=0)
    owner = lax.axis_index("chan")
    all_windows = windows * lax.axis_size("tm")

    def one_slot(slot):
        source_rows = nearby[pair_blocks[slot, 0] - owner + REACH]
        partner_rows = nearby[pair_blocks[slot, 1] - owner + REACH]
        return correlate(source_rows, partner_rows, LAG)

    cap = pair_blocks.shape[0]
    partial_sums = lax.map(one_slot, jnp.arange(cap, dtype=jnp.int32))
    used = jnp.arange(cap, dtype=jnp.int32) < pair_count[0]
    partial_sums = jnp.where(used[:, None, None, None], partial_sums, jnp.zeros_like(partial_sums))
    partial_sums = lax.psum_scatter(partial_sums, "tm", scatter_dimension=1, tiled=True)
    scale = float(all_windows * length) ** (-0.5)
    return partial_sums * scale


def solution(mesh):
    return jax.shard_map(
        body,
        mesh=mesh,
        in_specs=(
            P(("groups", "chan"), "tm", None),
            P(),
            P(("groups", "chan"), None),
            P(("groups", "chan")),
        ),
        out_specs=P(("groups", "chan"), "tm", None, None),
        check_vma=False,
    )
```

profile of v0, /device:TPU:0, one launch (start us, length us, event | category | flops | bytes accessed | tf_op | source)
XLA Modules:
  0.0 227.2 jit_solution(10723750141844342425)
XLA Ops:
  6.5 0.0 copy-start
  6.5 0.0 reduce-scatter.2.cloned.1.call-start
  6.5 2.1 fusion.325
  8.6 2.1 fusion.324
  10.7 2.1 fusion.323
  12.8 1.6 fusion.326
  14.4 0.0 copy-done
  14.4 43.7 %multiply_reduce_fusion = (f32[128]{0:T(128)S(1)}, f32[1024,128]{1,0:T(8,128)S(1)}) fusion(bf16[128,1,1024]{2,0,1:T(8,128)(2,1)S(1)} %copy-done, bf16[]{:T(256)} %bitcast.121, bf16[]{:T(256)} %bitcast.122, bf16[]{:T(256)} %bitcast.123, bf16[]{:T(256)} %bitcast.124, bf16[]{:T(256)} %bitcast.125, bf16[]{:T(256)} %bitcast.127, bf16[]{:T(256)} %bitcast.126, ...), kind=kOutput, calls=%fused_computation.264 | convolution fusion | flops 411303808 | bytes 787072 | tf_op jit(solution)/shard_map/dot_general | solution.py:41
  58.1 4.9 %collective-permute-start = (bf16[128,1,1024]{0,2,1:T(8,128)(2,1)S(1)}, bf16[128,1,1024]{0,2,1:T(8,128)(2,1)S(1)}, u32[]{:S(2)}, u32[]{:S(2)}) collective-permute-start(bf16[128,1,1024]{0,2,1:T(8,128)(2,1)S(1)} %fusion.256), channel_id=1, source_target_pairs={{0,4},{2,6},{4,8},{6,10},{8,12},{10,14},{1,5},{3,7},{5,9},{7,11},{... | collective-permute-start | bytes 786440 | tf_op jit(solution)/shard_map/ppermute | solution.py:13
  63.1 3.4 %collective-permute-start.1 = (bf16[128,1,1024]{0,2,1:T(8,128)(2,1)S(1)}, bf16[128,1,1024]{0,2,1:T(8,128)(2,1)S(1)}, u32[]{:S(2)}, u32[]{:S(2)}) collective-permute-start(bf16[128,1,1024]{0,2,1:T(8,128)(2,1)S(1)} %fusion.256), channel_id=1, source_target_pairs={{0,2},{2,4},{4,6},{6,8},{8,10},{10,12},{12,14},{1,3},{3,5},{5,7},{... | collective-permute-start | bytes 786440 | tf_op jit(solution)/shard_map/ppermute | solution.py:13
  66.5 1.3 collective-permute-start.2
  67.8 1.3 collective-permute-start.3
  69.8 0.0 collective-permute-done
  69.8 7.2 %collective-permute-done.1 = bf16[128,1,1024]{0,2,1:T(8,128)(2,1)S(1)} collective-permute-done((bf16[128,1,1024]{0,2,1:T(8,128)(2,1)S(1)}, bf16[128,1,1024]{0,2,1:T(8,128)(2,1)S(1)}, u32[]{:S(2)}, u32[]{:S(2)}) %collective-permute-start.1) | collective-permute-done | bytes 262176 | tf_op jit(solution)/shard_map/ppermute | solution.py:13
  77.1 0.0 copy-start.1
  77.2 0.0 collective-permute-done.2
  77.2 5.3 %collective-permute-done.3 = bf16[128,1,1024]{0,2,1:T(8,128)(2,1)S(1)} collective-permute-done((bf16[128,1,1024]{0,2,1:T(8,128)(2,1)S(1)}, bf16[128,1,1024]{0,2,1:T(8,128)(2,1)S(1)}, u32[]{:S(2)}, u32[]{:S(2)}) %collective-permute-start.3) | collective-permute-done | bytes 262176 | tf_op jit(solution)/shard_map/ppermute | solution.py:13
  82.5 0.6 copy.10
  83.2 0.0 copy-done.1
  83.2 91.3 %while.14 = (s32[]{:T(128)}, f32[4,128,65,128]{3,1,2,0:T(8,128)}, s32[4]{0:T(128)S(1)}, s32[4,2]{0,1:T(2,128)S(1)}, s32[]{:T(128)}, /*index=5*/bf16[5,128,1,1024]{3,1,2,0:T(8,128)(2,1)S(1)}) while((s32[]{:T(128)}, f32[4,128,65,128]{3,1,2,0:T(8,128)}, s32[4]{0:T(128)S(1)}, s32[4,2]{0,1:T(2,128)S(1)}, s32[]{:T(128)}, ...), condition=%wide.region_2.3_spmd.clone, body=%wide.region_1.2_spmd.sunk.clone | while | flops 2146435072 | bytes 6882051 | solution.py:64
  83.4 0.6 dynamic_slice.48
  85.7 0.6 constant_dynamic-slice_fusion.4
  87.6 0.4 copy.19
  88.0 0.4 copy.20
  88.4 17.8 %bitcast_dynamic-update-slice_fusion.8 = f32[4,128,65,128]{3,1,2,0:T(8,128)} fusion(f32[4,128,65,128]{3,1,2,0:T(8,128)} %get-tuple-element.272, s32[]{:T(128)} %get-tuple-element.271, bf16[128,1,1024]{0,1,2:T(2,128)(2,1)S(1)} %copy.19, bf16[128,1,1024]{0,1,2:T(2,128)(2,1)S(1)} %copy.20), kind=kOutput, calls=%fused_computation.clone.1.clone | convolution fusion | flops 2146435072 | bytes 4784640 | tf_op jit(solution)/shard_map/while/body/eval_jaxpr/transpose | solution.py:35
  106.2 0.6 dynamic_slice.48
  108.5 0.6 constant_dynamic-slice_fusion.4
  110.3 0.4 copy.19
  110.7 0.4 copy.20
  111.1 17.8 %bitcast_dynamic-update-slice_fusion.8 = f32[4,128,65,128]{3,1,2,0:T(8,128)} fusion(f32[4,128,65,128]{3,1,2,0:T(8,128)} %get-tuple-element.272, s32[]{:T(128)} %get-tuple-element.271, bf16[128,1,1024]{0,1,2:T(2,128)(2,1)S(1)} %copy.19, bf16[128,1,1024]{0,1,2:T(2,128)(2,1)S(1)} %copy.20), kind=kOutput, calls=%fused_computation.clone.1.clone | convolution fusion | flops 2146435072 | bytes 4784640 | tf_op jit(solution)/shard_map/while/body/eval_jaxpr/transpose | solution.py:35
  129.0 0.6 dynamic_slice.48
  131.3 0.6 constant_dynamic-slice_fusion.4
  133.1 0.4 copy.19
  133.5 0.4 copy.20
  133.9 17.8 %bitcast_dynamic-update-slice_fusion.8 = f32[4,128,65,128]{3,1,2,0:T(8,128)} fusion(f32[4,128,65,128]{3,1,2,0:T(8,128)} %get-tuple-element.272, s32[]{:T(128)} %get-tuple-element.271, bf16[128,1,1024]{0,1,2:T(2,128)(2,1)S(1)} %copy.19, bf16[128,1,1024]{0,1,2:T(2,128)(2,1)S(1)} %copy.20), kind=kOutput, calls=%fused_computation.clone.1.clone | convolution fusion | flops 2146435072 | bytes 4784640 | tf_op jit(solution)/shard_map/while/body/eval_jaxpr/transpose | solution.py:35
  151.7 0.6 dynamic_slice.48
  154.1 0.6 constant_dynamic-slice_fusion.4
  155.9 0.4 copy.19
  156.3 0.4 copy.20
  156.7 17.8 %bitcast_dynamic-update-slice_fusion.8 = f32[4,128,65,128]{3,1,2,0:T(8,128)} fusion(f32[4,128,65,128]{3,1,2,0:T(8,128)} %get-tuple-element.272, s32[]{:T(128)} %get-tuple-element.271, bf16[128,1,1024]{0,1,2:T(2,128)(2,1)S(1)} %copy.19, bf16[128,1,1024]{0,1,2:T(2,128)(2,1)S(1)} %copy.20), kind=kOutput, calls=%fused_computation.clone.1.clone | convolution fusion | flops 2146435072 | bytes 4784640 | tf_op jit(solution)/shard_map/while/body/eval_jaxpr/transpose | solution.py:35
  174.5 12.1 %broadcast_select_fusion = f32[4,128,65,128]{3,1,2,0:T(8,128)} fusion(f32[4,128,65,128]{3,1,2,0:T(8,128)} %get-tuple-element.103, pred[4]{0:T(512)(128)(4,1)S(1)} %iota_compare_fusion), kind=kLoop, calls=%fused_computation.6 | loop fusion | flops 4259840 | bytes 34078724 | tf_op jit(solution)/shard_map/jit(_where)/select_n | solution.py:66
  186.6 0.0 reduce-scatter.2.cloned.1.call-update
  186.6 24.9 %reduce-scatter.2.cloned.1.call-done = f32[4,64,65,128]{3,1,2,0:T(8,128)} async-done(((f32[4,128,65,128]{3,1,2,0:T(8,128)}), f32[4,64,65,128]{3,1,2,0:T(8,128)}) %reduce-scatter.2.cloned.1.call-update) | async-done | bytes 8519696 | tf_op jit(solution)/shard_map/reduce_scatter | solution.py:67
  211.5 8.9 %broadcast_multiply_fusion = f32[4,64,65,128]{3,1,2,0:T(8,128)} fusion(f32[4,64,65,128]{3,1,2,0:T(8,128)} %reduce-scatter.2.cloned.1.call-done), kind=kLoop, calls=%fused_computation.7 | loop fusion | flops 2129920 | bytes 17039360 | tf_op jit(solution)/shard_map/mul | solution.py:69
  (14 shorter events, 0.4 us)
Async XLA Ops:
  6.5 7.8 %copy-start = (bf16[128,1,1024]{2,0,1:T(8,128)(2,1)S(1)}, bf16[128,1,1024]{2,0,1:T(8,128)(2,1)}, u32[]{:S(2)}) copy-start(bf16[128,1,1024]{2,0,1:T(8,128)(2,1)} %param.6) | copy-start | bytes 786436
  6.5 204.9 %reduce-scatter.2.cloned.1.call-start = ((), (), s32[]{:S(2)}) async-start(), calls=%async_computation.1 | async-start | bytes 25559040 | tf_op jit(solution)/shard_map/reduce_scatter | solution.py:67
  58.1 11.7 %collective-permute-start = (bf16[128,1,1024]{0,2,1:T(8,128)(2,1)S(1)}, bf16[128,1,1024]{0,2,1:T(8,128)(2,1)S(1)}, u32[]{:S(2)}, u32[]{:S(2)}) collective-permute-start(bf16[128,1,1024]{0,2,1:T(8,128)(2,1)S(1)} %fusion.256), channel_id=1, source_target_pairs={{0,4},{2,6},{4,8},{6,10},{8,12},{10,14},{1,5},{3,7},{5,9},{7,11},{... | collective-permute-start | bytes 786440 | tf_op jit(solution)/shard_map/ppermute | solution.py:13
  63.1 14.0 %collective-permute-start.1 = (bf16[128,1,1024]{0,2,1:T(8,128)(2,1)S(1)}, bf16[128,1,1024]{0,2,1:T(8,128)(2,1)S(1)}, u32[]{:S(2)}, u32[]{:S(2)}) collective-permute-start(bf16[128,1,1024]{0,2,1:T(8,128)(2,1)S(1)} %fusion.256), channel_id=1, source_target_pairs={{0,2},{2,4},{4,6},{6,8},{8,10},{10,12},{12,14},{1,3},{3,5},{5,7},{... | collective-permute-start | bytes 786440 | tf_op jit(solution)/shard_map/ppermute | solution.py:13
  66.5 10.6 %collective-permute-start.2 = (bf16[128,1,1024]{0,2,1:T(8,128)(2,1)S(1)}, bf16[128,1,1024]{0,2,1:T(8,128)(2,1)S(1)}, u32[]{:S(2)}, u32[]{:S(2)}) collective-permute-start(bf16[128,1,1024]{0,2,1:T(8,128)(2,1)S(1)} %fusion.256), channel_id=1, source_target_pairs={{2,0},{4,2},{6,4},{8,6},{10,8},{12,10},{14,12},{3,1},{5,3},{7,5},{... | collective-permute-start | bytes 786440 | tf_op jit(solution)/shard_map/ppermute | solution.py:13
  67.8 14.7 %collective-permute-start.3 = (bf16[128,1,1024]{0,2,1:T(8,128)(2,1)S(1)}, bf16[128,1,1024]{0,2,1:T(8,128)(2,1)S(1)}, u32[]{:S(2)}, u32[]{:S(2)}) collective-permute-start(bf16[128,1,1024]{0,2,1:T(8,128)(2,1)S(1)} %fusion.256), channel_id=1, source_target_pairs={{4,0},{6,2},{8,4},{10,6},{12,8},{14,10},{5,1},{7,3},{9,5},{11,7},{... | collective-permute-start | bytes 786440 | tf_op jit(solution)/shard_map/ppermute | solution.py:13
  77.1 6.1 %copy-start.1 = (s32[4,2]{0,1:T(2,128)S(1)}, s32[4,2]{0,1:T(2,128)}, u32[]{:S(2)}) copy-start(s32[4,2]{0,1:T(2,128)} %param.8) | copy-start | bytes 100
Sparse Core Ops, SparseCore 0:
  186.7 24.7 reduce-scatter.1
where the time goes:
time: 228 us; the launch traced here: 227 us
  matrix products  115 us (50%)
  waiting for transfers between devices  37.4 us (16%)
  other arithmetic  21.1 us (9%)
  local copies, waits for them, and re-layouts  16.8 us (7%)
  between operations  14.2 us (6%)
  loops' own time  12 us (5%)
  starting transfers between devices  11 us (5%)
    transpose x4, matrix products, correlate(): return jnp.transpose(result, (1, 2, 0))  71.2 us
    dot_general x1, matrix products, body(): jnp.dot(traces.reshape(rows * windows, length), matrix, preferred_element...  43.7 us
    reduce_scatter x1, waiting for transfers between devices, body(): lax.psum_scatter(partial_sums, 'tm', scatter_dimension=1, tiled=True)  24.9 us
    ppermute x4, waiting for transfers between devices, passed_along(): return lax.ppermute(block, axis, route)  12.5 us
    select_n x1, other arithmetic, body(): jnp.where(used[:, None, None, None], partial_sums, jnp.zeros_like(partial...  12.1 us
    another operation x1, loops' own time, body(): partial_sums = lax.map(one_slot, jnp.arange(cap, dtype=jnp.int32))  12 us
    ppermute x4, starting transfers between devices, passed_along(): return lax.ppermute(block, axis, route)  11 us
    mul x1, other arithmetic, body(): return partial_sums * scale  8.89 us
  transfers between devices with their start and end apart: 5, of which 3 were waited for; matrix products, arithmetic and copies ran while one was open for 0% of the time, Pallas kernels for 0%

commit v1 on v0

v1 whole, which is shorter than its diff:
```python
import functools

import jax
import jax.numpy as jnp
from jax import lax
from jax.experimental import pallas as pl
from jax.experimental.pallas import tpu as pltpu
from jax.sharding import PartitionSpec as P

LAG = 32
REACH = 2
NEAR = 2 * REACH + 1
FINE = 8
COARSE = LAG // FINE
LANES = 128
TILE = 256


def passed_along(block, axis, distance):
    devices = range(lax.axis_size(axis))
    route = [(i - distance, i) for i in devices if i - distance in devices]
    return lax.ppermute(block, axis, route)


def swapped(block, axis):
    return lax.ppermute(block, axis, [(0, 1), (1, 0)])


def shifted(rows, amount):
    if amount == 0:
        return rows
    length = rows.shape[-1]
    moved = pltpu.roll(rows, amount % length, 1)
    edge = slice(0, LANES) if amount > 0 else slice(length - LANES, length)
    lane = lax.broadcasted_iota(jnp.int32, (rows.shape[0], LANES), 1)
    keep = lane >= amount if amount > 0 else lane < LANES + amount
    cut = jnp.where(keep, moved[:, edge], jnp.zeros((), rows.dtype))
    if amount > 0:
        return jnp.concatenate([cut, moved[:, LANES:]], axis=1)
    return jnp.concatenate([moved[:, : length - LANES], cut], axis=1)


def contract_lanes(left, right):
    return lax.dot_general(
        left, right, (((1,), (1,)), ((), ())), preferred_element_type=jnp.float32
    )


def kernel(scale, pairs_ref, count_ref, taps_ref, mine_ref, other_ref, out_ref,
           here_ref, after_ref, unit_ref, left_ref, right_ref):
    slot = pl.program_id(0)
    length = mine_ref.shape[-1]
    half_rows = out_ref.shape[2]

    @pl.when(slot == 0)
    def _():
        taps = taps_ref[...]
        wide = jnp.concatenate(
            [taps, jnp.zeros((1, TILE - taps.shape[1]), jnp.float32)], axis=1
        )
        band = pltpu.roll(
            jnp.broadcast_to(wide, (TILE, TILE)), 0, 1, stride=1, stride_axis=0
        )
        row = lax.broadcasted_iota(jnp.int32, (TILE, TILE), 0)
        column = lax.broadcasted_iota(jnp.int32, (TILE, TILE), 1)
        here_ref[...] = jnp.where(column >= row, band, 0.0).astype(jnp.bfloat16)
        after_ref[...] = jnp.where(column < row, band, 0.0).astype(jnp.bfloat16)

        for window, source in enumerate((mine_ref, other_ref)):
            for block in range(NEAR):
                pieces = []
                for start in range(0, length, TILE):
                    piece = jnp.dot(
                        source[block, :, start : start + TILE], here_ref[...],
                        preferred_element_type=jnp.float32,
                    )
                    if start > 0:
                        piece += jnp.dot(
                            source[block, :, start - TILE : start], after_ref[...],
                            preferred_element_type=jnp.float32,
                        )
                    pieces.append(piece)
                filtered = jnp.concatenate(pieces, axis=1)
                meansq = jnp.mean(filtered * filtered, axis=-1, keepdims=True)
                unit_ref[block, :, window * length : (window + 1) * length] = (
                    filtered * lax.rsqrt(meansq + 1e-06)
                ).astype(jnp.bfloat16)

    owner = lax.axis_index("chan")
    first_row = pl.multiple_of(lax.axis_index("tm") * half_rows, half_rows)
    source = pairs_ref[slot, 0] - owner + REACH
    partner = pairs_ref[slot, 1] - owner + REACH
    factor = jnp.where(slot < count_ref[0], scale, 0.0)
    channels = mine_ref.shape[1]

    for sign in (1, -1):
        for window in range(2):
            span = slice(window * length, (window + 1) * length)
            rows = unit_ref[source, pl.ds(first_row, half_rows), span]
            steps = range(FINE + 1) if sign > 0 else range(-FINE, 0)
            for place, step in enumerate(steps):
                left_ref[place * half_rows : (place + 1) * half_rows, span] = shifted(rows, step)
            rows = unit_ref[partner, :, span]
            for place in range(COARSE):
                right_ref[place * channels : (place + 1) * channels, span] = shifted(
                    rows, -sign * FINE * place
                )
        for pair in range(0, COARSE, 2):
            tall = FINE + 1 if sign > 0 and pair + 2 == COARSE else FINE
            result = contract_lanes(
                left_ref[: tall * half_rows, :],
                right_ref[pair * channels : (pair + 2) * channels, :],
            )
            for within in range(2):
                for place in range(tall):
                    if place == FINE and within == 0:
                        continue
                    coarse = sign * FINE * (pair + within)
                    lag = LAG + coarse + (place if sign > 0 else place - FINE)
                    out_ref[0, lag] = factor * result[
                        place * half_rows : (place + 1) * half_rows,
                        within * channels : (within + 1) * channels,
                    ]


def body(traces, fir_taps, pair_blocks, pair_count):
    rows, windows, length = traces.shape
    block = traces.reshape(rows, length)
    halves = lax.axis_size("tm")
    near = [
        block if offset == 0 else passed_along(block, "chan", -offset)
        for offset in range(-REACH, REACH + 1)
    ]
    mine = jnp.stack(near, axis=0)
    other = swapped(mine, "tm")
    cap = pair_blocks.shape[0]
    lags = 2 * LAG + 1
    half_rows = rows // halves
    scale = float(windows * halves * length) ** (-0.5)
    smem = pl.BlockSpec(memory_space=pltpu.SMEM)
    whole = lambda shape: pl.BlockSpec(shape, lambda slot: (0,) * len(shape))
    result = pl.pallas_call(
        functools.partial(kernel, scale),
        grid=(cap,),
        out_shape=jax.ShapeDtypeStruct((cap, lags, half_rows, rows), jnp.float32),
        in_specs=[
            smem,
            smem,
            whole((1, fir_taps.shape[0])),
            whole(mine.shape),
            whole(mine.shape),
        ],
        out_specs=pl.BlockSpec((1, lags, half_rows, rows), lambda slot: (slot, 0, 0, 0)),
        scratch_shapes=[
            pltpu.VMEM((TILE, TILE), jnp.bfloat16),
            pltpu.VMEM((TILE, TILE), jnp.bfloat16),
            pltpu.VMEM((NEAR, rows, halves * length), jnp.bfloat16),
            pltpu.VMEM(((FINE + 1) * half_rows, halves * length), jnp.bfloat16),
            pltpu.VMEM((COARSE * rows, halves * length), jnp.bfloat16),
        ],
        compiler_params=pltpu.CompilerParams(vmem_limit_bytes=48 * 1024 * 1024),
        cost_estimate=pl.CostEstimate(
            flops=2 * cap * lags * half_rows * rows * halves * length,
            bytes_accessed=cap * lags * half_rows * rows * 4 + 4 * mine.size,
            transcendentals=0,
        ),
    )(pair_blocks, pair_count, fir_taps.astype(jnp.float32)[None, :], mine, other)
    return jnp.transpose(result, (0, 2, 1, 3))


def solution(mesh):
    return jax.shard_map(
        body,
        mesh=mesh,
        in_specs=(
            P(("groups", "chan"), "tm", None),
            P(),
            P(("groups", "chan"), None),
            P(("groups", "chan")),
        ),
        out_specs=P(("groups", "chan"), "tm", None, None),
        check_vma=False,
    )
```

time: 228 us -> 40.1 us (0.18)
  the two profiles are of different devices: /device:TPU:0 before, /device:TPU:17 now
where the time goes in v1:
time: 40.1 us; the launch traced here: 39.9 us
  Pallas kernels  13.9 us (35%)
  starting transfers between devices  12.2 us (30%)
  waiting for transfers between devices  11.9 us (30%)
  local copies, waits for them, and re-layouts  1.14 us (3%)
  between operations  0.74 us (2%)
    pallas_call x1, Pallas kernels, body(): pl.pallas_call(functools.partial(kernel, scale), grid=(cap,), out_shape=j...  13.9 us
    ppermute x4, starting transfers between devices, passed_along(): return lax.ppermute(block, axis, route)  11.6 us
    ppermute x4, waiting for transfers between devices, passed_along(): return lax.ppermute(block, axis, route)  9.99 us
    ppermute x1, waiting for transfers between devices, swapped(): return lax.ppermute(block, axis, [(0, 1), (1, 0)])  1.9 us
    unnamed x9, local copies, waits for them, and re-layouts  1.13 us
  transfers between devices with their start and end apart: 5, of which 3 were waited for; matrix products, arithmetic and copies ran while one was open for 3% of the time, Pallas kernels for 0%

profile of v1, /device:TPU:17, one launch (start us, length us, event | category | flops | bytes accessed | tf_op | source)
XLA Modules:
  0.0 39.9 jit_solution(762144649277013091)
XLA Ops:
  0.0 0.0 copy-start
  0.0 0.0 copy-start.1
  0.0 3.3 %collective-permute-start = (bf16[128,1024]{1,0:T(8,128)(2,1)}, bf16[128,1024]{1,0:T(8,128)(2,1)S(1)}, u32[]{:S(2)}, u32[]{:S(2)}) collective-permute-start(bf16[128,1024]{1,0:T(8,128)(2,1)} %bitcast.15), channel_id=1, source_target_pairs={{0,4},{2,6},{4,8},{6,10},{8,12},{10,14},{1,5},{3,7},{5,9},{7,11},{... | collective-permute-start | bytes 786440 | tf_op jit(solution)/shard_map/ppermute | solution.py:22
  3.3 3.1 %collective-permute-start.1 = (bf16[128,1024]{1,0:T(8,128)(2,1)}, bf16[128,1024]{1,0:T(8,128)(2,1)S(1)}, u32[]{:S(2)}, u32[]{:S(2)}) collective-permute-start(bf16[128,1024]{1,0:T(8,128)(2,1)} %bitcast.16), channel_id=1, source_target_pairs={{0,2},{2,4},{4,6},{6,8},{8,10},{10,12},{12,14},{1,3},{3,5},{5,7},{... | collective-permute-start | bytes 786440 | tf_op jit(solution)/shard_map/ppermute | solution.py:22
  6.5 2.1 %collective-permute-start.3 = (bf16[128,1024]{1,0:T(8,128)(2,1)}, bf16[128,1024]{1,0:T(8,128)(2,1)S(1)}, u32[]{:S(2)}, u32[]{:S(2)}) collective-permute-start(bf16[128,1024]{1,0:T(8,128)(2,1)} %bitcast.17), channel_id=1, source_target_pairs={{4,0},{6,2},{8,4},{10,6},{12,8},{14,10},{5,1},{7,3},{9,5},{11,7},{... | collective-permute-start | bytes 786440 | tf_op jit(solution)/shard_map/ppermute | solution.py:22
  8.6 3.0 %collective-permute-start.2 = (bf16[128,1024]{1,0:T(8,128)(2,1)}, bf16[128,1024]{1,0:T(8,128)(2,1)S(1)}, u32[]{:S(2)}, u32[]{:S(2)}) collective-permute-start(bf16[128,1024]{1,0:T(8,128)(2,1)} %bitcast.18), channel_id=1, source_target_pairs={{2,0},{4,2},{6,4},{8,6},{10,8},{12,10},{14,12},{3,1},{5,3},{7,5},{... | collective-permute-start | bytes 786440 | tf_op jit(solution)/shard_map/ppermute | solution.py:22
  11.6 0.0 collective-permute-done
  11.7 4.4 %collective-permute-done.1 = bf16[128,1024]{1,0:T(8,128)(2,1)S(1)} collective-permute-done((bf16[128,1024]{1,0:T(8,128)(2,1)}, bf16[128,1024]{1,0:T(8,128)(2,1)S(1)}, u32[]{:S(2)}, u32[]{:S(2)}) %collective-permute-start.1) | collective-permute-done | bytes 262176 | tf_op jit(solution)/shard_map/ppermute | solution.py:22
  16.0 1.0 %bitcast_dynamic-update-slice_fusion.2 = bf16[5,128,1024]{2,1,0:T(8,128)(2,1)S(1)} fusion(bf16[5,128,1024]{2,1,0:T(8,128)(2,1)S(1)} %bitcast_dynamic-update-slice_fusion.3, bf16[128,1,1024]{2,0,1:T(8,128)(2,1)} %param.4), kind=kLoop, calls=%fused_computation.2 | loop fusion | bytes 524288
  17.0 5.6 %collective-permute-done.2 = bf16[128,1024]{1,0:T(8,128)(2,1)S(1)} collective-permute-done((bf16[128,1024]{1,0:T(8,128)(2,1)}, bf16[128,1024]{1,0:T(8,128)(2,1)S(1)}, u32[]{:S(2)}, u32[]{:S(2)}) %collective-permute-start.2) | collective-permute-done | bytes 262176 | tf_op jit(solution)/shard_map/ppermute | solution.py:22
  22.7 0.0 collective-permute-done.3
  22.7 0.6 %collective-permute-start.4 = (bf16[5,128,1024]{2,1,0:T(8,128)(2,1)S(1)}, bf16[5,128,1024]{2,1,0:T(8,128)(2,1)S(1)}, u32[]{:S(2)}, u32[]{:S(2)}) collective-permute-start(bf16[5,128,1024]{2,1,0:T(8,128)(2,1)S(1)} %bitcast_dynamic-update-slice_fusion.mine_ref), channel_id=1, source_target_pairs={{0,1},{1,0},{2,3},{3,2},{4,5},{5,4},{6,7},{7,6},{8,9},{9,8},{10,11... | collective-permute-start | bytes 3932168 | tf_op jit(solution)/shard_map/ppermute | solution.py:26
  23.9 0.0 copy-done
  23.9 0.1 copy.5.pairs_ref
  24.0 0.0 copy-done.1
  24.0 1.9 %collective-permute-done.4.other_ref = bf16[5,128,1024]{2,1,0:T(8,128)(2,1)S(1)} collective-permute-done((bf16[5,128,1024]{2,1,0:T(8,128)(2,1)S(1)}, bf16[5,128,1024]{2,1,0:T(8,128)(2,1)S(1)}, u32[]{:S(2)}, u32[]{:S(2)}) %collective-permute-start.4) | collective-permute-done | bytes 1310752 | tf_op jit(solution)/shard_map/ppermute | solution.py:26
  25.9 13.9 %shard_map.46 = f32[4,65,64,128]{3,2,1,0:T(8,128)} custom-call(s32[4,2]{1,0:T(4,128)S(1)} %copy.5.pairs_ref, s32[1]{0:T(128)S(6)} %copy.10.count_ref, f32[1,64]{1,0:T(1,128)S(1)} %bitcast_convert_fusion.taps_ref, bf16[5,128,1024]{2,1,0:T(8,128)(2,1)S(1)} %bitcast_dynamic-update-slice_fusion.mine_ref, bf16[5,128,1024]{2,1,0:T(8,128)(2,1)S(1)} %collective-permute-done.4.other_ref), custom_call_target="tpu_custom_call" | custom-call | flops 8724152320 | bytes 11141120 | tf_op jit(solution)/shard_map/pallas_call | solution.py:142
  (5 shorter events, 0.1 us)
Async XLA Ops:
  0.0 23.9 %copy-start = (s32[4,2]{0,1:T(2,128)S(1)}, s32[4,2]{0,1:T(2,128)}, u32[]{:S(2)}) copy-start(s32[4,2]{0,1:T(2,128)} %param.6) | copy-start | bytes 100
  0.0 24.0 %copy-start.1 = (bf16[64]{0:T(256)(128)(2,1)S(1)}, bf16[64]{0:T(256)(128)(2,1)}, u32[]{:S(2)}) copy-start(bf16[64]{0:T(256)(128)(2,1)} %param.5) | copy-start | bytes 388
  0.0 11.6 %collective-permute-start = (bf16[128,1024]{1,0:T(8,128)(2,1)}, bf16[128,1024]{1,0:T(8,128)(2,1)S(1)}, u32[]{:S(2)}, u32[]{:S(2)}) collective-permute-start(bf16[128,1024]{1,0:T(8,128)(2,1)} %bitcast.15), channel_id=1, source_target_pairs={{0,4},{2,6},{4,8},{6,10},{8,12},{10,14},{1,5},{3,7},{5,9},{7,11},{... | collective-permute-start | bytes 786440 | tf_op jit(solution)/shard_map/ppermute | solution.py:22
  3.3 12.7 %collective-permute-start.1 = (bf16[128,1024]{1,0:T(8,128)(2,1)}, bf16[128,1024]{1,0:T(8,128)(2,1)S(1)}, u32[]{:S(2)}, u32[]{:S(2)}) collective-permute-start(bf16[128,1024]{1,0:T(8,128)(2,1)} %bitcast.16), channel_id=1, source_target_pairs={{0,2},{2,4},{4,6},{6,8},{8,10},{10,12},{12,14},{1,3},{3,5},{5,7},{... | collective-permute-start | bytes 786440 | tf_op jit(solution)/shard_map/ppermute | solution.py:22
  6.5 16.2 %collective-permute-start.3 = (bf16[128,1024]{1,0:T(8,128)(2,1)}, bf16[128,1024]{1,0:T(8,128)(2,1)S(1)}, u32[]{:S(2)}, u32[]{:S(2)}) collective-permute-start(bf16[128,1024]{1,0:T(8,128)(2,1)} %bitcast.17), channel_id=1, source_target_pairs={{4,0},{6,2},{8,4},{10,6},{12,8},{14,10},{5,1},{7,3},{9,5},{11,7},{... | collective-permute-start | bytes 786440 | tf_op jit(solution)/shard_map/ppermute | solution.py:22
  8.6 14.1 %collective-permute-start.2 = (bf16[128,1024]{1,0:T(8,128)(2,1)}, bf16[128,1024]{1,0:T(8,128)(2,1)S(1)}, u32[]{:S(2)}, u32[]{:S(2)}) collective-permute-start(bf16[128,1024]{1,0:T(8,128)(2,1)} %bitcast.18), channel_id=1, source_target_pairs={{2,0},{4,2},{6,4},{8,6},{10,8},{12,10},{14,12},{3,1},{5,3},{7,5},{... | collective-permute-start | bytes 786440 | tf_op jit(solution)/shard_map/ppermute | solution.py:22
  22.7 3.2 %collective-permute-start.4 = (bf16[5,128,1024]{2,1,0:T(8,128)(2,1)S(1)}, bf16[5,128,1024]{2,1,0:T(8,128)(2,1)S(1)}, u32[]{:S(2)}, u32[]{:S(2)}) collective-permute-start(bf16[5,128,1024]{2,1,0:T(8,128)(2,1)S(1)} %bitcast_dynamic-update-slice_fusion.mine_ref), channel_id=1, source_target_pairs={{0,1},{1,0},{2,3},{3,2},{4,5},{5,4},{6,7},{7,6},{8,9},{9,8},{10,11... | collective-permute-start | bytes 3932168 | tf_op jit(solution)/shard_map/ppermute | solution.py:26

commit v2 on v1

--- a/solution.py
+++ b/solution.py
@@ -16,14 +16,26 @@
 TILE = 256
 
 
-def passed_along(block, axis, distance):
-    devices = range(lax.axis_size(axis))
-    route = [(i - distance, i) for i in devices if i - distance in devices]
+def passed(block, axis, target):
+    size = lax.axis_size(axis)
+    route = [(i, target(i)) for i in range(size) if 0 <= target(i) < size]
     return lax.ppermute(block, axis, route)
 
 
-def swapped(block, axis):
-    return lax.ppermute(block, axis, [(0, 1), (1, 0)])
+def partner_of(i):
+    return i + 1 if i % 2 == 0 else i - 1
+
+
+def diagonal_of(i):
+    return i - 1 if i % 2 == 0 else i + 1
+
+
+def place_of(block, owner):
+    offset = block - owner
+    side = jnp.where(offset == 1 - 2 * lax.rem(owner, 2), 3, 4)
+    return jnp.where(
+        offset == 0, 0, jnp.where(offset == -REACH, 1, jnp.where(offset == REACH, 2, side))
+    )
 
 
 def shifted(rows, amount):
@@ -46,10 +58,12 @@
     )
 
 
-def kernel(scale, pairs_ref, count_ref, taps_ref, mine_ref, other_ref, out_ref,
-           here_ref, after_ref, unit_ref, left_ref, right_ref):
+def kernel(scale, pairs_ref, count_ref, taps_ref, *refs):
+    near_refs, (out_ref, here_ref, after_ref, unit_ref, left_ref, right_ref) = (
+        refs[: 2 * NEAR], refs[2 * NEAR :]
+    )
     slot = pl.program_id(0)
-    length = mine_ref.shape[-1]
+    channels, length = near_refs[0].shape
     half_rows = out_ref.shape[2]
 
     @pl.when(slot == 0)
@@ -66,17 +80,18 @@
         here_ref[...] = jnp.where(column >= row, band, 0.0).astype(jnp.bfloat16)
         after_ref[...] = jnp.where(column < row, band, 0.0).astype(jnp.bfloat16)
 
-        for window, source in enumerate((mine_ref, other_ref)):
+        for window in range(2):
             for block in range(NEAR):
+                source = near_refs[window * NEAR + block]
                 pieces = []
                 for start in range(0, length, TILE):
                     piece = jnp.dot(
-                        source[block, :, start : start + TILE], here_ref[...],
+                        source[:, start : start + TILE], here_ref[...],
                         preferred_element_type=jnp.float32,
                     )
                     if start > 0:
                         piece += jnp.dot(
-                            source[block, :, start - TILE : start], after_ref[...],
+                            source[:, start - TILE : start], after_ref[...],
                             preferred_element_type=jnp.float32,
                         )
                     pieces.append(piece)
@@ -88,10 +103,9 @@
 
     owner = lax.axis_index("chan")
     first_row = pl.multiple_of(lax.axis_index("tm") * half_rows, half_rows)
-    source = pairs_ref[slot, 0] - owner + REACH
-    partner = pairs_ref[slot, 1] - owner + REACH
+    source = place_of(pairs_ref[slot, 0], owner)
+    partner = place_of(pairs_ref[slot, 1], owner)
     factor = jnp.where(slot < count_ref[0], scale, 0.0)
-    channels = mine_ref.shape[1]
 
     for sign in (1, -1):
         for window in range(2):
@@ -127,18 +141,20 @@
     rows, windows, length = traces.shape
     block = traces.reshape(rows, length)
     halves = lax.axis_size("tm")
-    near = [
-        block if offset == 0 else passed_along(block, "chan", -offset)
-        for offset in range(-REACH, REACH + 1)
-    ]
-    mine = jnp.stack(near, axis=0)
-    other = swapped(mine, "tm")
+    swap = lambda array: passed(array, "tm", lambda i: 1 - i)
+    other_own = swap(block)
+    diagonal = passed(block, "chan", diagonal_of)
+    below = passed(block, "chan", lambda i: i + REACH)
+    above = passed(block, "chan", lambda i: i - REACH)
+    partner = passed(block, "chan", partner_of)
+    mine = [block, below, above, partner, diagonal]
+    other = [other_own] + [swap(array) for array in mine[1:]]
     cap = pair_blocks.shape[0]
     lags = 2 * LAG + 1
     half_rows = rows // halves
     scale = float(windows * halves * length) ** (-0.5)
     smem = pl.BlockSpec(memory_space=pltpu.SMEM)
-    whole = lambda shape: pl.BlockSpec(shape, lambda slot: (0,) * len(shape))
+    vmem = pl.BlockSpec(memory_space=pltpu.VMEM)
     result = pl.pallas_call(
         functools.partial(kernel, scale),
         grid=(cap,),
@@ -146,9 +162,8 @@
         in_specs=[
             smem,
             smem,
-            whole((1, fir_taps.shape[0])),
-            whole(mine.shape),
-            whole(mine.shape),
+            vmem,
+            *[vmem] * (2 * NEAR),
         ],
         out_specs=pl.BlockSpec((1, lags, half_rows, rows), lambda slot: (slot, 0, 0, 0)),
         scratch_shapes=[
@@ -161,10 +176,10 @@
         compiler_params=pltpu.CompilerParams(vmem_limit_bytes=48 * 1024 * 1024),
         cost_estimate=pl.CostEstimate(
             flops=2 * cap * lags * half_rows * rows * halves * length,
-            bytes_accessed=cap * lags * half_rows * rows * 4 + 4 * mine.size,
+            bytes_accessed=cap * lags * half_rows * rows * 4 + 4 * NEAR * block.size,
             transcendentals=0,
         ),
-    )(pair_blocks, pair_count, fir_taps.astype(jnp.float32)[None, :], mine, other)
+    )(pair_blocks, pair_count, fir_taps.astype(jnp.float32)[None, :], *mine, *other)
     return jnp.transpose(result, (0, 2, 1, 3))
 
 

time: 40.1 us -> 36 us (0.90)
  the two profiles are of different devices: /device:TPU:17 before, /device:TPU:0 now
where the time goes in v2:
time: 36 us; the launch traced here: 35.8 us
  Pallas kernels  14 us (39%)
  starting transfers between devices  13.4 us (37%)
  waiting for transfers between devices  5.3 us (15%)
  local copies, waits for them, and re-layouts  1.71 us (5%)
  between operations  0.73 us (2%)
  other arithmetic  0.66 us (2%)
    pallas_call x1, Pallas kernels, body(): pl.pallas_call(functools.partial(kernel, scale), grid=(cap,), out_shape=j...  14 us
    ppermute x9, starting transfers between devices, passed(): return lax.ppermute(block, axis, route)  13.4 us
    ppermute x9, waiting for transfers between devices, passed(): return lax.ppermute(block, axis, route)  5.3 us
    unnamed x3, local copies, waits for them, and re-layouts  1.71 us
  transfers between devices with their start and end apart: 9, of which 2 were waited for; matrix products, arithmetic and copies ran while one was open for 4% of the time, Pallas kernels for 0%

profile of v2, /device:TPU:0, one launch (start us, length us, event | category | flops | bytes accessed | tf_op | source)
XLA Modules:
  0.0 35.8 jit_solution(17597041122930605423)
XLA Ops:
  0.0 0.7 %collective-permute-start.3 = (bf16[128,1024]{1,0:T(8,128)(2,1)}, bf16[128,1024]{1,0:T(8,128)(2,1)S(1)}, u32[]{:S(2)}, u32[]{:S(2)}) collective-permute-start(bf16[128,1024]{1,0:T(8,128)(2,1)} %bitcast.5), channel_id=1, source_target_pairs={{2,4},{4,2},{6,8},{8,6},{10,12},{12,10},{3,5},{5,3},{7,9},{9,7},{1... | collective-permute-start | bytes 786440 | tf_op jit(solution)/shard_map/ppermute | solution.py:22
  0.7 5.8 %collective-permute-start.2 = (bf16[128,1024]{1,0:T(8,128)(2,1)}, bf16[128,1024]{1,0:T(8,128)(2,1)S(1)}, u32[]{:S(2)}, u32[]{:S(2)}) collective-permute-start(bf16[128,1024]{1,0:T(8,128)(2,1)} %bitcast.6), channel_id=1, source_target_pairs={{0,2},{2,0},{4,6},{6,4},{8,10},{10,8},{12,14},{14,12},{1,3},{3,1},... | collective-permute-start | bytes 786440 | tf_op jit(solution)/shard_map/ppermute | solution.py:22
  6.5 1.3 %collective-permute-start.1 = (bf16[128,1024]{1,0:T(8,128)(2,1)}, bf16[128,1024]{1,0:T(8,128)(2,1)S(1)}, u32[]{:S(2)}, u32[]{:S(2)}) collective-permute-start(bf16[128,1024]{1,0:T(8,128)(2,1)} %bitcast.7), channel_id=1, source_target_pairs={{4,0},{6,2},{8,4},{10,6},{12,8},{14,10},{5,1},{7,3},{9,5},{11,7},{... | collective-permute-start | bytes 786440 | tf_op jit(solution)/shard_map/ppermute | solution.py:22
  7.7 4.6 %collective-permute-start = (bf16[128,1024]{1,0:T(8,128)(2,1)}, bf16[128,1024]{1,0:T(8,128)(2,1)S(1)}, u32[]{:S(2)}, u32[]{:S(2)}) collective-permute-start(bf16[128,1024]{1,0:T(8,128)(2,1)} %bitcast.8), channel_id=1, source_target_pairs={{0,4},{2,6},{4,8},{6,10},{8,12},{10,14},{1,5},{3,7},{5,9},{7,11},{... | collective-permute-start | bytes 786440 | tf_op jit(solution)/shard_map/ppermute | solution.py:22
  12.3 0.1 collective-permute-start.4
  12.4 0.0 collective-permute-done.3.refs_4_
  12.4 0.5 %collective-permute-start.8 = (bf16[128,1024]{1,0:T(8,128)(2,1)S(1)}, bf16[128,1024]{1,0:T(8,128)(2,1)S(1)}, u32[]{:S(2)}, u32[]{:S(2)}) collective-permute-start(bf16[128,1024]{1,0:T(8,128)(2,1)S(1)} %collective-permute-done.3.refs_4_), channel_id=1, source_target_pairs={{0,1},{1,0},{2,3},{3,2},{4,5},{5,4},{6,7},{7,6},{8,9},{9,8},{10,11... | collective-permute-start | bytes 786440 | tf_op jit(solution)/shard_map/ppermute | solution.py:22
  12.9 4.3 %collective-permute-done.2.refs_3_ = bf16[128,1024]{1,0:T(8,128)(2,1)S(1)} collective-permute-done((bf16[128,1024]{1,0:T(8,128)(2,1)}, bf16[128,1024]{1,0:T(8,128)(2,1)S(1)}, u32[]{:S(2)}, u32[]{:S(2)}) %collective-permute-start.2) | collective-permute-done | bytes 262176 | tf_op jit(solution)/shard_map/ppermute | solution.py:22
  17.2 0.0 collective-permute-start.7
  17.3 0.9 %collective-permute-done.1.refs_2_ = bf16[128,1024]{1,0:T(8,128)(2,1)S(1)} collective-permute-done((bf16[128,1024]{1,0:T(8,128)(2,1)}, bf16[128,1024]{1,0:T(8,128)(2,1)S(1)}, u32[]{:S(2)}, u32[]{:S(2)}) %collective-permute-start.1) | collective-permute-done | bytes 262176 | tf_op jit(solution)/shard_map/ppermute | solution.py:22
  18.2 0.0 collective-permute-start.6
  18.2 0.0 collective-permute-done.refs_1_
  18.2 0.5 %collective-permute-start.5 = (bf16[128,1024]{1,0:T(8,128)(2,1)S(1)}, bf16[128,1024]{1,0:T(8,128)(2,1)S(1)}, u32[]{:S(2)}, u32[]{:S(2)}) collective-permute-start(bf16[128,1024]{1,0:T(8,128)(2,1)S(1)} %collective-permute-done.refs_1_), channel_id=1, source_target_pairs={{0,1},{1,0},{2,3},{3,2},{4,5},{5,4},{6,7},{7,6},{8,9},{9,8},{10,11... | collective-permute-start | bytes 786440 | tf_op jit(solution)/shard_map/ppermute | solution.py:22
  19.4 0.8 %copy.5.pairs_ref = s32[4,2]{1,0:T(4,128)S(1)} copy(s32[4,2]{0,1:T(2,128)} %param.6) | data formatting | bytes 64 | tf_op args[2]
  20.1 0.7 %bitcast_convert_fusion.taps_ref = f32[1,64]{1,0:T(1,128)S(1)} fusion(bf16[64]{0:T(256)(128)(2,1)} %param.5), kind=kLoop, calls=%fused_computation | loop fusion | flops 64 | bytes 384 | tf_op jit(solution)/shard_map/broadcast_in_dim | solution.py:182
  20.8 0.0 collective-permute-done.4.refs_5_
  20.8 0.0 collective-permute-done.8.refs_9_
  20.8 0.0 collective-permute-done.7.refs_8_
  20.8 0.0 collective-permute-done.6.refs_7_
  20.8 0.0 collective-permute-done.5.refs_6_
  20.8 0.0 copy-start
  20.8 0.9 %copy-done = bf16[128,1,1024]{2,0,1:T(8,128)(2,1)S(1)} copy-done((bf16[128,1,1024]{2,0,1:T(8,128)(2,1)S(1)}, bf16[128,1,1024]{2,0,1:T(8,128)(2,1)}, u32[]{:S(2)}) %copy-start) | copy-done | bytes 262168
  21.8 14.0 %shard_map.46 = f32[4,65,64,128]{3,2,1,0:T(8,128)} custom-call(s32[4,2]{1,0:T(4,128)S(1)} %copy.5.pairs_ref, s32[1]{0:T(128)S(6)} %copy.6.count_ref, f32[1,64]{1,0:T(1,128)S(1)} %bitcast_convert_fusion.taps_ref, bf16[128,1024]{1,0:T(8,128)(2,1)S(1)} %bitcast.10, bf16[128,1024]{1,0:T(8,128)(2,1)S(1)} %collective-permute-done.refs_1_, ...), custom_call_target="tpu_custom_call" | custom-call | flops 8724152320 | bytes 11141120 | tf_op jit(solution)/shard_map/pallas_call | solution.py:158
Async XLA Ops:
  0.0 12.4 %collective-permute-start.3 = (bf16[128,1024]{1,0:T(8,128)(2,1)}, bf16[128,1024]{1,0:T(8,128)(2,1)S(1)}, u32[]{:S(2)}, u32[]{:S(2)}) collective-permute-start(bf16[128,1024]{1,0:T(8,128)(2,1)} %bitcast.5), channel_id=1, source_target_pairs={{2,4},{4,2},{6,8},{8,6},{10,12},{12,10},{3,5},{5,3},{7,9},{9,7},{1... | collective-permute-start | bytes 786440 | tf_op jit(solution)/shard_map/ppermute | solution.py:22
  0.7 16.6 %collective-permute-start.2 = (bf16[128,1024]{1,0:T(8,128)(2,1)}, bf16[128,1024]{1,0:T(8,128)(2,1)S(1)}, u32[]{:S(2)}, u32[]{:S(2)}) collective-permute-start(bf16[128,1024]{1,0:T(8,128)(2,1)} %bitcast.6), channel_id=1, source_target_pairs={{0,2},{2,0},{4,6},{6,4},{8,10},{10,8},{12,14},{14,12},{1,3},{3,1},... | collective-permute-start | bytes 786440 | tf_op jit(solution)/shard_map/ppermute | solution.py:22
  6.5 11.7 %collective-permute-start.1 = (bf16[128,1024]{1,0:T(8,128)(2,1)}, bf16[128,1024]{1,0:T(8,128)(2,1)S(1)}, u32[]{:S(2)}, u32[]{:S(2)}) collective-permute-start(bf16[128,1024]{1,0:T(8,128)(2,1)} %bitcast.7), channel_id=1, source_target_pairs={{4,0},{6,2},{8,4},{10,6},{12,8},{14,10},{5,1},{7,3},{9,5},{11,7},{... | collective-permute-start | bytes 786440 | tf_op jit(solution)/shard_map/ppermute | solution.py:22
  7.7 10.5 %collective-permute-start = (bf16[128,1024]{1,0:T(8,128)(2,1)}, bf16[128,1024]{1,0:T(8,128)(2,1)S(1)}, u32[]{:S(2)}, u32[]{:S(2)}) collective-permute-start(bf16[128,1024]{1,0:T(8,128)(2,1)} %bitcast.8), channel_id=1, source_target_pairs={{0,4},{2,6},{4,8},{6,10},{8,12},{10,14},{1,5},{3,7},{5,9},{7,11},{... | collective-permute-start | bytes 786440 | tf_op jit(solution)/shard_map/ppermute | solution.py:22
  12.3 8.5 %collective-permute-start.4 = (bf16[128,1024]{1,0:T(8,128)(2,1)}, bf16[128,1024]{1,0:T(8,128)(2,1)S(1)}, u32[]{:S(2)}, u32[]{:S(2)}) collective-permute-start(bf16[128,1024]{1,0:T(8,128)(2,1)} %bitcast.9), channel_id=1, source_target_pairs={{0,1},{1,0},{2,3},{3,2},{4,5},{5,4},{6,7},{7,6},{8,9},{9,8},{10,11... | collective-permute-start | bytes 786440 | tf_op jit(solution)/shard_map/ppermute | solution.py:22
  12.4 8.4 %collective-permute-start.8 = (bf16[128,1024]{1,0:T(8,128)(2,1)S(1)}, bf16[128,1024]{1,0:T(8,128)(2,1)S(1)}, u32[]{:S(2)}, u32[]{:S(2)}) collective-permute-start(bf16[128,1024]{1,0:T(8,128)(2,1)S(1)} %collective-permute-done.3.refs_4_), channel_id=1, source_target_pairs={{0,1},{1,0},{2,3},{3,2},{4,5},{5,4},{6,7},{7,6},{8,9},{9,8},{10,11... | collective-permute-start | bytes 786440 | tf_op jit(solution)/shard_map/ppermute | solution.py:22
  17.2 3.6 %collective-permute-start.7 = (bf16[128,1024]{1,0:T(8,128)(2,1)S(1)}, bf16[128,1024]{1,0:T(8,128)(2,1)S(1)}, u32[]{:S(2)}, u32[]{:S(2)}) collective-permute-start(bf16[128,1024]{1,0:T(8,128)(2,1)S(1)} %collective-permute-done.2.refs_3_), channel_id=1, source_target_pairs={{0,1},{1,0},{2,3},{3,2},{4,5},{5,4},{6,7},{7,6},{8,9},{9,8},{10,11... | collective-permute-start | bytes 786440 | tf_op jit(solution)/shard_map/ppermute | solution.py:22
  18.2 2.6 %collective-permute-start.6 = (bf16[128,1024]{1,0:T(8,128)(2,1)S(1)}, bf16[128,1024]{1,0:T(8,128)(2,1)S(1)}, u32[]{:S(2)}, u32[]{:S(2)}) collective-permute-start(bf16[128,1024]{1,0:T(8,128)(2,1)S(1)} %collective-permute-done.1.refs_2_), channel_id=1, source_target_pairs={{0,1},{1,0},{2,3},{3,2},{4,5},{5,4},{6,7},{7,6},{8,9},{9,8},{10,11... | collective-permute-start | bytes 786440 | tf_op jit(solution)/shard_map/ppermute | solution.py:22
  18.2 2.6 %collective-permute-start.5 = (bf16[128,1024]{1,0:T(8,128)(2,1)S(1)}, bf16[128,1024]{1,0:T(8,128)(2,1)S(1)}, u32[]{:S(2)}, u32[]{:S(2)}) collective-permute-start(bf16[128,1024]{1,0:T(8,128)(2,1)S(1)} %collective-permute-done.refs_1_), channel_id=1, source_target_pairs={{0,1},{1,0},{2,3},{3,2},{4,5},{5,4},{6,7},{7,6},{8,9},{9,8},{10,11... | collective-permute-start | bytes 786440 | tf_op jit(solution)/shard_map/ppermute | solution.py:22
  20.8 1.0 %copy-start = (bf16[128,1,1024]{2,0,1:T(8,128)(2,1)S(1)}, bf16[128,1,1024]{2,0,1:T(8,128)(2,1)}, u32[]{:S(2)}) copy-start(bf16[128,1,1024]{2,0,1:T(8,128)(2,1)} %param.4) | copy-start | bytes 786436

commit v3 on v2

v3 whole, which is shorter than its diff:
```python
import functools

import jax
import jax.numpy as jnp
from jax import lax
from jax.experimental import pallas as pl
from jax.experimental.pallas import tpu as pltpu
from jax.sharding import PartitionSpec as P

LAG = 32
REACH = 2
NEAR = 2 * REACH + 1
FINE = 8
COARSE = LAG // FINE
LANES = 128
TILE = 256
CHUNKS = 4
OWN, PARTNER, BELOW, ABOVE, DIAGONAL = range(NEAR)


def passed(block, axis, target):
    size = lax.axis_size(axis)
    route = [(i, target(i)) for i in range(size) if 0 <= target(i) < size]
    return lax.ppermute(block, axis, route)


def partner_of(i):
    return i + 1 if i % 2 == 0 else i - 1


def diagonal_of(i):
    return i - 1 if i % 2 == 0 else i + 1


def place_of(block, owner):
    offset = block - owner
    side = jnp.where(offset == 1 - 2 * lax.rem(owner, 2), PARTNER, DIAGONAL)
    away = jnp.where(offset == -REACH, BELOW, jnp.where(offset == REACH, ABOVE, side))
    return jnp.where(offset == 0, OWN, away)


def shifted(rows, amount):
    if amount == 0:
        return rows
    length = rows.shape[-1]
    moved = pltpu.roll(rows, amount % length, 1)
    edge = slice(0, LANES) if amount > 0 else slice(length - LANES, length)
    lane = lax.broadcasted_iota(jnp.int32, (rows.shape[0], LANES), 1)
    keep = lane >= amount if amount > 0 else lane < LANES + amount
    cut = jnp.where(keep, moved[:, edge], jnp.zeros((), rows.dtype))
    if amount > 0:
        return jnp.concatenate([cut, moved[:, LANES:]], axis=1)
    return jnp.concatenate([moved[:, : length - LANES], cut], axis=1)


def contract_lanes(left, right):
    return lax.dot_general(
        left, right, (((1,), (1,)), ((), ())), preferred_element_type=jnp.float32
    )


def make_band(taps_ref, band_ref):
    taps = taps_ref[...]
    wide = jnp.concatenate([taps, jnp.zeros((1, TILE - taps.shape[1]), jnp.float32)], axis=1)
    band = pltpu.roll(jnp.broadcast_to(wide, (TILE, TILE)), 0, 1, stride=1, stride_axis=0)
    row = lax.broadcasted_iota(jnp.int32, (TILE, TILE), 0)
    column = lax.broadcasted_iota(jnp.int32, (TILE, TILE), 1)
    band_ref[0] = jnp.where(column >= row, band, 0.0).astype(jnp.bfloat16)
    band_ref[1] = jnp.where(column < row, band, 0.0).astype(jnp.bfloat16)


def normalise(source_ref, band_ref, unit_ref, place, window):
    length = source_ref.shape[-1]
    pieces = []
    for start in range(0, length, TILE):
        piece = jnp.dot(
            source_ref[:, start : start + TILE], band_ref[0], preferred_element_type=jnp.float32
        )
        if start > 0:
            piece += jnp.dot(
                source_ref[:, start - TILE : start], band_ref[1],
                preferred_element_type=jnp.float32,
            )
        pieces.append(piece)
    filtered = jnp.concatenate(pieces, axis=1)
    meansq = jnp.mean(filtered * filtered, axis=-1, keepdims=True)
    unit_ref[place, :, window * length : (window + 1) * length] = (
        filtered * lax.rsqrt(meansq + 1e-06)
    ).astype(jnp.bfloat16)


def correlate(slot, scale, pairs_ref, count_ref, unit_ref, left_ref, right_ref, stage_ref,
              out_ref, sems):
    _, channels, both = unit_ref.shape
    half_rows = stage_ref.shape[1]
    length = both // 2
    owner = lax.axis_index("chan")
    first_row = pl.multiple_of(lax.axis_index("tm") * half_rows, half_rows)
    source = place_of(pairs_ref[0, slot], owner)
    partner = place_of(pairs_ref[1, slot], owner)
    factor = jnp.where(slot < count_ref[0], scale, 0.0)
    copies = []
    for sign in (1, -1):
        for window in range(2):
            span = slice(window * length, (window + 1) * length)
            rows = unit_ref[source, pl.ds(first_row, half_rows), span]
            for place in range(FINE + 1 if sign > 0 else FINE):
                step = place if sign > 0 else place - FINE
                left_ref[place * half_rows : (place + 1) * half_rows, span] = shifted(rows, step)
            rows = unit_ref[partner, :, span]
            for place in range(COARSE):
                right_ref[place * channels : (place + 1) * channels, span] = shifted(
                    rows, -sign * FINE * place
                )
        for pair in range(0, COARSE, 2):
            tall = FINE + 1 if sign > 0 and pair + 2 == COARSE else FINE
            result = contract_lanes(
                left_ref[: tall * half_rows, :],
                right_ref[pair * channels : (pair + 2) * channels, :],
            )
            lags = []
            for within in range(2):
                for place in range(tall):
                    if place == FINE and within == 0:
                        continue
                    coarse = sign * FINE * (pair + within)
                    lag = LAG + coarse + (place if sign > 0 else place - FINE)
                    stage_ref[lag] = factor * result[
                        place * half_rows : (place + 1) * half_rows,
                        within * channels : (within + 1) * channels,
                    ]
                    lags.append(lag)
            span = pl.ds(min(lags), len(lags))
            copy = pltpu.make_async_copy(
                stage_ref.at[span], out_ref.at[slot, span], sems.at[len(copies)]
            )
            copy.start()
            copies.append(copy)
    return copies


def early_kernel(taps_ref, *refs):
    blocks, (band_ref, unit_ref) = refs[:4], refs[4:]
    make_band(taps_ref, band_ref)
    for place in range(2):
        for window in range(2):
            normalise(blocks[2 * place + window], band_ref, unit_ref, OWN + place, window)


def stage_kernel(scale, slots, places, pairs_ref, count_ref, band_ref, *refs):
    blocks = refs[: 2 * len(places)]
    refs = refs[2 * len(places) :]
    refs = refs[1:] if len(slots) == 1 else refs[2:]
    unit_ref, out_ref, left_ref, right_ref, stage_ref, sems = refs
    for index, place in enumerate(places):
        for window in range(2):
            normalise(blocks[2 * index + window], band_ref, unit_ref, place, window)
    copies = []
    for index, slot in enumerate(slots):
        copies += correlate(
            slot, scale, pairs_ref, count_ref, unit_ref, left_ref, right_ref,
            stage_ref.at[index], out_ref, sems.at[index],
        )
    for copy in copies:
        copy.wait()


def body(traces, fir_taps, pair_blocks, pair_count):
    rows, windows, length = traces.shape
    block = traces.reshape(rows, length)
    halves = lax.axis_size("tm")
    cap = pair_blocks.shape[0]
    lags = 2 * LAG + 1
    half_rows = rows // halves
    scale = float(windows * halves * length) ** (-0.5)

    swap = lambda array: passed(array, "tm", lambda i: 1 - i)
    partner = passed(block, "chan", partner_of)
    below = passed(block, "chan", lambda i: i + REACH)
    above = passed(block, "chan", lambda i: i - REACH)
    diagonal = passed(block, "chan", diagonal_of)
    own, taps, pairs, count = lax.optimization_barrier(
        (block, fir_taps.astype(jnp.float32)[None, :], pair_blocks.T, pair_count)
    )

    smem = pl.BlockSpec(memory_space=pltpu.SMEM)
    vmem = pl.BlockSpec(memory_space=pltpu.VMEM)
    hbm = pl.BlockSpec(memory_space=pl.ANY)
    params = pltpu.CompilerParams(vmem_limit_bytes=40 * 1024 * 1024)
    band_shape = jax.ShapeDtypeStruct((2, TILE, TILE), jnp.bfloat16)
    unit_shape = jax.ShapeDtypeStruct((NEAR, rows, halves * length), jnp.bfloat16)
    out_shape = jax.ShapeDtypeStruct((cap, lags, half_rows, rows), jnp.float32)

    def cost(blocks, slots):
        return pl.CostEstimate(
            flops=blocks * 2 * 2 * rows * length * 2 * TILE
            + slots * 2 * lags * half_rows * rows * halves * length,
            bytes_accessed=slots * lags * half_rows * rows * 4,
            transcendentals=0,
        )

    def stage(slots, places, blocks, band, unit, out):
        aliased = [unit] if out is None else [unit, out]
        first = 3 + len(blocks)
        return pl.pallas_call(
            functools.partial(stage_kernel, scale, slots, places),
            out_shape=(unit_shape, out_shape),
            in_specs=[smem, smem, vmem] + [vmem] * len(blocks) + [vmem, hbm][: len(aliased)],
            out_specs=(vmem, hbm),
            input_output_aliases={first + i: i for i in range(len(aliased))},
            scratch_shapes=[
                pltpu.VMEM(((FINE + 1) * half_rows, halves * length), jnp.bfloat16),
                pltpu.VMEM((COARSE * rows, halves * length), jnp.bfloat16),
                pltpu.VMEM((len(slots), lags, half_rows, rows), jnp.float32),
                pltpu.SemaphoreType.DMA((len(slots), CHUNKS)),
            ],
            compiler_params=params,
            cost_estimate=cost(len(places), len(slots)),
        )(pairs, count, band, *blocks, *aliased)

    band, unit = pl.pallas_call(
        early_kernel,
        out_shape=(band_shape, unit_shape),
        in_specs=[vmem] * 5,
        out_specs=(vmem, vmem),
        compiler_params=params,
        cost_estimate=cost(2, 0),
    )(taps, own, swap(own), partner, swap(partner))
    unit, out = stage(
        (0,), (BELOW, ABOVE), (below, swap(below), above, swap(above)), band, unit, None
    )
    diagonal, unit = lax.optimization_barrier((diagonal, unit))
    unit, out = stage(
        tuple(range(1, cap)), (DIAGONAL,), (diagonal, swap(diagonal)), band, unit, out
    )
    return jnp.transpose(out, (0, 2, 1, 3))


def solution(mesh):
    return jax.shard_map(
        body,
        mesh=mesh,
        in_specs=(
            P(("groups", "chan"), "tm", None),
            P(),
            P(("groups", "chan"), None),
            P(("groups", "chan")),
        ),
        out_specs=P(("groups", "chan"), "tm", None, None),
        check_vma=False,
    )
```

time: 36 us -> 37 us (1.028)
  the two profiles are of different devices: /device:TPU:0 before, /device:TPU:27 now
where the time goes in v3:
time: 37 us; the launch traced here: 36.8 us
  Pallas kernels  15.5 us (42%)
  starting transfers between devices  13.5 us (36%)
  waiting for transfers between devices  4.74 us (13%)
  local copies, waits for them, and re-layouts  1.62 us (4%)
  between operations  0.74 us (2%)
  other arithmetic  0.66 us (2%)
    pallas_call x2, Pallas kernels, stage(): pl.pallas_call(functools.partial(stage_kernel, scale, slots, places), out...  14.5 us
    ppermute x9, starting transfers between devices, passed(): return lax.ppermute(block, axis, route)  13.5 us
    ppermute x9, waiting for transfers between devices, passed(): return lax.ppermute(block, axis, route)  4.74 us
    unnamed x4, local copies, waits for them, and re-layouts  1.62 us
    pallas_call x1, Pallas kernels, body(): pl.pallas_call(early_kernel, out_shape=(band_shape, unit_shape), in_specs...  0.93 us
  transfers between devices with their start and end apart: 9, of which 4 were waited for; matrix products, arithmetic and copies ran while one was open for 2% of the time, Pallas kernels for 16%

profile of v3, /device:TPU:27, one launch (start us, length us, event | category | flops | bytes accessed | tf_op | source)
XLA Modules:
  0.0 36.8 jit_solution(16185366071630340888)
XLA Ops:
  0.0 1.2 %collective-permute-start.1 = (bf16[128,1024]{1,0:T(8,128)(2,1)}, bf16[128,1024]{1,0:T(8,128)(2,1)S(1)}, u32[]{:S(2)}, u32[]{:S(2)}) collective-permute-start(bf16[128,1024]{1,0:T(8,128)(2,1)} %bitcast.6), channel_id=1, source_target_pairs={{0,2},{2,0},{4,6},{6,4},{8,10},{10,8},{12,14},{14,12},{1,3},{3,1},... | collective-permute-start | bytes 786440 | tf_op jit(solution)/shard_map/ppermute | solution.py:24
  1.2 2.1 %collective-permute-start.6 = (bf16[128,1024]{1,0:T(8,128)(2,1)}, bf16[128,1024]{1,0:T(8,128)(2,1)S(1)}, u32[]{:S(2)}, u32[]{:S(2)}) collective-permute-start(bf16[128,1024]{1,0:T(8,128)(2,1)} %bitcast.7), channel_id=1, source_target_pairs={{4,0},{6,2},{8,4},{10,6},{12,8},{14,10},{5,1},{7,3},{9,5},{11,7},{... | collective-permute-start | bytes 786440 | tf_op jit(solution)/shard_map/ppermute | solution.py:24
  3.3 1.3 %collective-permute-start.4 = (bf16[128,1024]{1,0:T(8,128)(2,1)}, bf16[128,1024]{1,0:T(8,128)(2,1)S(1)}, u32[]{:S(2)}, u32[]{:S(2)}) collective-permute-start(bf16[128,1024]{1,0:T(8,128)(2,1)} %bitcast.8), channel_id=1, source_target_pairs={{0,4},{2,6},{4,8},{6,10},{8,12},{10,14},{1,5},{3,7},{5,9},{7,11},{... | collective-permute-start | bytes 786440 | tf_op jit(solution)/shard_map/ppermute | solution.py:24
  4.6 0.7 %bitcast_convert_fusion.taps_ref = f32[1,64]{1,0:T(1,128)S(1)} fusion(bf16[64]{0:T(256)(128)(2,1)} %param.5), kind=kLoop, calls=%fused_computation | loop fusion | flops 64 | bytes 384 | tf_op jit(solution)/shard_map/broadcast_in_dim | solution.py:183
  5.3 1.2 %collective-permute-start = (bf16[128,1024]{1,0:T(8,128)(2,1)}, bf16[128,1024]{1,0:T(8,128)(2,1)S(1)}, u32[]{:S(2)}, u32[]{:S(2)}) collective-permute-start(bf16[128,1024]{1,0:T(8,128)(2,1)} %bitcast.9), channel_id=1, source_target_pairs={{0,1},{1,0},{2,3},{3,2},{4,5},{5,4},{6,7},{7,6},{8,9},{9,8},{10,11... | collective-permute-start | bytes 786440 | tf_op jit(solution)/shard_map/ppermute | solution.py:24
  6.5 0.9 %collective-permute-done.1.refs_2_ = bf16[128,1024]{1,0:T(8,128)(2,1)S(1)} collective-permute-done((bf16[128,1024]{1,0:T(8,128)(2,1)}, bf16[128,1024]{1,0:T(8,128)(2,1)S(1)}, u32[]{:S(2)}, u32[]{:S(2)}) %collective-permute-start.1) | collective-permute-done | bytes 262176 | tf_op jit(solution)/shard_map/ppermute | solution.py:24
  7.4 1.5 %collective-permute-start.2 = (bf16[128,1024]{1,0:T(8,128)(2,1)S(1)}, bf16[128,1024]{1,0:T(8,128)(2,1)S(1)}, u32[]{:S(2)}, u32[]{:S(2)}) collective-permute-start(bf16[128,1024]{1,0:T(8,128)(2,1)S(1)} %collective-permute-done.1.refs_2_), channel_id=1, source_target_pairs={{0,1},{1,0},{2,3},{3,2},{4,5},{5,4},{6,7},{7,6},{8,9},{9,8},{10,11... | collective-permute-start | bytes 786440 | tf_op jit(solution)/shard_map/ppermute | solution.py:24
  8.9 0.0 collective-permute-done.6.refs_2_
  8.9 1.2 %collective-permute-start.7 = (bf16[128,1024]{1,0:T(8,128)(2,1)S(1)}, bf16[128,1024]{1,0:T(8,128)(2,1)S(1)}, u32[]{:S(2)}, u32[]{:S(2)}) collective-permute-start(bf16[128,1024]{1,0:T(8,128)(2,1)S(1)} %collective-permute-done.6.refs_2_), channel_id=1, source_target_pairs={{0,1},{1,0},{2,3},{3,2},{4,5},{5,4},{6,7},{7,6},{8,9},{9,8},{10,11... | collective-permute-start | bytes 786440 | tf_op jit(solution)/shard_map/ppermute | solution.py:24
  10.1 1.9 %collective-permute-done.4.refs_0_ = bf16[128,1024]{1,0:T(8,128)(2,1)S(1)} collective-permute-done((bf16[128,1024]{1,0:T(8,128)(2,1)}, bf16[128,1024]{1,0:T(8,128)(2,1)S(1)}, u32[]{:S(2)}, u32[]{:S(2)}) %collective-permute-start.4) | collective-permute-done | bytes 262176 | tf_op jit(solution)/shard_map/ppermute | solution.py:24
  12.0 2.2 %collective-permute-start.5 = (bf16[128,1024]{1,0:T(8,128)(2,1)S(1)}, bf16[128,1024]{1,0:T(8,128)(2,1)S(1)}, u32[]{:S(2)}, u32[]{:S(2)}) collective-permute-start(bf16[128,1024]{1,0:T(8,128)(2,1)S(1)} %collective-permute-done.4.refs_0_), channel_id=1, source_target_pairs={{0,1},{1,0},{2,3},{3,2},{4,5},{5,4},{6,7},{7,6},{8,9},{9,8},{10,11... | collective-permute-start | bytes 786440 | tf_op jit(solution)/shard_map/ppermute | solution.py:24
  14.2 2.0 %collective-permute-start.3 = (bf16[128,1024]{1,0:T(8,128)(2,1)}, bf16[128,1024]{1,0:T(8,128)(2,1)S(1)}, u32[]{:S(2)}, u32[]{:S(2)}) collective-permute-start(bf16[128,1024]{1,0:T(8,128)(2,1)} %bitcast.10), channel_id=1, source_target_pairs={{2,4},{4,2},{6,8},{8,6},{10,12},{12,10},{3,5},{5,3},{7,9},{9,7},{1... | collective-permute-start | bytes 786440 | tf_op jit(solution)/shard_map/ppermute | solution.py:24
  16.8 0.0 collective-permute-done.refs_1_
  16.8 0.0 collective-permute-done.2.refs_3_
  16.8 0.0 copy-start
  16.8 0.9 %copy-done = bf16[128,1,1024]{2,0,1:T(8,128)(2,1)S(1)} copy-done((bf16[128,1,1024]{2,0,1:T(8,128)(2,1)S(1)}, bf16[128,1,1024]{2,0,1:T(8,128)(2,1)}, u32[]{:S(2)}) %copy-start) | copy-done | bytes 262168
  17.8 0.9 %shard_map.46 = (bf16[2,256,256]{2,1,0:T(8,128)(2,1)S(1)}, bf16[5,128,2048]{2,1,0:T(8,128)(2,1)S(1)}) custom-call(f32[1,64]{1,0:T(1,128)S(1)} %bitcast_convert_fusion.taps_ref, bf16[128,1024]{1,0:T(8,128)(2,1)S(1)} %bitcast.11, bf16[128,1024]{1,0:T(8,128)(2,1)S(1)} %collective-permute-done.refs_1_, bf16[128,1024]{1,0:T(8,128)(2,1)S(1)} %collective-permute-done.1.refs_2_, ...), custom_call_target="tpu_custom_call" | custom-call | flops 536870912 | tf_op jit(solution)/shard_map/pallas_call | solution.py:221
  18.7 0.0 collective-permute-done.7.refs_3_
  18.7 0.0 collective-permute-done.5.refs_1_
  18.7 0.0 copy-start.1
  18.8 0.7 %copy-done.1 = s32[4,2]{0,1:T(2,128)S(1)} copy-done((s32[4,2]{0,1:T(2,128)S(1)}, s32[4,2]{0,1:T(2,128)}, u32[]{:S(2)}) %copy-start.1) | copy-done | bytes 56
  19.4 4.8 %shard_map.47 = (bf16[5,128,2048]{2,1,0:T(8,128)(2,1)S(1)}, f32[4,65,64,128]{3,2,1,0:T(8,128)}) custom-call(s32[2,4]{1,0:T(2,128)S(1)} %bitcast.12, s32[1]{0:T(128)S(6)} %copy.11.count_ref, bf16[2,256,256]{2,1,0:T(8,128)(2,1)S(1)} %get-tuple-element.20.band_ref, ...), custom_call_target="tpu_custom_call", output_to_operand_aliasing={{0}: (7, {})} | custom-call | flops 2717908992 | bytes 2129920 | tf_op jit(solution)/shard_map/pallas_call | solution.py:205
  24.3 0.8 %collective-permute-done.3.refs_0_ = bf16[128,1024]{1,0:T(8,128)(2,1)S(1)} collective-permute-done((bf16[128,1024]{1,0:T(8,128)(2,1)}, bf16[128,1024]{1,0:T(8,128)(2,1)S(1)}, u32[]{:S(2)}, u32[]{:S(2)}) %collective-permute-start.3) | collective-permute-done | bytes 262176 | tf_op jit(solution)/shard_map/ppermute | solution.py:24
  25.1 0.8 %collective-permute-start.8 = (bf16[128,1024]{1,0:T(8,128)(2,1)S(1)}, bf16[128,1024]{1,0:T(8,128)(2,1)S(1)}, u32[]{:S(2)}, u32[]{:S(2)}) collective-permute-start(bf16[128,1024]{1,0:T(8,128)(2,1)S(1)} %collective-permute-done.3.refs_0_), channel_id=1, source_target_pairs={{0,1},{1,0},{2,3},{3,2},{4,5},{5,4},{6,7},{7,6},{8,9},{9,8},{10,11... | collective-permute-start | bytes 786440 | tf_op jit(solution)/shard_map/ppermute | solution.py:24
  25.9 1.2 %collective-permute-done.8.refs_1_ = bf16[128,1024]{1,0:T(8,128)(2,1)S(1)} collective-permute-done((bf16[128,1024]{1,0:T(8,128)(2,1)S(1)}, bf16[128,1024]{1,0:T(8,128)(2,1)S(1)}, u32[]{:S(2)}, u32[]{:S(2)}) %collective-permute-start.8) | collective-permute-done | bytes 262176 | tf_op jit(solution)/shard_map/ppermute | solution.py:24
  27.0 9.7 %shard_map.48 = (bf16[5,128,2048]{2,1,0:T(8,128)(2,1)S(1)}, f32[4,65,64,128]{3,2,1,0:T(8,128)}) custom-call(s32[2,4]{1,0:T(2,128)S(1)} %bitcast.13, s32[1]{0:T(128)S(6)} %copy.11.count_ref, bf16[2,256,256]{2,1,0:T(8,128)(2,1)S(1)} %get-tuple-element.20.band_ref, ...), custom_call_target="tpu_custom_call", output_to_operand_aliasing={{0}: (5, {}), {1}: (6, {})} | custom-call | flops 6811549696 | bytes 6389760 | tf_op jit(solution)/shard_map/pallas_call | solution.py:205
Async XLA Ops:
  0.0 7.4 %collective-permute-start.1 = (bf16[128,1024]{1,0:T(8,128)(2,1)}, bf16[128,1024]{1,0:T(8,128)(2,1)S(1)}, u32[]{:S(2)}, u32[]{:S(2)}) collective-permute-start(bf16[128,1024]{1,0:T(8,128)(2,1)} %bitcast.6), channel_id=1, source_target_pairs={{0,2},{2,0},{4,6},{6,4},{8,10},{10,8},{12,14},{14,12},{1,3},{3,1},... | collective-permute-start | bytes 786440 | tf_op jit(solution)/shard_map/ppermute | solution.py:24
  1.2 7.7 %collective-permute-start.6 = (bf16[128,1024]{1,0:T(8,128)(2,1)}, bf16[128,1024]{1,0:T(8,128)(2,1)S(1)}, u32[]{:S(2)}, u32[]{:S(2)}) collective-permute-start(bf16[128,1024]{1,0:T(8,128)(2,1)} %bitcast.7), channel_id=1, source_target_pairs={{4,0},{6,2},{8,4},{10,6},{12,8},{14,10},{5,1},{7,3},{9,5},{11,7},{... | collective-permute-start | bytes 786440 | tf_op jit(solution)/shard_map/ppermute | solution.py:24
  3.3 8.7 %collective-permute-start.4 = (bf16[128,1024]{1,0:T(8,128)(2,1)}, bf16[128,1024]{1,0:T(8,128)(2,1)S(1)}, u32[]{:S(2)}, u32[]{:S(2)}) collective-permute-start(bf16[128,1024]{1,0:T(8,128)(2,1)} %bitcast.8), channel_id=1, source_target_pairs={{0,4},{2,6},{4,8},{6,10},{8,12},{10,14},{1,5},{3,7},{5,9},{7,11},{... | collective-permute-start | bytes 786440 | tf_op jit(solution)/shard_map/ppermute | solution.py:24
  5.3 11.5 %collective-permute-start = (bf16[128,1024]{1,0:T(8,128)(2,1)}, bf16[128,1024]{1,0:T(8,128)(2,1)S(1)}, u32[]{:S(2)}, u32[]{:S(2)}) collective-permute-start(bf16[128,1024]{1,0:T(8,128)(2,1)} %bitcast.9), channel_id=1, source_target_pairs={{0,1},{1,0},{2,3},{3,2},{4,5},{5,4},{6,7},{7,6},{8,9},{9,8},{10,11... | collective-permute-start | bytes 786440 | tf_op jit(solution)/shard_map/ppermute | solution.py:24
  7.4 9.4 %collective-permute-start.2 = (bf16[128,1024]{1,0:T(8,128)(2,1)S(1)}, bf16[128,1024]{1,0:T(8,128)(2,1)S(1)}, u32[]{:S(2)}, u32[]{:S(2)}) collective-permute-start(bf16[128,1024]{1,0:T(8,128)(2,1)S(1)} %collective-permute-done.1.refs_2_), channel_id=1, source_target_pairs={{0,1},{1,0},{2,3},{3,2},{4,5},{5,4},{6,7},{7,6},{8,9},{9,8},{10,11... | collective-permute-start | bytes 786440 | tf_op jit(solution)/shard_map/ppermute | solution.py:24
  8.9 9.8 %collective-permute-start.7 = (bf16[128,1024]{1,0:T(8,128)(2,1)S(1)}, bf16[128,1024]{1,0:T(8,128)(2,1)S(1)}, u32[]{:S(2)}, u32[]{:S(2)}) collective-permute-start(bf16[128,1024]{1,0:T(8,128)(2,1)S(1)} %collective-permute-done.6.refs_2_), channel_id=1, source_target_pairs={{0,1},{1,0},{2,3},{3,2},{4,5},{5,4},{6,7},{7,6},{8,9},{9,8},{10,11... | collective-permute-start | bytes 786440 | tf_op jit(solution)/shard_map/ppermute | solution.py:24
  12.0 6.7 %collective-permute-start.5 = (bf16[128,1024]{1,0:T(8,128)(2,1)S(1)}, bf16[128,1024]{1,0:T(8,128)(2,1)S(1)}, u32[]{:S(2)}, u32[]{:S(2)}) collective-permute-start(bf16[128,1024]{1,0:T(8,128)(2,1)S(1)} %collective-permute-done.4.refs_0_), channel_id=1, source_target_pairs={{0,1},{1,0},{2,3},{3,2},{4,5},{5,4},{6,7},{7,6},{8,9},{9,8},{10,11... | collective-permute-start | bytes 786440 | tf_op jit(solution)/shard_map/ppermute | solution.py:24
  14.2 10.9 %collective-permute-start.3 = (bf16[128,1024]{1,0:T(8,128)(2,1)}, bf16[128,1024]{1,0:T(8,128)(2,1)S(1)}, u32[]{:S(2)}, u32[]{:S(2)}) collective-permute-start(bf16[128,1024]{1,0:T(8,128)(2,1)} %bitcast.10), channel_id=1, source_target_pairs={{2,4},{4,2},{6,8},{8,6},{10,12},{12,10},{3,5},{5,3},{7,9},{9,7},{1... | collective-permute-start | bytes 786440 | tf_op jit(solution)/shard_map/ppermute | solution.py:24
  16.8 1.0 %copy-start = (bf16[128,1,1024]{2,0,1:T(8,128)(2,1)S(1)}, bf16[128,1,1024]{2,0,1:T(8,128)(2,1)}, u32[]{:S(2)}) copy-start(bf16[128,1,1024]{2,0,1:T(8,128)(2,1)} %param.4) | copy-start | bytes 786436
  18.7 0.7 %copy-start.1 = (s32[4,2]{0,1:T(2,128)S(1)}, s32[4,2]{0,1:T(2,128)}, u32[]{:S(2)}) copy-start(s32[4,2]{0,1:T(2,128)} %param.6) | copy-start | bytes 100
  25.1 1.9 %collective-permute-start.8 = (bf16[128,1024]{1,0:T(8,128)(2,1)S(1)}, bf16[128,1024]{1,0:T(8,128)(2,1)S(1)}, u32[]{:S(2)}, u32[]{:S(2)}) collective-permute-start(bf16[128,1024]{1,0:T(8,128)(2,1)S(1)} %collective-permute-done.3.refs_0_), channel_id=1, source_target_pairs={{0,1},{1,0},{2,3},{3,2},{4,5},{5,4},{6,7},{7,6},{8,9},{9,8},{10,11... | collective-permute-start | bytes 786440 | tf_op jit(solution)/shard_map/ppermute | solution.py:24

commit v4 on v3

v4 whole, which is shorter than its diff:
```python
import functools

import jax
import jax.numpy as jnp
from jax import lax
from jax.experimental import pallas as pl
from jax.experimental.pallas import tpu as pltpu
from jax.sharding import PartitionSpec as P

LAG = 32
REACH = 2
NEAR = 2 * REACH + 1
FINE = 8
COARSE = LAG // FINE
LANES = 128
TILE = 256
CHUNKS = 4
OWN, PARTNER, BELOW, ABOVE, DIAGONAL = range(NEAR)


def passed(block, axis, target):
    size = lax.axis_size(axis)
    route = [(i, target(i)) for i in range(size) if 0 <= target(i) < size]
    return lax.ppermute(block, axis, route)


def partner_of(i):
    return i + 1 if i % 2 == 0 else i - 1


def diagonal_of(i):
    return i - 1 if i % 2 == 0 else i + 1


def place_of(block, owner):
    offset = block - owner
    side = jnp.where(offset == 1 - 2 * lax.rem(owner, 2), PARTNER, DIAGONAL)
    away = jnp.where(offset == -REACH, BELOW, jnp.where(offset == REACH, ABOVE, side))
    return jnp.where(offset == 0, OWN, away)


def shifted(rows, amount):
    if amount == 0:
        return rows
    length = rows.shape[-1]
    moved = pltpu.roll(rows, amount % length, 1)
    edge = slice(0, LANES) if amount > 0 else slice(length - LANES, length)
    lane = lax.broadcasted_iota(jnp.int32, (rows.shape[0], LANES), 1)
    keep = lane >= amount if amount > 0 else lane < LANES + amount
    cut = jnp.where(keep, moved[:, edge], jnp.zeros((), rows.dtype))
    if amount > 0:
        return jnp.concatenate([cut, moved[:, LANES:]], axis=1)
    return jnp.concatenate([moved[:, : length - LANES], cut], axis=1)


def contract_lanes(left, right):
    return lax.dot_general(
        left, right, (((1,), (1,)), ((), ())), preferred_element_type=jnp.float32
    )


def make_band(taps_ref, band_ref):
    taps = taps_ref[...]
    wide = jnp.concatenate([taps, jnp.zeros((1, TILE - taps.shape[1]), jnp.float32)], axis=1)
    band = pltpu.roll(jnp.broadcast_to(wide, (TILE, TILE)), 0, 1, stride=1, stride_axis=0)
    row = lax.broadcasted_iota(jnp.int32, (TILE, TILE), 0)
    column = lax.broadcasted_iota(jnp.int32, (TILE, TILE), 1)
    band_ref[0] = jnp.where(column >= row, band, 0.0).astype(jnp.bfloat16)
    band_ref[1] = jnp.where(column < row, band, 0.0).astype(jnp.bfloat16)


def normalise(source_ref, band_ref, unit_ref, place, window):
    rows, length = unit_ref.shape[1], source_ref.shape[-1]
    pieces = []
    for start in range(0, length, TILE):
        piece = jnp.dot(
            source_ref[:rows, start : start + TILE], band_ref[0], preferred_element_type=jnp.float32
        )
        if start > 0:
            piece += jnp.dot(
                source_ref[:rows, start - TILE : start], band_ref[1],
                preferred_element_type=jnp.float32,
            )
        pieces.append(piece)
    filtered = jnp.concatenate(pieces, axis=1)
    meansq = jnp.mean(filtered * filtered, axis=-1, keepdims=True)
    unit_ref[place, :, window * length : (window + 1) * length] = (
        filtered * lax.rsqrt(meansq + 1e-06)
    ).astype(jnp.bfloat16)


def prepare(slot, sign, pairs_ref, unit_ref, left_ref, right_ref, half_rows):
    _, channels, both = unit_ref.shape
    length = both // 2
    owner = lax.axis_index("chan")
    first_row = pl.multiple_of(lax.axis_index("tm") * half_rows, half_rows)
    source = place_of(pairs_ref[0, slot], owner)
    partner = place_of(pairs_ref[1, slot], owner)
    for window in range(2):
        span = slice(window * length, (window + 1) * length)
        rows = unit_ref[source, pl.ds(first_row, half_rows), span]
        for place in range(FINE + 1 if sign > 0 else FINE):
            step = place if sign > 0 else place - FINE
            left_ref[place * half_rows : (place + 1) * half_rows, span] = shifted(rows, step)
        rows = unit_ref[partner, :, span]
        for place in range(COARSE):
            right_ref[place * channels : (place + 1) * channels, span] = shifted(
                rows, -sign * FINE * place
            )


def correlate(slot, sign, pair, factor, left_ref, right_ref, stage_ref, out_ref, sem):
    half_rows, channels = stage_ref.shape[1:]
    tall = FINE + 1 if sign > 0 and pair + 2 == COARSE else FINE
    result = contract_lanes(
        left_ref[: tall * half_rows, :],
        right_ref[pair * channels : (pair + 2) * channels, :],
    )
    lags = []
    for within in range(2):
        for place in range(tall):
            if place == FINE and within == 0:
                continue
            coarse = sign * FINE * (pair + within)
            lag = LAG + coarse + (place if sign > 0 else place - FINE)
            stage_ref[lag] = factor * result[
                place * half_rows : (place + 1) * half_rows,
                within * channels : (within + 1) * channels,
            ]
            lags.append(lag)
    span = pl.ds(min(lags), len(lags))
    copy = pltpu.make_async_copy(stage_ref.at[span], out_ref.at[slot, span], sem)
    copy.start()
    return copy


def early_kernel(pairs_ref, count_ref, taps_ref, *refs):
    blocks, (band_ref, unit_ref) = refs[:2], refs[2:]
    make_band(taps_ref, band_ref)
    for window in range(2):
        normalise(blocks[window], band_ref, unit_ref, OWN, window)


def stage_kernel(scale, slots, places, pairs_ref, count_ref, band_ref, *refs):
    blocks = refs[: 2 * len(places)]
    refs = refs[2 * len(places) :]
    refs = refs[1:] if len(slots) == 1 else refs[2:]
    unit_ref, out_ref, left_ref, right_ref, stage_ref, sems = refs
    for index, place in enumerate(places):
        for window in range(2):
            normalise(blocks[2 * index + window], band_ref, unit_ref, place, window)
    steps = [(index, slot, sign) for index, slot in enumerate(slots) for sign in (1, -1)]

    def ready(number):
        if number < len(steps):
            _, slot, sign = steps[number]
            prepare(
                slot, sign, pairs_ref, unit_ref, left_ref.at[number % 2],
                right_ref.at[number % 2], stage_ref.shape[2],
            )

    copies = []
    ready(0)
    for number, (index, slot, sign) in enumerate(steps):
        ready(number + 1)
        factor = jnp.where(slot < count_ref[0], scale, 0.0)
        for pair in range(0, COARSE, 2):
            copies.append(
                correlate(
                    slot, sign, pair, factor, left_ref.at[number % 2], right_ref.at[number % 2],
                    stage_ref.at[index], out_ref, sems.at[index, len(copies) % CHUNKS],
                )
            )
    for copy in copies:
        copy.wait()


def body(traces, fir_taps, pair_blocks, pair_count):
    rows, windows, length = traces.shape
    block = traces.reshape(rows, length)
    halves = lax.axis_size("tm")
    cap = pair_blocks.shape[0]
    lags = 2 * LAG + 1
    half_rows = rows // halves
    scale = float(windows * halves * length) ** (-0.5)

    swap = lambda array: passed(array, "tm", lambda i: 1 - i)
    partner = passed(block, "chan", partner_of)
    below = passed(block, "chan", lambda i: i + REACH)
    above = passed(block, "chan", lambda i: i - REACH)
    padded = jnp.pad(block, ((0, 16), (0, 0)))
    diagonal = passed(padded, "chan", diagonal_of)
    own, pairs, count = block, pair_blocks.T, pair_count
    taps = fir_taps.astype(jnp.float32)[None, :]

    smem = pl.BlockSpec(memory_space=pltpu.SMEM)
    vmem = pl.BlockSpec(memory_space=pltpu.VMEM)
    hbm = pl.BlockSpec(memory_space=pl.ANY)
    params = pltpu.CompilerParams(vmem_limit_bytes=40 * 1024 * 1024)
    band_shape = jax.ShapeDtypeStruct((2, TILE, TILE), jnp.bfloat16)
    unit_shape = jax.ShapeDtypeStruct((NEAR, rows, halves * length), jnp.bfloat16)
    out_shape = jax.ShapeDtypeStruct((cap, lags, half_rows, rows), jnp.float32)

    light = pl.CostEstimate(flops=1, bytes_accessed=1, transcendentals=0)
    heavy = pl.CostEstimate(
        flops=2 * (cap - 1) * lags * half_rows * rows * halves * length,
        bytes_accessed=(cap - 1) * lags * half_rows * rows * 4,
        transcendentals=0,
    )

    def stage(slots, places, blocks, band, unit, out):
        aliased = [unit] if out is None else [unit, out]
        first = 3 + len(blocks)
        return pl.pallas_call(
            functools.partial(stage_kernel, scale, slots, places),
            out_shape=(unit_shape, out_shape),
            in_specs=[smem, smem, vmem] + [vmem] * len(blocks) + [vmem, hbm][: len(aliased)],
            out_specs=(vmem, hbm),
            input_output_aliases={first + i: i for i in range(len(aliased))},
            scratch_shapes=[
                pltpu.VMEM((2, (FINE + 1) * half_rows, halves * length), jnp.bfloat16),
                pltpu.VMEM((2, COARSE * rows, halves * length), jnp.bfloat16),
                pltpu.VMEM((len(slots), lags, half_rows, rows), jnp.float32),
                pltpu.SemaphoreType.DMA((len(slots), CHUNKS)),
            ],
            compiler_params=params,
            cost_estimate=light if out is None else heavy,
        )(pairs, count, band, *blocks, *aliased)

    band, unit = pl.pallas_call(
        early_kernel,
        out_shape=(band_shape, unit_shape),
        in_specs=[smem, smem] + [vmem] * 3,
        out_specs=(vmem, vmem),
        compiler_params=params,
        cost_estimate=light,
    )(pairs, count, taps, padded, swap(own))
    partner, band = lax.optimization_barrier((partner, band))
    unit, out = stage(
        (0,), (ABOVE, BELOW, PARTNER),
        (above, swap(above), below, swap(below), partner, swap(partner)), band, unit, None,
    )
    diagonal, unit = lax.optimization_barrier((diagonal, unit))
    unit, out = stage(
        tuple(range(1, cap)), (DIAGONAL,), (diagonal, swap(diagonal)), band, unit, out
    )
    return jnp.transpose(out, (0, 2, 1, 3))


def solution(mesh):
    return jax.shard_map(
        body,
        mesh=mesh,
        in_specs=(
            P(("groups", "chan"), "tm", None),
            P(),
            P(("groups", "chan"), None),
            P(("groups", "chan")),
        ),
        out_specs=P(("groups", "chan"), "tm", None, None),
        check_vma=False,
    )
```

time: 37 us -> 36.5 us (0.986)
  the two profiles are of different devices: /device:TPU:27 before, /device:TPU:0 now
where the time goes in v4:
time: 36.5 us; the launch traced here: 36.3 us
  Pallas kernels  16.1 us (44%)
  starting transfers between devices  9.15 us (25%)
  waiting for transfers between devices  7.94 us (22%)
  local copies, waits for them, and re-layouts  1.65 us (5%)
  between operations  0.74 us (2%)
  other arithmetic  0.66 us (2%)
    pallas_call x2, Pallas kernels, stage(): pl.pallas_call(functools.partial(stage_kernel, scale, slots, places), out...  15 us
    ppermute x9, starting transfers between devices, passed(): return lax.ppermute(block, axis, route)  9.15 us
    ppermute x9, waiting for transfers between devices, passed(): return lax.ppermute(block, axis, route)  7.94 us
    pallas_call x1, Pallas kernels, body(): pl.pallas_call(early_kernel, out_shape=(band_shape, unit_shape), in_specs...  1.18 us
    pad x1, local copies, waits for them, and re-layouts, body(): padded = jnp.pad(block, ((0, 16), (0, 0)))  0.97 us
  transfers between devices with their start and end apart: 9, of which 5 were waited for; matrix products, arithmetic and copies ran while one was open for 4% of the time, Pallas kernels for 18%

profile of v4, /device:TPU:0, one launch (start us, length us, event | category | flops | bytes accessed | tf_op | source)
XLA Modules:
  0.0 36.3 jit_solution(7921453253929788440)
XLA Ops:
  0.0 0.5 %collective-permute-start.1 = (bf16[128,1024]{1,0:T(8,128)(2,1)}, bf16[128,1024]{1,0:T(8,128)(2,1)S(1)}, u32[]{:S(2)}, u32[]{:S(2)}) collective-permute-start(bf16[128,1024]{1,0:T(8,128)(2,1)} %bitcast.9), channel_id=1, source_target_pairs={{0,1},{1,0},{2,3},{3,2},{4,5},{5,4},{6,7},{7,6},{8,9},{9,8},{10,11... | collective-permute-start | bytes 786440 | tf_op jit(solution)/shard_map/ppermute | solution.py:24
  0.5 2.5 %collective-permute-start = (bf16[128,1024]{1,0:T(8,128)(2,1)}, bf16[128,1024]{1,0:T(8,128)(2,1)S(1)}, u32[]{:S(2)}, u32[]{:S(2)}) collective-permute-start(bf16[128,1024]{1,0:T(8,128)(2,1)} %bitcast.10), channel_id=1, source_target_pairs={{0,2},{2,0},{4,6},{6,4},{8,10},{10,8},{12,14},{14,12},{1,3},{3,1},... | collective-permute-start | bytes 786440 | tf_op jit(solution)/shard_map/ppermute | solution.py:24
  3.0 3.5 %collective-permute-start.5 = (bf16[128,1024]{1,0:T(8,128)(2,1)}, bf16[128,1024]{1,0:T(8,128)(2,1)S(1)}, u32[]{:S(2)}, u32[]{:S(2)}) collective-permute-start(bf16[128,1024]{1,0:T(8,128)(2,1)} %bitcast.11), channel_id=1, source_target_pairs={{0,4},{2,6},{4,8},{6,10},{8,12},{10,14},{1,5},{3,7},{5,9},{7,11},{... | collective-permute-start | bytes 786440 | tf_op jit(solution)/shard_map/ppermute | solution.py:24
  6.5 1.3 %collective-permute-start.3 = (bf16[128,1024]{1,0:T(8,128)(2,1)}, bf16[128,1024]{1,0:T(8,128)(2,1)S(1)}, u32[]{:S(2)}, u32[]{:S(2)}) collective-permute-start(bf16[128,1024]{1,0:T(8,128)(2,1)} %bitcast.12), channel_id=1, source_target_pairs={{4,0},{6,2},{8,4},{10,6},{12,8},{14,10},{5,1},{7,3},{9,5},{11,7},{... | collective-permute-start | bytes 786440 | tf_op jit(solution)/shard_map/ppermute | solution.py:24
  7.8 1.0 %pad.4.refs_0_ = bf16[144,1024]{1,0:T(8,128)(2,1)S(1)} pad(bf16[128,1024]{1,0:T(8,128)(2,1)} %bitcast.13, bf16[]{:T(256)} %constant.2.clone.1), padding=0_16x0_0 | pad | bytes 557058 | tf_op jit(solution)/shard_map/jit(_pad)/pad | solution.py:191
  8.7 0.7 %collective-permute-start.2 = (bf16[144,1024]{1,0:T(8,128)(2,1)S(1)}, bf16[144,1024]{1,0:T(8,128)(2,1)S(1)}, u32[]{:S(2)}, u32[]{:S(2)}) collective-permute-start(bf16[144,1024]{1,0:T(8,128)(2,1)S(1)} %pad.4.refs_0_), channel_id=1, source_target_pairs={{2,4},{4,2},{6,8},{8,6},{10,12},{12,10},{3,5},{5,3},{7,9},{9,7},{1... | collective-permute-start | bytes 884744 | tf_op jit(solution)/shard_map/ppermute | solution.py:24
  9.4 0.7 %bitcast_convert_fusion.taps_ref = f32[1,64]{1,0:T(1,128)S(1)} fusion(bf16[64]{0:T(256)(128)(2,1)} %param.5), kind=kLoop, calls=%fused_computation | loop fusion | flops 64 | bytes 384 | tf_op jit(solution)/shard_map/broadcast_in_dim | solution.py:194
  10.7 0.0 collective-permute-done.1.refs_1_
  10.8 0.0 copy-start
  10.8 0.7 %copy-done = s32[4,2]{0,1:T(2,128)S(1)} copy-done((s32[4,2]{0,1:T(2,128)S(1)}, s32[4,2]{0,1:T(2,128)}, u32[]{:S(2)}) %copy-start) | copy-done | bytes 56
  11.4 1.2 %shard_map.46 = (bf16[2,256,256]{2,1,0:T(8,128)(2,1)S(1)}, bf16[5,128,2048]{2,1,0:T(8,128)(2,1)S(1)}) custom-call(s32[2,4]{1,0:T(2,128)S(1)} %bitcast.6, s32[1]{0:T(128)S(6)} %copy.11.count_ref, f32[1,64]{1,0:T(1,128)S(1)} %bitcast_convert_fusion.taps_ref, bf16[144,1024]{1,0:T(8,128)(2,1)S(1)} %pad.4.refs_0_, ...), custom_call_target="tpu_custom_call" | custom-call | flops 1 | bytes 1 | tf_op jit(solution)/shard_map/pallas_call | solution.py:230
  12.6 0.0 collective-permute-done.refs_4_
  12.6 0.1 collective-permute-done.5.refs_2_
  12.7 0.0 collective-permute-start.6
  12.7 5.0 %collective-permute-done.3.refs_0_ = bf16[128,1024]{1,0:T(8,128)(2,1)S(1)} collective-permute-done((bf16[128,1024]{1,0:T(8,128)(2,1)}, bf16[128,1024]{1,0:T(8,128)(2,1)S(1)}, u32[]{:S(2)}, u32[]{:S(2)}) %collective-permute-start.3) | collective-permute-done | bytes 262176 | tf_op jit(solution)/shard_map/ppermute | solution.py:24
  17.7 0.0 collective-permute-start.4
  17.7 0.5 %collective-permute-start.7 = (bf16[128,1024]{1,0:T(8,128)(2,1)S(1)}, bf16[128,1024]{1,0:T(8,128)(2,1)S(1)}, u32[]{:S(2)}, u32[]{:S(2)}) collective-permute-start(bf16[128,1024]{1,0:T(8,128)(2,1)S(1)} %collective-permute-done.refs_4_), channel_id=1, source_target_pairs={{0,1},{1,0},{2,3},{3,2},{4,5},{5,4},{6,7},{7,6},{8,9},{9,8},{10,11... | collective-permute-start | bytes 786440 | tf_op jit(solution)/shard_map/ppermute | solution.py:24
  18.3 0.0 collective-permute-done.6.refs_3_
  18.3 1.0 %collective-permute-done.4.refs_1_ = bf16[128,1024]{1,0:T(8,128)(2,1)S(1)} collective-permute-done((bf16[128,1024]{1,0:T(8,128)(2,1)S(1)}, bf16[128,1024]{1,0:T(8,128)(2,1)S(1)}, u32[]{:S(2)}, u32[]{:S(2)}) %collective-permute-start.4) | collective-permute-done | bytes 262176 | tf_op jit(solution)/shard_map/ppermute | solution.py:24
  19.3 0.4 %collective-permute-done.7.refs_5_ = bf16[128,1024]{1,0:T(8,128)(2,1)S(1)} collective-permute-done((bf16[128,1024]{1,0:T(8,128)(2,1)S(1)}, bf16[128,1024]{1,0:T(8,128)(2,1)S(1)}, u32[]{:S(2)}, u32[]{:S(2)}) %collective-permute-start.7) | collective-permute-done | bytes 262176 | tf_op jit(solution)/shard_map/ppermute | solution.py:24
  19.7 5.2 %shard_map.47 = (bf16[5,128,2048]{2,1,0:T(8,128)(2,1)S(1)}, f32[4,65,64,128]{3,2,1,0:T(8,128)}) custom-call(s32[2,4]{1,0:T(2,128)S(1)} %bitcast.7, s32[1]{0:T(128)S(6)} %copy.11.count_ref, bf16[2,256,256]{2,1,0:T(8,128)(2,1)S(1)} %get-tuple-element.15.band_ref, ...), custom_call_target="tpu_custom_call", output_to_operand_aliasing={{0}: (9, {})} | custom-call | flops 1 | bytes 1 | tf_op jit(solution)/shard_map/pallas_call | solution.py:214
  24.9 0.0 collective-permute-done.2.refs_0_
  24.9 0.2 collective-permute-start.8
  25.1 1.4 %collective-permute-done.8.refs_1_ = bf16[144,1024]{1,0:T(8,128)(2,1)S(1)} collective-permute-done((bf16[144,1024]{1,0:T(8,128)(2,1)S(1)}, bf16[144,1024]{1,0:T(8,128)(2,1)S(1)}, u32[]{:S(2)}, u32[]{:S(2)}) %collective-permute-start.8) | collective-permute-done | bytes 294944 | tf_op jit(solution)/shard_map/ppermute | solution.py:24
  26.5 9.7 %shard_map.48 = (bf16[5,128,2048]{2,1,0:T(8,128)(2,1)S(1)}, f32[4,65,64,128]{3,2,1,0:T(8,128)}) custom-call(s32[2,4]{1,0:T(2,128)S(1)} %bitcast.8, s32[1]{0:T(128)S(6)} %copy.11.count_ref, bf16[2,256,256]{2,1,0:T(8,128)(2,1)S(1)} %get-tuple-element.15.band_ref, ...), custom_call_target="tpu_custom_call", output_to_operand_aliasing={{0}: (5, {}), {1}: (6, {})} | custom-call | flops 6543114240 | bytes 6389760 | tf_op jit(solution)/shard_map/pallas_call | solution.py:214
Async XLA Ops:
  0.0 10.7 %collective-permute-start.1 = (bf16[128,1024]{1,0:T(8,128)(2,1)}, bf16[128,1024]{1,0:T(8,128)(2,1)S(1)}, u32[]{:S(2)}, u32[]{:S(2)}) collective-permute-start(bf16[128,1024]{1,0:T(8,128)(2,1)} %bitcast.9), channel_id=1, source_target_pairs={{0,1},{1,0},{2,3},{3,2},{4,5},{5,4},{6,7},{7,6},{8,9},{9,8},{10,11... | collective-permute-start | bytes 786440 | tf_op jit(solution)/shard_map/ppermute | solution.py:24
  0.5 12.2 %collective-permute-start = (bf16[128,1024]{1,0:T(8,128)(2,1)}, bf16[128,1024]{1,0:T(8,128)(2,1)S(1)}, u32[]{:S(2)}, u32[]{:S(2)}) collective-permute-start(bf16[128,1024]{1,0:T(8,128)(2,1)} %bitcast.10), channel_id=1, source_target_pairs={{0,2},{2,0},{4,6},{6,4},{8,10},{10,8},{12,14},{14,12},{1,3},{3,1},... | collective-permute-start | bytes 786440 | tf_op jit(solution)/shard_map/ppermute | solution.py:24
  3.0 9.7 %collective-permute-start.5 = (bf16[128,1024]{1,0:T(8,128)(2,1)}, bf16[128,1024]{1,0:T(8,128)(2,1)S(1)}, u32[]{:S(2)}, u32[]{:S(2)}) collective-permute-start(bf16[128,1024]{1,0:T(8,128)(2,1)} %bitcast.11), channel_id=1, source_target_pairs={{0,4},{2,6},{4,8},{6,10},{8,12},{10,14},{1,5},{3,7},{5,9},{7,11},{... | collective-permute-start | bytes 786440 | tf_op jit(solution)/shard_map/ppermute | solution.py:24
  6.5 11.3 %collective-permute-start.3 = (bf16[128,1024]{1,0:T(8,128)(2,1)}, bf16[128,1024]{1,0:T(8,128)(2,1)S(1)}, u32[]{:S(2)}, u32[]{:S(2)}) collective-permute-start(bf16[128,1024]{1,0:T(8,128)(2,1)} %bitcast.12), channel_id=1, source_target_pairs={{4,0},{6,2},{8,4},{10,6},{12,8},{14,10},{5,1},{7,3},{9,5},{11,7},{... | collective-permute-start | bytes 786440 | tf_op jit(solution)/shard_map/ppermute | solution.py:24
  8.7 16.1 %collective-permute-start.2 = (bf16[144,1024]{1,0:T(8,128)(2,1)S(1)}, bf16[144,1024]{1,0:T(8,128)(2,1)S(1)}, u32[]{:S(2)}, u32[]{:S(2)}) collective-permute-start(bf16[144,1024]{1,0:T(8,128)(2,1)S(1)} %pad.4.refs_0_), channel_id=1, source_target_pairs={{2,4},{4,2},{6,8},{8,6},{10,12},{12,10},{3,5},{5,3},{7,9},{9,7},{1... | collective-permute-start | bytes 884744 | tf_op jit(solution)/shard_map/ppermute | solution.py:24
  10.8 0.7 %copy-start = (s32[4,2]{0,1:T(2,128)S(1)}, s32[4,2]{0,1:T(2,128)}, u32[]{:S(2)}) copy-start(s32[4,2]{0,1:T(2,128)} %param.6) | copy-start | bytes 100
  12.7 5.6 %collective-permute-start.6 = (bf16[128,1024]{1,0:T(8,128)(2,1)S(1)}, bf16[128,1024]{1,0:T(8,128)(2,1)S(1)}, u32[]{:S(2)}, u32[]{:S(2)}) collective-permute-start(bf16[128,1024]{1,0:T(8,128)(2,1)S(1)} %collective-permute-done.5.refs_2_), channel_id=1, source_target_pairs={{0,1},{1,0},{2,3},{3,2},{4,5},{5,4},{6,7},{7,6},{8,9},{9,8},{10,11... | collective-permute-start | bytes 786440 | tf_op jit(solution)/shard_map/ppermute | solution.py:24
  17.7 1.5 %collective-permute-start.4 = (bf16[128,1024]{1,0:T(8,128)(2,1)S(1)}, bf16[128,1024]{1,0:T(8,128)(2,1)S(1)}, u32[]{:S(2)}, u32[]{:S(2)}) collective-permute-start(bf16[128,1024]{1,0:T(8,128)(2,1)S(1)} %collective-permute-done.3.refs_0_), channel_id=1, source_target_pairs={{0,1},{1,0},{2,3},{3,2},{4,5},{5,4},{6,7},{7,6},{8,9},{9,8},{10,11... | collective-permute-start | bytes 786440 | tf_op jit(solution)/shard_map/ppermute | solution.py:24
  17.7 1.9 %collective-permute-start.7 = (bf16[128,1024]{1,0:T(8,128)(2,1)S(1)}, bf16[128,1024]{1,0:T(8,128)(2,1)S(1)}, u32[]{:S(2)}, u32[]{:S(2)}) collective-permute-start(bf16[128,1024]{1,0:T(8,128)(2,1)S(1)} %collective-permute-done.refs_4_), channel_id=1, source_target_pairs={{0,1},{1,0},{2,3},{3,2},{4,5},{5,4},{6,7},{7,6},{8,9},{9,8},{10,11... | collective-permute-start | bytes 786440 | tf_op jit(solution)/shard_map/ppermute | solution.py:24
  24.9 1.6 %collective-permute-start.8 = (bf16[144,1024]{1,0:T(8,128)(2,1)S(1)}, bf16[144,1024]{1,0:T(8,128)(2,1)S(1)}, u32[]{:S(2)}, u32[]{:S(2)}) collective-permute-start(bf16[144,1024]{1,0:T(8,128)(2,1)S(1)} %collective-permute-done.2.refs_0_), channel_id=1, source_target_pairs={{0,1},{1,0},{2,3},{3,2},{4,5},{5,4},{6,7},{7,6},{8,9},{9,8},{10,11... | collective-permute-start | bytes 884744 | tf_op jit(solution)/shard_map/ppermute | solution.py:24

commit v5 on v4

--- a/solution.py
+++ b/solution.py
@@ -15,6 +15,7 @@
 LANES = 128
 TILE = 256
 CHUNKS = 4
+MARGIN = 32
 OWN, PARTNER, BELOW, ABOVE, DIAGONAL = range(NEAR)
 
 
@@ -53,12 +54,6 @@
     return jnp.concatenate([moved[:, : length - LANES], cut], axis=1)
 
 
-def contract_lanes(left, right):
-    return lax.dot_general(
-        left, right, (((1,), (1,)), ((), ())), preferred_element_type=jnp.float32
-    )
-
-
 def make_band(taps_ref, band_ref):
     taps = taps_ref[...]
     wide = jnp.concatenate([taps, jnp.zeros((1, TILE - taps.shape[1]), jnp.float32)], axis=1)
@@ -69,7 +64,7 @@
     band_ref[1] = jnp.where(column < row, band, 0.0).astype(jnp.bfloat16)
 
 
-def normalise(source_ref, band_ref, unit_ref, place, window):
+def normalise(source_ref, band_ref, unit_ref, tall_ref, place, window):
     rows, length = unit_ref.shape[1], source_ref.shape[-1]
     pieces = []
     for start in range(0, length, TILE):
@@ -84,37 +79,57 @@
         pieces.append(piece)
     filtered = jnp.concatenate(pieces, axis=1)
     meansq = jnp.mean(filtered * filtered, axis=-1, keepdims=True)
-    unit_ref[place, :, window * length : (window + 1) * length] = (
-        filtered * lax.rsqrt(meansq + 1e-06)
+    unit = filtered * lax.rsqrt(meansq + 1e-06)
+    unit_ref[place, :, window * length : (window + 1) * length] = unit.astype(jnp.bfloat16)
+    tall = unit.T
+    gap = jnp.zeros((FINE, rows), jnp.float32)
+    edge = jnp.zeros((MARGIN, rows), jnp.bfloat16)
+    inner = MARGIN - 2 * FINE
+    for phase in range(2):
+        tall_ref[place, window, phase, :MARGIN] = edge
+        tall_ref[place, window, phase, length + MARGIN :] = edge
+    tall_ref[place, window, 0, MARGIN : MARGIN + length] = tall.astype(jnp.bfloat16)
+    tall_ref[place, window, 1, inner : inner + length + 2 * FINE] = jnp.concatenate(
+        [gap, tall, gap], axis=0
     ).astype(jnp.bfloat16)
 
 
-def prepare(slot, sign, pairs_ref, unit_ref, left_ref, right_ref, half_rows):
-    _, channels, both = unit_ref.shape
-    length = both // 2
-    owner = lax.axis_index("chan")
+def prepare(source, sign, unit_ref, left_ref, half_rows):
+    length = unit_ref.shape[2] // 2
     first_row = pl.multiple_of(lax.axis_index("tm") * half_rows, half_rows)
-    source = place_of(pairs_ref[0, slot], owner)
-    partner = place_of(pairs_ref[1, slot], owner)
     for window in range(2):
         span = slice(window * length, (window + 1) * length)
         rows = unit_ref[source, pl.ds(first_row, half_rows), span]
         for place in range(FINE + 1 if sign > 0 else FINE):
             step = place if sign > 0 else place - FINE
             left_ref[place * half_rows : (place + 1) * half_rows, span] = shifted(rows, step)
-        rows = unit_ref[partner, :, span]
-        for place in range(COARSE):
-            right_ref[place * channels : (place + 1) * channels, span] = shifted(
-                rows, -sign * FINE * place
-            )
-
-
-def correlate(slot, sign, pair, factor, left_ref, right_ref, stage_ref, out_ref, sem):
+
+
+def coarse_rows(tall_ref, partner, window, amount):
+    length = tall_ref.shape[3] - 2 * MARGIN
+    phase = amount // FINE % 2
+    first = MARGIN + amount - FINE * phase
+    return tall_ref[partner, window, phase, first : first + length]
+
+
+def correlate(slot, sign, pair, factor, partner, left_ref, tall_ref, stage_ref, out_ref, sem):
     half_rows, channels = stage_ref.shape[1:]
     tall = FINE + 1 if sign > 0 and pair + 2 == COARSE else FINE
-    result = contract_lanes(
-        left_ref[: tall * half_rows, :],
-        right_ref[pair * channels : (pair + 2) * channels, :],
+    right = jnp.concatenate(
+        [
+            jnp.concatenate(
+                [
+                    coarse_rows(tall_ref, partner, window, sign * FINE * (pair + within))
+                    for within in range(2)
+                ],
+                axis=1,
+            )
+            for window in range(2)
+        ],
+        axis=0,
+    )
+    result = jnp.dot(
+        left_ref[: tall * half_rows, :], right, preferred_element_type=jnp.float32
     )
     lags = []
     for within in range(2):
@@ -135,39 +150,42 @@
 
 
 def early_kernel(pairs_ref, count_ref, taps_ref, *refs):
-    blocks, (band_ref, unit_ref) = refs[:2], refs[2:]
+    blocks, (band_ref, unit_ref, tall_ref) = refs[:2], refs[2:]
     make_band(taps_ref, band_ref)
     for window in range(2):
-        normalise(blocks[window], band_ref, unit_ref, OWN, window)
+        normalise(blocks[window], band_ref, unit_ref, tall_ref, OWN, window)
 
 
 def stage_kernel(scale, slots, places, pairs_ref, count_ref, band_ref, *refs):
     blocks = refs[: 2 * len(places)]
     refs = refs[2 * len(places) :]
-    refs = refs[1:] if len(slots) == 1 else refs[2:]
-    unit_ref, out_ref, left_ref, right_ref, stage_ref, sems = refs
+    refs = refs[2:] if len(slots) == 1 else refs[3:]
+    unit_ref, tall_ref, out_ref, left_ref, stage_ref, sems = refs
     for index, place in enumerate(places):
         for window in range(2):
-            normalise(blocks[2 * index + window], band_ref, unit_ref, place, window)
+            normalise(
+                blocks[2 * index + window], band_ref, unit_ref, tall_ref, place, window
+            )
     steps = [(index, slot, sign) for index, slot in enumerate(slots) for sign in (1, -1)]
+
+    owner = lax.axis_index("chan")
 
     def ready(number):
         if number < len(steps):
             _, slot, sign = steps[number]
-            prepare(
-                slot, sign, pairs_ref, unit_ref, left_ref.at[number % 2],
-                right_ref.at[number % 2], stage_ref.shape[2],
-            )
+            source = place_of(pairs_ref[0, slot], owner)
+            prepare(source, sign, unit_ref, left_ref.at[number % 2], stage_ref.shape[2])
 
     copies = []
     ready(0)
     for number, (index, slot, sign) in enumerate(steps):
         ready(number + 1)
         factor = jnp.where(slot < count_ref[0], scale, 0.0)
+        partner = place_of(pairs_ref[1, slot], owner)
         for pair in range(0, COARSE, 2):
             copies.append(
                 correlate(
-                    slot, sign, pair, factor, left_ref.at[number % 2], right_ref.at[number % 2],
+                    slot, sign, pair, factor, partner, left_ref.at[number % 2], tall_ref,
                     stage_ref.at[index], out_ref, sems.at[index, len(copies) % CHUNKS],
                 )
             )
@@ -189,16 +207,18 @@
     below = passed(block, "chan", lambda i: i + REACH)
     above = passed(block, "chan", lambda i: i - REACH)
     padded = jnp.pad(block, ((0, 16), (0, 0)))
-    diagonal = passed(padded, "chan", diagonal_of)
     own, pairs, count = block, pair_blocks.T, pair_count
     taps = fir_taps.astype(jnp.float32)[None, :]
 
     smem = pl.BlockSpec(memory_space=pltpu.SMEM)
     vmem = pl.BlockSpec(memory_space=pltpu.VMEM)
     hbm = pl.BlockSpec(memory_space=pl.ANY)
-    params = pltpu.CompilerParams(vmem_limit_bytes=40 * 1024 * 1024)
+    params = pltpu.CompilerParams(vmem_limit_bytes=32 * 1024 * 1024)
     band_shape = jax.ShapeDtypeStruct((2, TILE, TILE), jnp.bfloat16)
     unit_shape = jax.ShapeDtypeStruct((NEAR, rows, halves * length), jnp.bfloat16)
+    tall_shape = jax.ShapeDtypeStruct(
+        (NEAR, halves, 2, length + 2 * MARGIN, rows), jnp.bfloat16
+    )
     out_shape = jax.ShapeDtypeStruct((cap, lags, half_rows, rows), jnp.float32)
 
     light = pl.CostEstimate(flops=1, bytes_accessed=1, transcendentals=0)
@@ -208,18 +228,17 @@
         transcendentals=0,
     )
 
-    def stage(slots, places, blocks, band, unit, out):
-        aliased = [unit] if out is None else [unit, out]
+    def stage(slots, places, blocks, band, unit, tall, out):
+        aliased = [unit, tall] if out is None else [unit, tall, out]
         first = 3 + len(blocks)
         return pl.pallas_call(
             functools.partial(stage_kernel, scale, slots, places),
-            out_shape=(unit_shape, out_shape),
-            in_specs=[smem, smem, vmem] + [vmem] * len(blocks) + [vmem, hbm][: len(aliased)],
-            out_specs=(vmem, hbm),
+            out_shape=(unit_shape, tall_shape, out_shape),
+            in_specs=[smem, smem, vmem] + [vmem] * len(blocks) + [vmem, vmem, hbm][: len(aliased)],
+            out_specs=(vmem, vmem, hbm),
             input_output_aliases={first + i: i for i in range(len(aliased))},
             scratch_shapes=[
                 pltpu.VMEM((2, (FINE + 1) * half_rows, halves * length), jnp.bfloat16),
-                pltpu.VMEM((2, COARSE * rows, halves * length), jnp.bfloat16),
                 pltpu.VMEM((len(slots), lags, half_rows, rows), jnp.float32),
                 pltpu.SemaphoreType.DMA((len(slots), CHUNKS)),
             ],
@@ -227,22 +246,23 @@
             cost_estimate=light if out is None else heavy,
         )(pairs, count, band, *blocks, *aliased)
 
-    band, unit = pl.pallas_call(
+    band, unit, tall = pl.pallas_call(
         early_kernel,
-        out_shape=(band_shape, unit_shape),
+        out_shape=(band_shape, unit_shape, tall_shape),
         in_specs=[smem, smem] + [vmem] * 3,
-        out_specs=(vmem, vmem),
+        out_specs=(vmem, vmem, vmem),
         compiler_params=params,
         cost_estimate=light,
     )(pairs, count, taps, padded, swap(own))
-    partner, band = lax.optimization_barrier((partner, band))
-    unit, out = stage(
+    sent, band = lax.optimization_barrier((padded, band))
+    diagonal = passed(sent, "chan", diagonal_of)
+    unit, tall, out = stage(
         (0,), (ABOVE, BELOW, PARTNER),
-        (above, swap(above), below, swap(below), partner, swap(partner)), band, unit, None,
+        (above, swap(above), below, swap(below), partner, swap(partner)), band, unit, tall, None,
     )
     diagonal, unit = lax.optimization_barrier((diagonal, unit))
-    unit, out = stage(
-        tuple(range(1, cap)), (DIAGONAL,), (diagonal, swap(diagonal)), band, unit, out
+    unit, tall, out = stage(
+        tuple(range(1, cap)), (DIAGONAL,), (diagonal, swap(diagonal)), band, unit, tall, out
     )
     return jnp.transpose(out, (0, 2, 1, 3))
 

time: 36.5 us -> 35.6 us (0.975)
  waiting for transfers between devices: 7.94 us -> 6.37 us
  Pallas kernels: 16.1 us -> 16.7 us
    ppermute x9, waiting for transfers between devices: 7.94 us -> 6.37 us  [passed(): return lax.ppermute(block, axis, route)]
    pallas_call x2, Pallas kernels: 15 us -> 15.4 us  [stage(): pl.pallas_call(functools.partial(stage_kernel, scale, slots, places), out...]
  transfers between devices with their start and end apart: 9 -> 9, of which waited for: 5 -> 3; matrix products, arithmetic and copies ran while one was open for 4% -> 5% of each run, Pallas kernels for 18% -> 20%
where the time goes in v5:
time: 35.6 us; the launch traced here: 35.3 us
  Pallas kernels  16.7 us (47%)
  starting transfers between devices  9.18 us (26%)
  waiting for transfers between devices  6.37 us (18%)
  local copies, waits for them, and re-layouts  1.65 us (5%)
  between operations  0.73 us (2%)
  other arithmetic  0.66 us (2%)
    pallas_call x2, Pallas kernels, stage(): pl.pallas_call(functools.partial(stage_kernel, scale, slots, places), out...  15.4 us
    ppermute x9, starting transfers between devices, passed(): return lax.ppermute(block, axis, route)  9.18 us
    ppermute x9, waiting for transfers between devices, passed(): return lax.ppermute(block, axis, route)  6.37 us
    pallas_call x1, Pallas kernels, body(): pl.pallas_call(early_kernel, out_shape=(band_shape, unit_shape, tall_shap...  1.33 us
    pad x1, local copies, waits for them, and re-layouts, body(): padded = jnp.pad(block, ((0, 16), (0, 0)))  0.97 us
  transfers between devices with their start and end apart: 9, of which 3 were waited for; matrix products, arithmetic and copies ran while one was open for 5% of the time, Pallas kernels for 20%

profile of v5, /device:TPU:0, one launch (start us, length us, event | category | flops | bytes accessed | tf_op | source)
XLA Modules:
  0.0 35.3 jit_solution(3819421150085305997)
XLA Ops:
  0.0 0.5 %collective-permute-start = (bf16[128,1024]{1,0:T(8,128)(2,1)}, bf16[128,1024]{1,0:T(8,128)(2,1)S(1)}, u32[]{:S(2)}, u32[]{:S(2)}) collective-permute-start(bf16[128,1024]{1,0:T(8,128)(2,1)} %bitcast.9), channel_id=1, source_target_pairs={{0,1},{1,0},{2,3},{3,2},{4,5},{5,4},{6,7},{7,6},{8,9},{9,8},{10,11... | collective-permute-start | bytes 786440 | tf_op jit(solution)/shard_map/ppermute | solution.py:25
  0.5 2.5 %collective-permute-start.6 = (bf16[128,1024]{1,0:T(8,128)(2,1)}, bf16[128,1024]{1,0:T(8,128)(2,1)S(1)}, u32[]{:S(2)}, u32[]{:S(2)}) collective-permute-start(bf16[128,1024]{1,0:T(8,128)(2,1)} %bitcast.10), channel_id=1, source_target_pairs={{0,2},{2,0},{4,6},{6,4},{8,10},{10,8},{12,14},{14,12},{1,3},{3,1},... | collective-permute-start | bytes 786440 | tf_op jit(solution)/shard_map/ppermute | solution.py:25
  3.0 3.5 %collective-permute-start.4 = (bf16[128,1024]{1,0:T(8,128)(2,1)}, bf16[128,1024]{1,0:T(8,128)(2,1)S(1)}, u32[]{:S(2)}, u32[]{:S(2)}) collective-permute-start(bf16[128,1024]{1,0:T(8,128)(2,1)} %bitcast.11), channel_id=1, source_target_pairs={{0,4},{2,6},{4,8},{6,10},{8,12},{10,14},{1,5},{3,7},{5,9},{7,11},{... | collective-permute-start | bytes 786440 | tf_op jit(solution)/shard_map/ppermute | solution.py:25
  6.5 1.3 %collective-permute-start.2 = (bf16[128,1024]{1,0:T(8,128)(2,1)}, bf16[128,1024]{1,0:T(8,128)(2,1)S(1)}, u32[]{:S(2)}, u32[]{:S(2)}) collective-permute-start(bf16[128,1024]{1,0:T(8,128)(2,1)} %bitcast.12), channel_id=1, source_target_pairs={{4,0},{6,2},{8,4},{10,6},{12,8},{14,10},{5,1},{7,3},{9,5},{11,7},{... | collective-permute-start | bytes 786440 | tf_op jit(solution)/shard_map/ppermute | solution.py:25
  8.4 1.0 %pad.4.refs_0_ = bf16[144,1024]{1,0:T(8,128)(2,1)S(1)} pad(bf16[128,1024]{1,0:T(8,128)(2,1)} %bitcast.13, bf16[]{:T(256)} %constant.2.clone.1), padding=0_16x0_0 | pad | bytes 557058 | tf_op jit(solution)/shard_map/jit(_pad)/pad | solution.py:209
  9.4 0.7 %bitcast_convert_fusion.taps_ref = f32[1,64]{1,0:T(1,128)S(1)} fusion(bf16[64]{0:T(256)(128)(2,1)} %param.5), kind=kLoop, calls=%fused_computation | loop fusion | flops 64 | bytes 384 | tf_op jit(solution)/shard_map/broadcast_in_dim | solution.py:211
  10.0 0.0 collective-permute-done.refs_1_
  10.1 0.0 copy-start
  10.1 0.7 %copy-done = s32[4,2]{0,1:T(2,128)S(1)} copy-done((s32[4,2]{0,1:T(2,128)S(1)}, s32[4,2]{0,1:T(2,128)}, u32[]{:S(2)}) %copy-start) | copy-done | bytes 56
  10.7 1.3 %shard_map.46 = (bf16[2,256,256]{2,1,0:T(8,128)(2,1)S(1)}, bf16[5,128,2048]{2,1,0:T(8,128)(2,1)S(1)}, bf16[5,2,2,1088,128]{4,3,2,1,0:T(8,128)(2,1)S(1)}) custom-call(s32[2,4]{1,0:T(2,128)S(1)} %bitcast.6, s32[1]{0:T(128)S(6)} %copy.15.count_ref, f32[1,64]{1,0:T(1,128)S(1)} %bitcast_convert_fusion.taps_ref, bf16[144,1024]{1,0:T(8,128)(2,1)S(1)} %pad.4.refs_0_, ...), custom_call_target="tpu_custom_call" | custom-call | flops 1 | bytes 1 | tf_op jit(solution)/shard_map/pallas_call | solution.py:249
  12.1 0.7 %collective-permute-start.1 = (bf16[144,1024]{1,0:T(8,128)(2,1)S(1)}, bf16[144,1024]{1,0:T(8,128)(2,1)S(1)}, u32[]{:S(2)}, u32[]{:S(2)}) collective-permute-start(bf16[144,1024]{1,0:T(8,128)(2,1)S(1)} %pad.4.refs_0_), channel_id=1, source_target_pairs={{2,4},{4,2},{6,8},{8,6},{10,12},{12,10},{3,5},{5,3},{7,9},{9,7},{1... | collective-permute-start | bytes 884744 | tf_op jit(solution)/shard_map/ppermute | solution.py:25
  12.8 0.0 collective-permute-done.6.refs_4_
  12.8 0.1 collective-permute-start.7
  12.8 0.0 collective-permute-done.4.refs_2_
  12.9 0.5 %collective-permute-start.5 = (bf16[128,1024]{1,0:T(8,128)(2,1)S(1)}, bf16[128,1024]{1,0:T(8,128)(2,1)S(1)}, u32[]{:S(2)}, u32[]{:S(2)}) collective-permute-start(bf16[128,1024]{1,0:T(8,128)(2,1)S(1)} %collective-permute-done.4.refs_2_), channel_id=1, source_target_pairs={{0,1},{1,0},{2,3},{3,2},{4,5},{5,4},{6,7},{7,6},{8,9},{9,8},{10,11... | collective-permute-start | bytes 786440 | tf_op jit(solution)/shard_map/ppermute | solution.py:25
  13.3 3.4 %collective-permute-done.2.refs_0_ = bf16[128,1024]{1,0:T(8,128)(2,1)S(1)} collective-permute-done((bf16[128,1024]{1,0:T(8,128)(2,1)}, bf16[128,1024]{1,0:T(8,128)(2,1)S(1)}, u32[]{:S(2)}, u32[]{:S(2)}) %collective-permute-start.2) | collective-permute-done | bytes 262176 | tf_op jit(solution)/shard_map/ppermute | solution.py:25
  16.7 0.0 collective-permute-start.3
  16.7 0.0 collective-permute-done.7.refs_5_
  16.7 0.0 collective-permute-done.5.refs_3_
  16.7 1.5 %collective-permute-done.3.refs_1_ = bf16[128,1024]{1,0:T(8,128)(2,1)S(1)} collective-permute-done((bf16[128,1024]{1,0:T(8,128)(2,1)S(1)}, bf16[128,1024]{1,0:T(8,128)(2,1)S(1)}, u32[]{:S(2)}, u32[]{:S(2)}) %collective-permute-start.3) | collective-permute-done | bytes 262176 | tf_op jit(solution)/shard_map/ppermute | solution.py:25
  18.3 5.7 %shard_map.47 = (bf16[5,128,2048]{2,1,0:T(8,128)(2,1)S(1)}, bf16[5,2,2,1088,128]{4,3,2,1,0:T(8,128)(2,1)S(1)}, f32[4,65,64,128]{3,2,1,0:T(8,128)}) custom-call(s32[2,4]{1,0:T(2,128)S(1)} %bitcast.7, s32[1]{0:T(128)S(6)} %copy.15.count_ref, bf16[2,256,256]{2,1,0:T(8,128)(2,1)S(1)} %get-tuple-element.17.band_ref, ...), custom_call_target="tpu_custom_call", output_to_operand_aliasing={{0}: (9, {}), {1}: (10, {})} | custom-call | flops 1 | bytes 1 | tf_op jit(solution)/shard_map/pallas_call | solution.py:234
  24.0 0.0 collective-permute-done.1.refs_0_
  24.0 0.2 collective-permute-start.8
  24.2 1.5 %collective-permute-done.8.refs_1_ = bf16[144,1024]{1,0:T(8,128)(2,1)S(1)} collective-permute-done((bf16[144,1024]{1,0:T(8,128)(2,1)S(1)}, bf16[144,1024]{1,0:T(8,128)(2,1)S(1)}, u32[]{:S(2)}, u32[]{:S(2)}) %collective-permute-start.8) | collective-permute-done | bytes 294944 | tf_op jit(solution)/shard_map/ppermute | solution.py:25
  25.7 9.7 %shard_map.48 = (bf16[5,128,2048]{2,1,0:T(8,128)(2,1)S(1)}, bf16[5,2,2,1088,128]{4,3,2,1,0:T(8,128)(2,1)S(1)}, f32[4,65,64,128]{3,2,1,0:T(8,128)}) custom-call(s32[2,4]{1,0:T(2,128)S(1)} %bitcast.8, s32[1]{0:T(128)S(6)} %copy.15.count_ref, ...), custom_call_target="tpu_custom_call", output_to_operand_aliasing={{0}: (5, {}), {1}: (6, {}), {2}: (7, {})} | custom-call | flops 6543114240 | bytes 6389760 | tf_op jit(solution)/shard_map/pallas_call | solution.py:234
Async XLA Ops:
  0.0 10.0 %collective-permute-start = (bf16[128,1024]{1,0:T(8,128)(2,1)}, bf16[128,1024]{1,0:T(8,128)(2,1)S(1)}, u32[]{:S(2)}, u32[]{:S(2)}) collective-permute-start(bf16[128,1024]{1,0:T(8,128)(2,1)} %bitcast.9), channel_id=1, source_target_pairs={{0,1},{1,0},{2,3},{3,2},{4,5},{5,4},{6,7},{7,6},{8,9},{9,8},{10,11... | collective-permute-start | bytes 786440 | tf_op jit(solution)/shard_map/ppermute | solution.py:25
  0.5 12.3 %collective-permute-start.6 = (bf16[128,1024]{1,0:T(8,128)(2,1)}, bf16[128,1024]{1,0:T(8,128)(2,1)S(1)}, u32[]{:S(2)}, u32[]{:S(2)}) collective-permute-start(bf16[128,1024]{1,0:T(8,128)(2,1)} %bitcast.10), channel_id=1, source_target_pairs={{0,2},{2,0},{4,6},{6,4},{8,10},{10,8},{12,14},{14,12},{1,3},{3,1},... | collective-permute-start | bytes 786440 | tf_op jit(solution)/shard_map/ppermute | solution.py:25
  3.0 9.9 %collective-permute-start.4 = (bf16[128,1024]{1,0:T(8,128)(2,1)}, bf16[128,1024]{1,0:T(8,128)(2,1)S(1)}, u32[]{:S(2)}, u32[]{:S(2)}) collective-permute-start(bf16[128,1024]{1,0:T(8,128)(2,1)} %bitcast.11), channel_id=1, source_target_pairs={{0,4},{2,6},{4,8},{6,10},{8,12},{10,14},{1,5},{3,7},{5,9},{7,11},{... | collective-permute-start | bytes 786440 | tf_op jit(solution)/shard_map/ppermute | solution.py:25
  6.5 10.3 %collective-permute-start.2 = (bf16[128,1024]{1,0:T(8,128)(2,1)}, bf16[128,1024]{1,0:T(8,128)(2,1)S(1)}, u32[]{:S(2)}, u32[]{:S(2)}) collective-permute-start(bf16[128,1024]{1,0:T(8,128)(2,1)} %bitcast.12), channel_id=1, source_target_pairs={{4,0},{6,2},{8,4},{10,6},{12,8},{14,10},{5,1},{7,3},{9,5},{11,7},{... | collective-permute-start | bytes 786440 | tf_op jit(solution)/shard_map/ppermute | solution.py:25
  10.1 0.7 %copy-start = (s32[4,2]{0,1:T(2,128)S(1)}, s32[4,2]{0,1:T(2,128)}, u32[]{:S(2)}) copy-start(s32[4,2]{0,1:T(2,128)} %param.6) | copy-start | bytes 100
  12.1 11.9 %collective-permute-start.1 = (bf16[144,1024]{1,0:T(8,128)(2,1)S(1)}, bf16[144,1024]{1,0:T(8,128)(2,1)S(1)}, u32[]{:S(2)}, u32[]{:S(2)}) collective-permute-start(bf16[144,1024]{1,0:T(8,128)(2,1)S(1)} %pad.4.refs_0_), channel_id=1, source_target_pairs={{2,4},{4,2},{6,8},{8,6},{10,12},{12,10},{3,5},{5,3},{7,9},{9,7},{1... | collective-permute-start | bytes 884744 | tf_op jit(solution)/shard_map/ppermute | solution.py:25
  12.8 4.0 %collective-permute-start.7 = (bf16[128,1024]{1,0:T(8,128)(2,1)S(1)}, bf16[128,1024]{1,0:T(8,128)(2,1)S(1)}, u32[]{:S(2)}, u32[]{:S(2)}) collective-permute-start(bf16[128,1024]{1,0:T(8,128)(2,1)S(1)} %collective-permute-done.6.refs_4_), channel_id=1, source_target_pairs={{0,1},{1,0},{2,3},{3,2},{4,5},{5,4},{6,7},{7,6},{8,9},{9,8},{10,11... | collective-permute-start | bytes 786440 | tf_op jit(solution)/shard_map/ppermute | solution.py:25
  12.9 3.9 %collective-permute-start.5 = (bf16[128,1024]{1,0:T(8,128)(2,1)S(1)}, bf16[128,1024]{1,0:T(8,128)(2,1)S(1)}, u32[]{:S(2)}, u32[]{:S(2)}) collective-permute-start(bf16[128,1024]{1,0:T(8,128)(2,1)S(1)} %collective-permute-done.4.refs_2_), channel_id=1, source_target_pairs={{0,1},{1,0},{2,3},{3,2},{4,5},{5,4},{6,7},{7,6},{8,9},{9,8},{10,11... | collective-permute-start | bytes 786440 | tf_op jit(solution)/shard_map/ppermute | solution.py:25
  16.7 1.5 %collective-permute-start.3 = (bf16[128,1024]{1,0:T(8,128)(2,1)S(1)}, bf16[128,1024]{1,0:T(8,128)(2,1)S(1)}, u32[]{:S(2)}, u32[]{:S(2)}) collective-permute-start(bf16[128,1024]{1,0:T(8,128)(2,1)S(1)} %collective-permute-done.2.refs_0_), channel_id=1, source_target_pairs={{0,1},{1,0},{2,3},{3,2},{4,5},{5,4},{6,7},{7,6},{8,9},{9,8},{10,11... | collective-permute-start | bytes 786440 | tf_op jit(solution)/shard_map/ppermute | solution.py:25
  24.0 1.6 %collective-permute-start.8 = (bf16[144,1024]{1,0:T(8,128)(2,1)S(1)}, bf16[144,1024]{1,0:T(8,128)(2,1)S(1)}, u32[]{:S(2)}, u32[]{:S(2)}) collective-permute-start(bf16[144,1024]{1,0:T(8,128)(2,1)S(1)} %collective-permute-done.1.refs_0_), channel_id=1, source_target_pairs={{0,1},{1,0},{2,3},{3,2},{4,5},{5,4},{6,7},{7,6},{8,9},{9,8},{10,11... | collective-permute-start | bytes 884744 | tf_op jit(solution)/shard_map/ppermute | solution.py:25

commit v6 on v5

--- a/solution.py
+++ b/solution.py
@@ -14,7 +14,6 @@
 COARSE = LAG // FINE
 LANES = 128
 TILE = 256
-CHUNKS = 4
 MARGIN = 32
 OWN, PARTNER, BELOW, ABOVE, DIAGONAL = range(NEAR)
 
@@ -112,37 +111,43 @@
     return tall_ref[partner, window, phase, first : first + length]
 
 
-def correlate(slot, sign, pair, factor, partner, left_ref, tall_ref, stage_ref, out_ref, sem):
-    half_rows, channels = stage_ref.shape[1:]
-    tall = FINE + 1 if sign > 0 and pair + 2 == COARSE else FINE
-    right = jnp.concatenate(
+def coarse_columns(tall_ref, partner, amounts):
+    return jnp.concatenate(
         [
             jnp.concatenate(
-                [
-                    coarse_rows(tall_ref, partner, window, sign * FINE * (pair + within))
-                    for within in range(2)
-                ],
-                axis=1,
+                [coarse_rows(tall_ref, partner, window, amount) for amount in amounts], axis=1
             )
             for window in range(2)
         ],
         axis=0,
     )
+
+
+def correlate(slot, sign, factor, partner, left_ref, tall_ref, stage_ref, out_ref, sem):
+    half_rows, channels = stage_ref.shape[1:]
+    amounts = [sign * FINE * place for place in range(COARSE)]
+    lags = []
+
+    def keep(result, base, steps, amounts):
+        for column, amount in enumerate(amounts):
+            for row, step in enumerate(steps):
+                stage_ref[base + amount + step] = factor * result[
+                    row * half_rows : (row + 1) * half_rows,
+                    column * channels : (column + 1) * channels,
+                ]
+                lags.append(base + amount + step)
+
     result = jnp.dot(
-        left_ref[: tall * half_rows, :], right, preferred_element_type=jnp.float32
-    )
-    lags = []
-    for within in range(2):
-        for place in range(tall):
-            if place == FINE and within == 0:
-                continue
-            coarse = sign * FINE * (pair + within)
-            lag = LAG + coarse + (place if sign > 0 else place - FINE)
-            stage_ref[lag] = factor * result[
-                place * half_rows : (place + 1) * half_rows,
-                within * channels : (within + 1) * channels,
-            ]
-            lags.append(lag)
+        left_ref[: FINE * half_rows, :], coarse_columns(tall_ref, partner, amounts),
+        preferred_element_type=jnp.float32,
+    )
+    keep(result, LAG, range(FINE) if sign > 0 else range(-FINE, 0), amounts)
+    if sign > 0:
+        result = jnp.dot(
+            left_ref[FINE * half_rows :, :], coarse_columns(tall_ref, partner, amounts[-1:]),
+            preferred_element_type=jnp.float32,
+        )
+        keep(result, LAG, [FINE], amounts[-1:])
     span = pl.ds(min(lags), len(lags))
     copy = pltpu.make_async_copy(stage_ref.at[span], out_ref.at[slot, span], sem)
     copy.start()
@@ -156,46 +161,46 @@
         normalise(blocks[window], band_ref, unit_ref, tall_ref, OWN, window)
 
 
-def stage_kernel(scale, slots, places, pairs_ref, count_ref, band_ref, *refs):
-    blocks = refs[: 2 * len(places)]
-    refs = refs[2 * len(places) :]
-    refs = refs[2:] if len(slots) == 1 else refs[3:]
+def filter_kernel(units, band_ref, *refs):
+    blocks, (unit_ref, tall_ref) = refs[: len(units)], refs[len(units) + 2 :]
+    for block, (place, window) in zip(blocks, units):
+        normalise(block, band_ref, unit_ref, tall_ref, place, window)
+
+
+def stack_kernel(scale, units, pairs_ref, count_ref, band_ref, *refs):
+    blocks, refs = refs[: len(units)], refs[len(units) + 2 :]
     unit_ref, tall_ref, out_ref, left_ref, stage_ref, sems = refs
-    for index, place in enumerate(places):
-        for window in range(2):
-            normalise(
-                blocks[2 * index + window], band_ref, unit_ref, tall_ref, place, window
-            )
-    steps = [(index, slot, sign) for index, slot in enumerate(slots) for sign in (1, -1)]
-
+    for block, (place, window) in zip(blocks, units):
+        normalise(block, band_ref, unit_ref, tall_ref, place, window)
+    slots = out_ref.shape[0]
+    steps = [(slot, sign) for slot in range(slots) for sign in (1, -1)]
     owner = lax.axis_index("chan")
 
     def ready(number):
         if number < len(steps):
-            _, slot, sign = steps[number]
+            slot, sign = steps[number]
             source = place_of(pairs_ref[0, slot], owner)
             prepare(source, sign, unit_ref, left_ref.at[number % 2], stage_ref.shape[2])
 
     copies = []
     ready(0)
-    for number, (index, slot, sign) in enumerate(steps):
+    for number, (slot, sign) in enumerate(steps):
         ready(number + 1)
         factor = jnp.where(slot < count_ref[0], scale, 0.0)
         partner = place_of(pairs_ref[1, slot], owner)
-        for pair in range(0, COARSE, 2):
-            copies.append(
-                correlate(
-                    slot, sign, pair, factor, partner, left_ref.at[number % 2], tall_ref,
-                    stage_ref.at[index], out_ref, sems.at[index, len(copies) % CHUNKS],
-                )
+        copies.append(
+            correlate(
+                slot, sign, factor, partner, left_ref.at[number % 2], tall_ref,
+                stage_ref.at[slot], out_ref, sems.at[number],
             )
+        )
     for copy in copies:
         copy.wait()
 
 
 def body(traces, fir_taps, pair_blocks, pair_count):
     rows, windows, length = traces.shape
-    block = traces.reshape(rows, length)
+    own = traces.reshape(rows, length)
     halves = lax.axis_size("tm")
     cap = pair_blocks.shape[0]
     lags = 2 * LAG + 1
@@ -203,11 +208,11 @@
     scale = float(windows * halves * length) ** (-0.5)
 
     swap = lambda array: passed(array, "tm", lambda i: 1 - i)
-    partner = passed(block, "chan", partner_of)
-    below = passed(block, "chan", lambda i: i + REACH)
-    above = passed(block, "chan", lambda i: i - REACH)
-    padded = jnp.pad(block, ((0, 16), (0, 0)))
-    own, pairs, count = block, pair_blocks.T, pair_count
+    partner = passed(own, "chan", partner_of)
+    below = passed(own, "chan", lambda i: i + REACH)
+    above = passed(own, "chan", lambda i: i - REACH)
+    diagonal = passed(own, "chan", diagonal_of)
+    pairs, count = pair_blocks.T, pair_count
     taps = fir_taps.astype(jnp.float32)[None, :]
 
     smem = pl.BlockSpec(memory_space=pltpu.SMEM)
@@ -220,31 +225,12 @@
         (NEAR, halves, 2, length + 2 * MARGIN, rows), jnp.bfloat16
     )
     out_shape = jax.ShapeDtypeStruct((cap, lags, half_rows, rows), jnp.float32)
-
     light = pl.CostEstimate(flops=1, bytes_accessed=1, transcendentals=0)
     heavy = pl.CostEstimate(
-        flops=2 * (cap - 1) * lags * half_rows * rows * halves * length,
-        bytes_accessed=(cap - 1) * lags * half_rows * rows * 4,
+        flops=2 * cap * lags * half_rows * rows * halves * length,
+        bytes_accessed=cap * lags * half_rows * rows * 4,
         transcendentals=0,
     )
-
-    def stage(slots, places, blocks, band, unit, tall, out):
-        aliased = [unit, tall] if out is None else [unit, tall, out]
-        first = 3 + len(blocks)
-        return pl.pallas_call(
-            functools.partial(stage_kernel, scale, slots, places),
-            out_shape=(unit_shape, tall_shape, out_shape),
-            in_specs=[smem, smem, vmem] + [vmem] * len(blocks) + [vmem, vmem, hbm][: len(aliased)],
-            out_specs=(vmem, vmem, hbm),
-            input_output_aliases={first + i: i for i in range(len(aliased))},
-            scratch_shapes=[
-                pltpu.VMEM((2, (FINE + 1) * half_rows, halves * length), jnp.bfloat16),
-                pltpu.VMEM((len(slots), lags, half_rows, rows), jnp.float32),
-                pltpu.SemaphoreType.DMA((len(slots), CHUNKS)),
-            ],
-            compiler_params=params,
-            cost_estimate=light if out is None else heavy,
-        )(pairs, count, band, *blocks, *aliased)
 
     band, unit, tall = pl.pallas_call(
         early_kernel,
@@ -253,17 +239,42 @@
         out_specs=(vmem, vmem, vmem),
         compiler_params=params,
         cost_estimate=light,
-    )(pairs, count, taps, padded, swap(own))
-    sent, band = lax.optimization_barrier((padded, band))
-    diagonal = passed(sent, "chan", diagonal_of)
-    unit, tall, out = stage(
-        (0,), (ABOVE, BELOW, PARTNER),
-        (above, swap(above), below, swap(below), partner, swap(partner)), band, unit, tall, None,
-    )
-    diagonal, unit = lax.optimization_barrier((diagonal, unit))
-    unit, tall, out = stage(
-        tuple(range(1, cap)), (DIAGONAL,), (diagonal, swap(diagonal)), band, unit, tall, out
-    )
+    )(pairs, count, taps, own, swap(own))
+
+    def more(units, blocks, unit, tall):
+        return pl.pallas_call(
+            functools.partial(filter_kernel, units),
+            out_shape=(unit_shape, tall_shape),
+            in_specs=[vmem] * (len(units) + 3),
+            out_specs=(vmem, vmem),
+            input_output_aliases={len(units) + 1: 0, len(units) + 2: 1},
+            compiler_params=params,
+            cost_estimate=light,
+        )(band, *blocks, unit, tall)
+
+    mine, other = 0, 1
+    diagonal, band = lax.optimization_barrier((diagonal, band))
+    unit, tall = more(
+        ((DIAGONAL, mine), (DIAGONAL, other)), (diagonal, swap(diagonal)), unit, tall
+    )
+    unit, tall = more(
+        ((ABOVE, mine), (BELOW, mine), (PARTNER, mine)), (above, below, partner), unit, tall
+    )
+    units = ((ABOVE, other), (BELOW, other), (PARTNER, other))
+    _, _, out = pl.pallas_call(
+        functools.partial(stack_kernel, scale, units),
+        out_shape=(unit_shape, tall_shape, out_shape),
+        in_specs=[smem, smem] + [vmem] * (len(units) + 3),
+        out_specs=(vmem, vmem, hbm),
+        input_output_aliases={len(units) + 3: 0, len(units) + 4: 1},
+        scratch_shapes=[
+            pltpu.VMEM((2, (FINE + 1) * half_rows, halves * length), jnp.bfloat16),
+            pltpu.VMEM((cap, lags, half_rows, rows), jnp.float32),
+            pltpu.SemaphoreType.DMA((2 * cap,)),
+        ],
+        compiler_params=params,
+        cost_estimate=heavy,
+    )(pairs, count, band, swap(above), swap(below), swap(partner), unit, tall)
     return jnp.transpose(out, (0, 2, 1, 3))
 
 

time: 35.6 us -> 33.7 us (0.947)
  starting transfers between devices: 9.18 us -> 11.8 us
  waiting for transfers between devices: 6.37 us -> 3.83 us
  Pallas kernels: 16.7 us -> 14.7 us
    ppermute x9, starting transfers between devices: 9.18 us -> 11.8 us  [passed(): return lax.ppermute(block, axis, route)]
    ppermute x9, waiting for transfers between devices: 6.37 us -> 3.83 us  [passed(): return lax.ppermute(block, axis, route)]
    pallas_call x2 -> x3, Pallas kernels: 15.4 us -> 13.4 us  [the longest x1 11.8 us: body(): pl.pallas_call(functools.partial(stack_kernel, scale, units), out_shape=(...]
    pad x1 -> x0, local copies, waits for them, and re-layouts: 0.97 us -> none  [body(): padded = jnp.pad(block, ((0, 16), (0, 0)))]
    unnamed x2 -> x6, local copies, waits for them, and re-layouts: 0.68 us -> 1.64 us
  transfers between devices with their start and end apart: 9 -> 9, of which waited for: 3 -> 2; matrix products, arithmetic and copies ran while one was open for 5% -> 2% of each run, Pallas kernels for 20% -> 9%
where the time goes in v6:
time: 33.7 us; the launch traced here: 33.4 us
  Pallas kernels  14.7 us (44%)
  starting transfers between devices  11.8 us (35%)
  waiting for transfers between devices  3.83 us (11%)
  local copies, waits for them, and re-layouts  1.64 us (5%)
  between operations  0.75 us (2%)
  other arithmetic  0.66 us (2%)
    ppermute x9, starting transfers between devices, passed(): return lax.ppermute(block, axis, route)  11.8 us
    pallas_call x1, Pallas kernels, body(): pl.pallas_call(functools.partial(stack_kernel, scale, units), out_shape=(...  11.8 us
    ppermute x9, waiting for transfers between devices, passed(): return lax.ppermute(block, axis, route)  3.83 us
    unnamed x6, local copies, waits for them, and re-layouts  1.64 us
    pallas_call x2, Pallas kernels, more(): pl.pallas_call(functools.partial(filter_kernel, units), out_shape=(unit_s...  1.59 us
    pallas_call x1, Pallas kernels, body(): pl.pallas_call(early_kernel, out_shape=(band_shape, unit_shape, tall_shap...  1.33 us
  transfers between devices with their start and end apart: 9, of which 2 were waited for; matrix products, arithmetic and copies ran while one was open for 2% of the time, Pallas kernels for 9%

profile of v6, /device:TPU:0, one launch (start us, length us, event | category | flops | bytes accessed | tf_op | source)
XLA Modules:
  0.0 33.4 jit_solution(13737842090153433298)
XLA Ops:
  0.0 0.5 %collective-permute-start.1 = (bf16[128,1024]{1,0:T(8,128)(2,1)}, bf16[128,1024]{1,0:T(8,128)(2,1)S(1)}, u32[]{:S(2)}, u32[]{:S(2)}) collective-permute-start(bf16[128,1024]{1,0:T(8,128)(2,1)} %bitcast.6), channel_id=1, source_target_pairs={{0,1},{1,0},{2,3},{3,2},{4,5},{5,4},{6,7},{7,6},{8,9},{9,8},{10,11... | collective-permute-start | bytes 786440 | tf_op jit(solution)/shard_map/ppermute | solution.py:24
  0.5 0.7 %collective-permute-start = (bf16[128,1024]{1,0:T(8,128)(2,1)}, bf16[128,1024]{1,0:T(8,128)(2,1)S(1)}, u32[]{:S(2)}, u32[]{:S(2)}) collective-permute-start(bf16[128,1024]{1,0:T(8,128)(2,1)} %bitcast.7), channel_id=1, source_target_pairs={{2,4},{4,2},{6,8},{8,6},{10,12},{12,10},{3,5},{5,3},{7,9},{9,7},{1... | collective-permute-start | bytes 786440 | tf_op jit(solution)/shard_map/ppermute | solution.py:24
  1.1 5.3 %collective-permute-start.6 = (bf16[128,1024]{1,0:T(8,128)(2,1)}, bf16[128,1024]{1,0:T(8,128)(2,1)S(1)}, u32[]{:S(2)}, u32[]{:S(2)}) collective-permute-start(bf16[128,1024]{1,0:T(8,128)(2,1)} %bitcast.8), channel_id=1, source_target_pairs={{0,2},{2,0},{4,6},{6,4},{8,10},{10,8},{12,14},{14,12},{1,3},{3,1},... | collective-permute-start | bytes 786440 | tf_op jit(solution)/shard_map/ppermute | solution.py:24
  6.5 3.5 %collective-permute-start.4 = (bf16[128,1024]{1,0:T(8,128)(2,1)}, bf16[128,1024]{1,0:T(8,128)(2,1)S(1)}, u32[]{:S(2)}, u32[]{:S(2)}) collective-permute-start(bf16[128,1024]{1,0:T(8,128)(2,1)} %bitcast.9), channel_id=1, source_target_pairs={{0,4},{2,6},{4,8},{6,10},{8,12},{10,14},{1,5},{3,7},{5,9},{7,11},{... | collective-permute-start | bytes 786440 | tf_op jit(solution)/shard_map/ppermute | solution.py:24
  10.0 1.3 %collective-permute-start.2 = (bf16[128,1024]{1,0:T(8,128)(2,1)}, bf16[128,1024]{1,0:T(8,128)(2,1)S(1)}, u32[]{:S(2)}, u32[]{:S(2)}) collective-permute-start(bf16[128,1024]{1,0:T(8,128)(2,1)} %bitcast.10), channel_id=1, source_target_pairs={{4,0},{6,2},{8,4},{10,6},{12,8},{14,10},{5,1},{7,3},{9,5},{11,7},{... | collective-permute-start | bytes 786440 | tf_op jit(solution)/shard_map/ppermute | solution.py:24
  11.9 0.7 %bitcast_convert_fusion.taps_ref = f32[1,64]{1,0:T(1,128)S(1)} fusion(bf16[64]{0:T(256)(128)(2,1)} %param.5), kind=kLoop, calls=%fused_computation | loop fusion | flops 64 | bytes 384 | tf_op jit(solution)/shard_map/broadcast_in_dim | solution.py:216
  12.6 0.0 collective-permute-done.1.refs_1_
  12.6 0.0 copy-start
  12.6 0.9 %copy-done = bf16[128,1,1024]{2,0,1:T(8,128)(2,1)S(1)} copy-done((bf16[128,1,1024]{2,0,1:T(8,128)(2,1)S(1)}, bf16[128,1,1024]{2,0,1:T(8,128)(2,1)}, u32[]{:S(2)}) %copy-start) | copy-done | bytes 262168
  13.5 0.0 copy-start.1
  13.5 0.7 %copy-done.1 = s32[4,2]{0,1:T(2,128)S(1)} copy-done((s32[4,2]{0,1:T(2,128)S(1)}, s32[4,2]{0,1:T(2,128)}, u32[]{:S(2)}) %copy-start.1) | copy-done | bytes 56
  14.2 1.3 %shard_map.46 = (bf16[2,256,256]{2,1,0:T(8,128)(2,1)S(1)}, bf16[5,128,2048]{2,1,0:T(8,128)(2,1)S(1)}, bf16[5,2,2,1088,128]{4,3,2,1,0:T(8,128)(2,1)S(1)}) custom-call(s32[2,4]{1,0:T(2,128)S(1)} %bitcast.12, s32[1]{0:T(128)S(6)} %copy.17.count_ref, f32[1,64]{1,0:T(1,128)S(1)} %bitcast_convert_fusion.taps_ref, bf16[128,1024]{1,0:T(8,128)(2,1)S(1)} %bitcast.11, ...), custom_call_target="tpu_custom_call" | custom-call | flops 1 | bytes 1 | tf_op jit(solution)/shard_map/pallas_call | solution.py:235
  15.5 0.0 collective-permute-done.refs_0_
  15.5 0.1 collective-permute-start.8
  15.6 2.3 %collective-permute-done.6.refs_2_ = bf16[128,1024]{1,0:T(8,128)(2,1)S(1)} collective-permute-done((bf16[128,1024]{1,0:T(8,128)(2,1)}, bf16[128,1024]{1,0:T(8,128)(2,1)S(1)}, u32[]{:S(2)}, u32[]{:S(2)}) %collective-permute-start.6) | collective-permute-done | bytes 262176 | tf_op jit(solution)/shard_map/ppermute | solution.py:24
  17.9 0.0 collective-permute-start.7
  18.0 0.0 collective-permute-done.4.refs_1_
  18.0 0.5 %collective-permute-start.5 = (bf16[128,1024]{1,0:T(8,128)(2,1)S(1)}, bf16[128,1024]{1,0:T(8,128)(2,1)S(1)}, u32[]{:S(2)}, u32[]{:S(2)}) collective-permute-start(bf16[128,1024]{1,0:T(8,128)(2,1)S(1)} %collective-permute-done.4.refs_1_), channel_id=1, source_target_pairs={{0,1},{1,0},{2,3},{3,2},{4,5},{5,4},{6,7},{7,6},{8,9},{9,8},{10,11... | collective-permute-start | bytes 786440 | tf_op jit(solution)/shard_map/ppermute | solution.py:24
  18.4 1.5 %collective-permute-done.2.refs_0_ = bf16[128,1024]{1,0:T(8,128)(2,1)S(1)} collective-permute-done((bf16[128,1024]{1,0:T(8,128)(2,1)}, bf16[128,1024]{1,0:T(8,128)(2,1)S(1)}, u32[]{:S(2)}, u32[]{:S(2)}) %collective-permute-start.2) | collective-permute-done | bytes 262176 | tf_op jit(solution)/shard_map/ppermute | solution.py:24
  19.9 0.0 collective-permute-start.3
  19.9 0.0 collective-permute-done.8.refs_1_
  19.9 0.7 %shard_map.47 = (bf16[5,128,2048]{2,1,0:T(8,128)(2,1)S(1)}, bf16[5,2,2,1088,128]{4,3,2,1,0:T(8,128)(2,1)S(1)}) custom-call(bf16[2,256,256]{2,1,0:T(8,128)(2,1)S(1)} %get-tuple-element.16.band_ref, bf16[128,1024]{1,0:T(8,128)(2,1)S(1)} %collective-permute-done.refs_0_, ...), custom_call_target="tpu_custom_call", output_to_operand_aliasing={{0}: (3, {}), {1}: (4, {})} | custom-call | flops 1 | bytes 1 | tf_op jit(solution)/shard_map/pallas_call | solution.py:245
  20.6 0.0 copy-start.2
  20.6 0.9 %shard_map.48 = (bf16[5,128,2048]{2,1,0:T(8,128)(2,1)S(1)}, bf16[5,2,2,1088,128]{4,3,2,1,0:T(8,128)(2,1)S(1)}) custom-call(bf16[2,256,256]{2,1,0:T(8,128)(2,1)S(1)} %get-tuple-element.16.band_ref, bf16[128,1024]{1,0:T(8,128)(2,1)S(1)} %collective-permute-done.2.refs_0_, ...), custom_call_target="tpu_custom_call", output_to_operand_aliasing={{0}: (4, {}), {1}: (5, {})} | custom-call | flops 1 | bytes 1 | tf_op jit(solution)/shard_map/pallas_call | solution.py:245
  21.6 0.0 collective-permute-done.7.refs_2_
  21.6 0.0 collective-permute-done.5.refs_1_
  21.6 0.0 collective-permute-done.3.refs_0_
  21.6 0.0 copy-done.2
  21.6 11.8 %shard_map.49 = (bf16[5,128,2048]{2,1,0:T(8,128)(2,1)S(1)}, bf16[5,2,2,1088,128]{4,3,2,1,0:T(8,128)(2,1)S(1)}, f32[4,65,64,128]{3,2,1,0:T(8,128)}) custom-call(s32[2,4]{1,0:T(2,128)S(1)} %bitcast.13, s32[1]{0:T(128)S(6)} %copy.17.count_ref, bf16[2,256,256]{2,1,0:T(8,128)(2,1)S(1)} %get-tuple-element.16.band_ref, ...), custom_call_target="tpu_custom_call", output_to_operand_aliasing={{0}: (6, {}), {1}: (7, {})} | custom-call | flops 8724152320 | bytes 8519680 | tf_op jit(solution)/shard_map/pallas_call | solution.py:264
Async XLA Ops:
  0.0 12.6 %collective-permute-start.1 = (bf16[128,1024]{1,0:T(8,128)(2,1)}, bf16[128,1024]{1,0:T(8,128)(2,1)S(1)}, u32[]{:S(2)}, u32[]{:S(2)}) collective-permute-start(bf16[128,1024]{1,0:T(8,128)(2,1)} %bitcast.6), channel_id=1, source_target_pairs={{0,1},{1,0},{2,3},{3,2},{4,5},{5,4},{6,7},{7,6},{8,9},{9,8},{10,11... | collective-permute-start | bytes 786440 | tf_op jit(solution)/shard_map/ppermute | solution.py:24
  0.5 15.1 %collective-permute-start = (bf16[128,1024]{1,0:T(8,128)(2,1)}, bf16[128,1024]{1,0:T(8,128)(2,1)S(1)}, u32[]{:S(2)}, u32[]{:S(2)}) collective-permute-start(bf16[128,1024]{1,0:T(8,128)(2,1)} %bitcast.7), channel_id=1, source_target_pairs={{2,4},{4,2},{6,8},{8,6},{10,12},{12,10},{3,5},{5,3},{7,9},{9,7},{1... | collective-permute-start | bytes 786440 | tf_op jit(solution)/shard_map/ppermute | solution.py:24
  1.1 16.8 %collective-permute-start.6 = (bf16[128,1024]{1,0:T(8,128)(2,1)}, bf16[128,1024]{1,0:T(8,128)(2,1)S(1)}, u32[]{:S(2)}, u32[]{:S(2)}) collective-permute-start(bf16[128,1024]{1,0:T(8,128)(2,1)} %bitcast.8), channel_id=1, source_target_pairs={{0,2},{2,0},{4,6},{6,4},{8,10},{10,8},{12,14},{14,12},{1,3},{3,1},... | collective-permute-start | bytes 786440 | tf_op jit(solution)/shard_map/ppermute | solution.py:24
  6.5 11.5 %collective-permute-start.4 = (bf16[128,1024]{1,0:T(8,128)(2,1)}, bf16[128,1024]{1,0:T(8,128)(2,1)S(1)}, u32[]{:S(2)}, u32[]{:S(2)}) collective-permute-start(bf16[128,1024]{1,0:T(8,128)(2,1)} %bitcast.9), channel_id=1, source_target_pairs={{0,4},{2,6},{4,8},{6,10},{8,12},{10,14},{1,5},{3,7},{5,9},{7,11},{... | collective-permute-start | bytes 786440 | tf_op jit(solution)/shard_map/ppermute | solution.py:24
  10.0 10.0 %collective-permute-start.2 = (bf16[128,1024]{1,0:T(8,128)(2,1)}, bf16[128,1024]{1,0:T(8,128)(2,1)S(1)}, u32[]{:S(2)}, u32[]{:S(2)}) collective-permute-start(bf16[128,1024]{1,0:T(8,128)(2,1)} %bitcast.10), channel_id=1, source_target_pairs={{4,0},{6,2},{8,4},{10,6},{12,8},{14,10},{5,1},{7,3},{9,5},{11,7},{... | collective-permute-start | bytes 786440 | tf_op jit(solution)/shard_map/ppermute | solution.py:24
  12.6 1.0 %copy-start = (bf16[128,1,1024]{2,0,1:T(8,128)(2,1)S(1)}, bf16[128,1,1024]{2,0,1:T(8,128)(2,1)}, u32[]{:S(2)}) copy-start(bf16[128,1,1024]{2,0,1:T(8,128)(2,1)} %param.4) | copy-start | bytes 786436
  13.5 0.7 %copy-start.1 = (s32[4,2]{0,1:T(2,128)S(1)}, s32[4,2]{0,1:T(2,128)}, u32[]{:S(2)}) copy-start(s32[4,2]{0,1:T(2,128)} %param.6) | copy-start | bytes 100
  15.5 4.4 %collective-permute-start.8 = (bf16[128,1024]{1,0:T(8,128)(2,1)S(1)}, bf16[128,1024]{1,0:T(8,128)(2,1)S(1)}, u32[]{:S(2)}, u32[]{:S(2)}) collective-permute-start(bf16[128,1024]{1,0:T(8,128)(2,1)S(1)} %collective-permute-done.refs_0_), channel_id=1, source_target_pairs={{0,1},{1,0},{2,3},{3,2},{4,5},{5,4},{6,7},{7,6},{8,9},{9,8},{10,11... | collective-permute-start | bytes 786440 | tf_op jit(solution)/shard_map/ppermute | solution.py:24
  17.9 3.6 %collective-permute-start.7 = (bf16[128,1024]{1,0:T(8,128)(2,1)S(1)}, bf16[128,1024]{1,0:T(8,128)(2,1)S(1)}, u32[]{:S(2)}, u32[]{:S(2)}) collective-permute-start(bf16[128,1024]{1,0:T(8,128)(2,1)S(1)} %collective-permute-done.6.refs_2_), channel_id=1, source_target_pairs={{0,1},{1,0},{2,3},{3,2},{4,5},{5,4},{6,7},{7,6},{8,9},{9,8},{10,11... | collective-permute-start | bytes 786440 | tf_op jit(solution)/shard_map/ppermute | solution.py:24
  18.0 3.6 %collective-permute-start.5 = (bf16[128,1024]{1,0:T(8,128)(2,1)S(1)}, bf16[128,1024]{1,0:T(8,128)(2,1)S(1)}, u32[]{:S(2)}, u32[]{:S(2)}) collective-permute-start(bf16[128,1024]{1,0:T(8,128)(2,1)S(1)} %collective-permute-done.4.refs_1_), channel_id=1, source_target_pairs={{0,1},{1,0},{2,3},{3,2},{4,5},{5,4},{6,7},{7,6},{8,9},{9,8},{10,11... | collective-permute-start | bytes 786440 | tf_op jit(solution)/shard_map/ppermute | solution.py:24
  19.9 1.6 %collective-permute-start.3 = (bf16[128,1024]{1,0:T(8,128)(2,1)S(1)}, bf16[128,1024]{1,0:T(8,128)(2,1)S(1)}, u32[]{:S(2)}, u32[]{:S(2)}) collective-permute-start(bf16[128,1024]{1,0:T(8,128)(2,1)S(1)} %collective-permute-done.2.refs_0_), channel_id=1, source_target_pairs={{0,1},{1,0},{2,3},{3,2},{4,5},{5,4},{6,7},{7,6},{8,9},{9,8},{10,11... | collective-permute-start | bytes 786440 | tf_op jit(solution)/shard_map/ppermute | solution.py:24
  20.6 1.0 %copy-start.2 = (s32[4,2]{0,1:T(2,128)S(1)}, s32[4,2]{0,1:T(2,128)}, u32[]{:S(2)}) copy-start(s32[4,2]{0,1:T(2,128)} %param.6) | copy-start | bytes 100

commit v7 on v6

--- a/solution.py
+++ b/solution.py
@@ -65,17 +65,16 @@
 
 def normalise(source_ref, band_ref, unit_ref, tall_ref, place, window):
     rows, length = unit_ref.shape[1], source_ref.shape[-1]
-    pieces = []
-    for start in range(0, length, TILE):
-        piece = jnp.dot(
-            source_ref[:rows, start : start + TILE], band_ref[0], preferred_element_type=jnp.float32
-        )
-        if start > 0:
-            piece += jnp.dot(
-                source_ref[:rows, start - TILE : start], band_ref[1],
-                preferred_element_type=jnp.float32,
-            )
-        pieces.append(piece)
+    tiles = length // TILE
+    stacked = jnp.concatenate(
+        [source_ref[:rows, tile * TILE : (tile + 1) * TILE] for tile in range(tiles)], axis=0
+    )
+    here = jnp.dot(stacked, band_ref[0], preferred_element_type=jnp.float32)
+    after = jnp.dot(stacked[:-rows], band_ref[1], preferred_element_type=jnp.float32)
+    pieces = [here[:rows]] + [
+        here[tile * rows : (tile + 1) * rows] + after[(tile - 1) * rows : tile * rows]
+        for tile in range(1, tiles)
+    ]
     filtered = jnp.concatenate(pieces, axis=1)
     meansq = jnp.mean(filtered * filtered, axis=-1, keepdims=True)
     unit = filtered * lax.rsqrt(meansq + 1e-06)
@@ -126,28 +125,21 @@
 def correlate(slot, sign, factor, partner, left_ref, tall_ref, stage_ref, out_ref, sem):
     half_rows, channels = stage_ref.shape[1:]
     amounts = [sign * FINE * place for place in range(COARSE)]
+    steps = list(range(FINE + 1) if sign > 0 else range(-FINE, 0))
+    result = jnp.dot(
+        left_ref[: len(steps) * half_rows, :], coarse_columns(tall_ref, partner, amounts),
+        preferred_element_type=jnp.float32,
+    )
     lags = []
-
-    def keep(result, base, steps, amounts):
-        for column, amount in enumerate(amounts):
-            for row, step in enumerate(steps):
-                stage_ref[base + amount + step] = factor * result[
-                    row * half_rows : (row + 1) * half_rows,
-                    column * channels : (column + 1) * channels,
-                ]
-                lags.append(base + amount + step)
-
-    result = jnp.dot(
-        left_ref[: FINE * half_rows, :], coarse_columns(tall_ref, partner, amounts),
-        preferred_element_type=jnp.float32,
-    )
-    keep(result, LAG, range(FINE) if sign > 0 else range(-FINE, 0), amounts)
-    if sign > 0:
-        result = jnp.dot(
-            left_ref[FINE * half_rows :, :], coarse_columns(tall_ref, partner, amounts[-1:]),
-            preferred_element_type=jnp.float32,
-        )
-        keep(result, LAG, [FINE], amounts[-1:])
+    for column, amount in enumerate(amounts):
+        for row, step in enumerate(steps):
+            if step == FINE and column < COARSE - 1:
+                continue
+            lags.append(LAG + amount + step)
+            stage_ref[lags[-1]] = factor * result[
+                row * half_rows : (row + 1) * half_rows,
+                column * channels : (column + 1) * channels,
+            ]
     span = pl.ds(min(lags), len(lags))
     copy = pltpu.make_async_copy(stage_ref.at[span], out_ref.at[slot, span], sem)
     copy.start()
@@ -155,10 +147,10 @@
 
 
 def early_kernel(pairs_ref, count_ref, taps_ref, *refs):
-    blocks, (band_ref, unit_ref, tall_ref) = refs[:2], refs[2:]
+    blocks, (band_ref, unit_ref, tall_ref) = refs[:3], refs[3:]
     make_band(taps_ref, band_ref)
-    for window in range(2):
-        normalise(blocks[window], band_ref, unit_ref, tall_ref, OWN, window)
+    for block, (place, window) in zip(blocks, ((OWN, 0), (OWN, 1), (DIAGONAL, 0))):
+        normalise(block, band_ref, unit_ref, tall_ref, place, window)
 
 
 def filter_kernel(units, band_ref, *refs):
@@ -235,11 +227,11 @@
     band, unit, tall = pl.pallas_call(
         early_kernel,
         out_shape=(band_shape, unit_shape, tall_shape),
-        in_specs=[smem, smem] + [vmem] * 3,
+        in_specs=[smem, smem] + [vmem] * 4,
         out_specs=(vmem, vmem, vmem),
         compiler_params=params,
         cost_estimate=light,
-    )(pairs, count, taps, own, swap(own))
+    )(pairs, count, taps, own, swap(own), diagonal)
 
     def more(units, blocks, unit, tall):
         return pl.pallas_call(
@@ -253,12 +245,10 @@
         )(band, *blocks, unit, tall)
 
     mine, other = 0, 1
-    diagonal, band = lax.optimization_barrier((diagonal, band))
+    sent, band = lax.optimization_barrier((diagonal, band))
     unit, tall = more(
-        ((DIAGONAL, mine), (DIAGONAL, other)), (diagonal, swap(diagonal)), unit, tall
-    )
-    unit, tall = more(
-        ((ABOVE, mine), (BELOW, mine), (PARTNER, mine)), (above, below, partner), unit, tall
+        ((ABOVE, mine), (BELOW, mine), (PARTNER, mine), (DIAGONAL, other)),
+        (above, below, partner, swap(sent)), unit, tall,
     )
     units = ((ABOVE, other), (BELOW, other), (PARTNER, other))
     _, _, out = pl.pallas_call(

time: 33.7 us -> 33.8 us (level)
    pallas_call x2 -> x1, Pallas kernels: 1.59 us -> 1 us  [more(): pl.pallas_call(functools.partial(filter_kernel, units), out_shape=(unit_s...]
  transfers between devices with their start and end apart: 9 -> 9, of which waited for: 2 -> 3; matrix products, arithmetic and copies ran while one was open for 2% -> 2% of each run, Pallas kernels for 9% -> 7%
where the time goes in v7:
time: 33.8 us; the launch traced here: 33.6 us
  Pallas kernels  14.5 us (43%)
  starting transfers between devices  12 us (36%)
  waiting for transfers between devices  4.05 us (12%)
  local copies, waits for them, and re-layouts  1.63 us (5%)
  between operations  0.72 us (2%)
  other arithmetic  0.66 us (2%)
    pallas_call x1, Pallas kernels, body(): pl.pallas_call(functools.partial(stack_kernel, scale, units), out_shape=(...  12.1 us
    ppermute x9, starting transfers between devices, passed(): return lax.ppermute(block, axis, route)  12 us
    ppermute x9, waiting for transfers between devices, passed(): return lax.ppermute(block, axis, route)  4.05 us
    unnamed x6, local copies, waits for them, and re-layouts  1.63 us
    pallas_call x1, Pallas kernels, body(): pl.pallas_call(early_kernel, out_shape=(band_shape, unit_shape, tall_shap...  1.46 us
    pallas_call x1, Pallas kernels, more(): pl.pallas_call(functools.partial(filter_kernel, units), out_shape=(unit_s...  1 us
  transfers between devices with their start and end apart: 9, of which 3 were waited for; matrix products, arithmetic and copies ran while one was open for 2% of the time, Pallas kernels for 7%

profile of v7, /device:TPU:0, one launch (start us, length us, event | category | flops | bytes accessed | tf_op | source)
XLA Modules:
  0.0 33.6 jit_solution(8137639915012543354)
XLA Ops:
  0.0 0.0 copy-start.2
  0.0 0.5 %collective-permute-start.1 = (bf16[128,1024]{1,0:T(8,128)(2,1)}, bf16[128,1024]{1,0:T(8,128)(2,1)S(1)}, u32[]{:S(2)}, u32[]{:S(2)}) collective-permute-start(bf16[128,1024]{1,0:T(8,128)(2,1)} %bitcast.6), channel_id=1, source_target_pairs={{0,1},{1,0},{2,3},{3,2},{4,5},{5,4},{6,7},{7,6},{8,9},{9,8},{10,11... | collective-permute-start | bytes 786440 | tf_op jit(solution)/shard_map/ppermute | solution.py:24
  0.5 0.7 %collective-permute-start = (bf16[128,1024]{1,0:T(8,128)(2,1)}, bf16[128,1024]{1,0:T(8,128)(2,1)S(1)}, u32[]{:S(2)}, u32[]{:S(2)}) collective-permute-start(bf16[128,1024]{1,0:T(8,128)(2,1)} %bitcast.7), channel_id=1, source_target_pairs={{2,4},{4,2},{6,8},{8,6},{10,12},{12,10},{3,5},{5,3},{7,9},{9,7},{1... | collective-permute-start | bytes 786440 | tf_op jit(solution)/shard_map/ppermute | solution.py:24
  1.1 5.5 %collective-permute-start.6 = (bf16[128,1024]{1,0:T(8,128)(2,1)}, bf16[128,1024]{1,0:T(8,128)(2,1)S(1)}, u32[]{:S(2)}, u32[]{:S(2)}) collective-permute-start(bf16[128,1024]{1,0:T(8,128)(2,1)} %bitcast.8), channel_id=1, source_target_pairs={{0,2},{2,0},{4,6},{6,4},{8,10},{10,8},{12,14},{14,12},{1,3},{3,1},... | collective-permute-start | bytes 786440 | tf_op jit(solution)/shard_map/ppermute | solution.py:24
  6.6 3.5 %collective-permute-start.4 = (bf16[128,1024]{1,0:T(8,128)(2,1)}, bf16[128,1024]{1,0:T(8,128)(2,1)S(1)}, u32[]{:S(2)}, u32[]{:S(2)}) collective-permute-start(bf16[128,1024]{1,0:T(8,128)(2,1)} %bitcast.9), channel_id=1, source_target_pairs={{0,4},{2,6},{4,8},{6,10},{8,12},{10,14},{1,5},{3,7},{5,9},{7,11},{... | collective-permute-start | bytes 786440 | tf_op jit(solution)/shard_map/ppermute | solution.py:24
  10.1 1.3 %collective-permute-start.2 = (bf16[128,1024]{1,0:T(8,128)(2,1)}, bf16[128,1024]{1,0:T(8,128)(2,1)S(1)}, u32[]{:S(2)}, u32[]{:S(2)}) collective-permute-start(bf16[128,1024]{1,0:T(8,128)(2,1)} %bitcast.10), channel_id=1, source_target_pairs={{4,0},{6,2},{8,4},{10,6},{12,8},{14,10},{5,1},{7,3},{9,5},{11,7},{... | collective-permute-start | bytes 786440 | tf_op jit(solution)/shard_map/ppermute | solution.py:24
  12.1 0.7 %bitcast_convert_fusion.taps_ref = f32[1,64]{1,0:T(1,128)S(1)} fusion(bf16[64]{0:T(256)(128)(2,1)} %param.5), kind=kLoop, calls=%fused_computation | loop fusion | flops 64 | bytes 384 | tf_op jit(solution)/shard_map/broadcast_in_dim | solution.py:208
  12.7 0.0 collective-permute-done.1.refs_1_
  12.7 0.0 collective-permute-done.refs_2_
  12.7 0.0 copy-start
  12.7 0.9 %copy-done = bf16[128,1,1024]{2,0,1:T(8,128)(2,1)S(1)} copy-done((bf16[128,1,1024]{2,0,1:T(8,128)(2,1)S(1)}, bf16[128,1,1024]{2,0,1:T(8,128)(2,1)}, u32[]{:S(2)}) %copy-start) | copy-done | bytes 262168
  13.7 0.0 copy-start.1
  13.7 0.7 %copy-done.1 = s32[4,2]{0,1:T(2,128)S(1)} copy-done((s32[4,2]{0,1:T(2,128)S(1)}, s32[4,2]{0,1:T(2,128)}, u32[]{:S(2)}) %copy-start.1) | copy-done | bytes 56
  14.4 1.5 %shard_map.46 = (bf16[2,256,256]{2,1,0:T(8,128)(2,1)S(1)}, bf16[5,128,2048]{2,1,0:T(8,128)(2,1)S(1)}, bf16[5,2,2,1088,128]{4,3,2,1,0:T(8,128)(2,1)S(1)}) custom-call(s32[2,4]{1,0:T(2,128)S(1)} %bitcast.12, s32[1]{0:T(128)S(6)} %copy.13.count_ref, f32[1,64]{1,0:T(1,128)S(1)} %bitcast_convert_fusion.taps_ref, bf16[128,1024]{1,0:T(8,128)(2,1)S(1)} %bitcast.11, ...), custom_call_target="tpu_custom_call" | custom-call | flops 1 | bytes 1 | tf_op jit(solution)/shard_map/pallas_call | solution.py:227
  15.8 0.1 collective-permute-start.8
  15.9 2.0 %collective-permute-done.6.refs_2_ = bf16[128,1024]{1,0:T(8,128)(2,1)S(1)} collective-permute-done((bf16[128,1024]{1,0:T(8,128)(2,1)}, bf16[128,1024]{1,0:T(8,128)(2,1)S(1)}, u32[]{:S(2)}, u32[]{:S(2)}) %collective-permute-start.6) | collective-permute-done | bytes 262176 | tf_op jit(solution)/shard_map/ppermute | solution.py:24
  17.9 0.0 collective-permute-start.7
  18.0 0.0 collective-permute-done.4.refs_1_
  18.0 0.5 %collective-permute-start.5 = (bf16[128,1024]{1,0:T(8,128)(2,1)S(1)}, bf16[128,1024]{1,0:T(8,128)(2,1)S(1)}, u32[]{:S(2)}, u32[]{:S(2)}) collective-permute-start(bf16[128,1024]{1,0:T(8,128)(2,1)S(1)} %collective-permute-done.4.refs_1_), channel_id=1, source_target_pairs={{0,1},{1,0},{2,3},{3,2},{4,5},{5,4},{6,7},{7,6},{8,9},{9,8},{10,11... | collective-permute-start | bytes 786440 | tf_op jit(solution)/shard_map/ppermute | solution.py:24
  18.4 1.5 %collective-permute-done.2.refs_0_ = bf16[128,1024]{1,0:T(8,128)(2,1)S(1)} collective-permute-done((bf16[128,1024]{1,0:T(8,128)(2,1)}, bf16[128,1024]{1,0:T(8,128)(2,1)S(1)}, u32[]{:S(2)}, u32[]{:S(2)}) %collective-permute-start.2) | collective-permute-done | bytes 262176 | tf_op jit(solution)/shard_map/ppermute | solution.py:24
  19.9 0.0 collective-permute-start.3
  19.9 0.0 collective-permute-done.8.refs_3_
  19.9 1.0 %shard_map.47 = (bf16[5,128,2048]{2,1,0:T(8,128)(2,1)S(1)}, bf16[5,2,2,1088,128]{4,3,2,1,0:T(8,128)(2,1)S(1)}) custom-call(bf16[2,256,256]{2,1,0:T(8,128)(2,1)S(1)} %get-tuple-element.14.band_ref, bf16[128,1024]{1,0:T(8,128)(2,1)S(1)} %collective-permute-done.2.refs_0_, ...), custom_call_target="tpu_custom_call", output_to_operand_aliasing={{0}: (5, {}), {1}: (6, {})} | custom-call | flops 1 | bytes 1 | tf_op jit(solution)/shard_map/pallas_call | solution.py:237
  21.0 0.0 collective-permute-done.7.refs_2_
  21.0 0.0 collective-permute-done.5.refs_1_
  21.0 0.5 %collective-permute-done.3.refs_0_ = bf16[128,1024]{1,0:T(8,128)(2,1)S(1)} collective-permute-done((bf16[128,1024]{1,0:T(8,128)(2,1)S(1)}, bf16[128,1024]{1,0:T(8,128)(2,1)S(1)}, u32[]{:S(2)}, u32[]{:S(2)}) %collective-permute-start.3) | collective-permute-done | bytes 262176 | tf_op jit(solution)/shard_map/ppermute | solution.py:24
  21.5 0.0 copy-done.2
  21.5 12.1 %shard_map.48 = (bf16[5,128,2048]{2,1,0:T(8,128)(2,1)S(1)}, bf16[5,2,2,1088,128]{4,3,2,1,0:T(8,128)(2,1)S(1)}, f32[4,65,64,128]{3,2,1,0:T(8,128)}) custom-call(s32[2,4]{1,0:T(2,128)S(1)} %bitcast.13, s32[1]{0:T(128)S(6)} %copy.13.count_ref, bf16[2,256,256]{2,1,0:T(8,128)(2,1)S(1)} %get-tuple-element.14.band_ref, ...), custom_call_target="tpu_custom_call", output_to_operand_aliasing={{0}: (6, {}), {1}: (7, {})} | custom-call | flops 8724152320 | bytes 8519680 | tf_op jit(solution)/shard_map/pallas_call | solution.py:254
Async XLA Ops:
  0.0 21.5 %copy-start.2 = (s32[4,2]{0,1:T(2,128)S(1)}, s32[4,2]{0,1:T(2,128)}, u32[]{:S(2)}) copy-start(s32[4,2]{0,1:T(2,128)} %param.6) | copy-start | bytes 100
  0.0 12.7 %collective-permute-start.1 = (bf16[128,1024]{1,0:T(8,128)(2,1)}, bf16[128,1024]{1,0:T(8,128)(2,1)S(1)}, u32[]{:S(2)}, u32[]{:S(2)}) collective-permute-start(bf16[128,1024]{1,0:T(8,128)(2,1)} %bitcast.6), channel_id=1, source_target_pairs={{0,1},{1,0},{2,3},{3,2},{4,5},{5,4},{6,7},{7,6},{8,9},{9,8},{10,11... | collective-permute-start | bytes 786440 | tf_op jit(solution)/shard_map/ppermute | solution.py:24
  0.5 12.3 %collective-permute-start = (bf16[128,1024]{1,0:T(8,128)(2,1)}, bf16[128,1024]{1,0:T(8,128)(2,1)S(1)}, u32[]{:S(2)}, u32[]{:S(2)}) collective-permute-start(bf16[128,1024]{1,0:T(8,128)(2,1)} %bitcast.7), channel_id=1, source_target_pairs={{2,4},{4,2},{6,8},{8,6},{10,12},{12,10},{3,5},{5,3},{7,9},{9,7},{1... | collective-permute-start | bytes 786440 | tf_op jit(solution)/shard_map/ppermute | solution.py:24
  1.1 16.8 %collective-permute-start.6 = (bf16[128,1024]{1,0:T(8,128)(2,1)}, bf16[128,1024]{1,0:T(8,128)(2,1)S(1)}, u32[]{:S(2)}, u32[]{:S(2)}) collective-permute-start(bf16[128,1024]{1,0:T(8,128)(2,1)} %bitcast.8), channel_id=1, source_target_pairs={{0,2},{2,0},{4,6},{6,4},{8,10},{10,8},{12,14},{14,12},{1,3},{3,1},... | collective-permute-start | bytes 786440 | tf_op jit(solution)/shard_map/ppermute | solution.py:24
  6.6 11.3 %collective-permute-start.4 = (bf16[128,1024]{1,0:T(8,128)(2,1)}, bf16[128,1024]{1,0:T(8,128)(2,1)S(1)}, u32[]{:S(2)}, u32[]{:S(2)}) collective-permute-start(bf16[128,1024]{1,0:T(8,128)(2,1)} %bitcast.9), channel_id=1, source_target_pairs={{0,4},{2,6},{4,8},{6,10},{8,12},{10,14},{1,5},{3,7},{5,9},{7,11},{... | collective-permute-start | bytes 786440 | tf_op jit(solution)/shard_map/ppermute | solution.py:24
  10.1 9.8 %collective-permute-start.2 = (bf16[128,1024]{1,0:T(8,128)(2,1)}, bf16[128,1024]{1,0:T(8,128)(2,1)S(1)}, u32[]{:S(2)}, u32[]{:S(2)}) collective-permute-start(bf16[128,1024]{1,0:T(8,128)(2,1)} %bitcast.10), channel_id=1, source_target_pairs={{4,0},{6,2},{8,4},{10,6},{12,8},{14,10},{5,1},{7,3},{9,5},{11,7},{... | collective-permute-start | bytes 786440 | tf_op jit(solution)/shard_map/ppermute | solution.py:24
  12.7 1.0 %copy-start = (bf16[128,1,1024]{2,0,1:T(8,128)(2,1)S(1)}, bf16[128,1,1024]{2,0,1:T(8,128)(2,1)}, u32[]{:S(2)}) copy-start(bf16[128,1,1024]{2,0,1:T(8,128)(2,1)} %param.4) | copy-start | bytes 786436
  13.7 0.7 %copy-start.1 = (s32[4,2]{0,1:T(2,128)S(1)}, s32[4,2]{0,1:T(2,128)}, u32[]{:S(2)}) copy-start(s32[4,2]{0,1:T(2,128)} %param.6) | copy-start | bytes 100
  15.8 4.1 %collective-permute-start.8 = (bf16[128,1024]{1,0:T(8,128)(2,1)S(1)}, bf16[128,1024]{1,0:T(8,128)(2,1)S(1)}, u32[]{:S(2)}, u32[]{:S(2)}) collective-permute-start(bf16[128,1024]{1,0:T(8,128)(2,1)S(1)} %collective-permute-done.refs_2_), channel_id=1, source_target_pairs={{0,1},{1,0},{2,3},{3,2},{4,5},{5,4},{6,7},{7,6},{8,9},{9,8},{10,11... | collective-permute-start | bytes 786440 | tf_op jit(solution)/shard_map/ppermute | solution.py:24
  17.9 3.0 %collective-permute-start.7 = (bf16[128,1024]{1,0:T(8,128)(2,1)S(1)}, bf16[128,1024]{1,0:T(8,128)(2,1)S(1)}, u32[]{:S(2)}, u32[]{:S(2)}) collective-permute-start(bf16[128,1024]{1,0:T(8,128)(2,1)S(1)} %collective-permute-done.6.refs_2_), channel_id=1, source_target_pairs={{0,1},{1,0},{2,3},{3,2},{4,5},{5,4},{6,7},{7,6},{8,9},{9,8},{10,11... | collective-permute-start | bytes 786440 | tf_op jit(solution)/shard_map/ppermute | solution.py:24
  18.0 3.0 %collective-permute-start.5 = (bf16[128,1024]{1,0:T(8,128)(2,1)S(1)}, bf16[128,1024]{1,0:T(8,128)(2,1)S(1)}, u32[]{:S(2)}, u32[]{:S(2)}) collective-permute-start(bf16[128,1024]{1,0:T(8,128)(2,1)S(1)} %collective-permute-done.4.refs_1_), channel_id=1, source_target_pairs={{0,1},{1,0},{2,3},{3,2},{4,5},{5,4},{6,7},{7,6},{8,9},{9,8},{10,11... | collective-permute-start | bytes 786440 | tf_op jit(solution)/shard_map/ppermute | solution.py:24
  19.9 1.5 %collective-permute-start.3 = (bf16[128,1024]{1,0:T(8,128)(2,1)S(1)}, bf16[128,1024]{1,0:T(8,128)(2,1)S(1)}, u32[]{:S(2)}, u32[]{:S(2)}) collective-permute-start(bf16[128,1024]{1,0:T(8,128)(2,1)S(1)} %collective-permute-done.2.refs_0_), channel_id=1, source_target_pairs={{0,1},{1,0},{2,3},{3,2},{4,5},{5,4},{6,7},{7,6},{8,9},{9,8},{10,11... | collective-permute-start | bytes 786440 | tf_op jit(solution)/shard_map/ppermute | solution.py:24

commit v8 on v7

--- a/solution.py
+++ b/solution.py
@@ -12,6 +12,8 @@
 NEAR = 2 * REACH + 1
 FINE = 8
 COARSE = LAG // FINE
+CHUNK = 4
+COPIES = COARSE * (FINE // CHUNK) + 1
 LANES = 128
 TILE = 256
 MARGIN = 32
@@ -122,28 +124,36 @@
     )
 
 
-def correlate(slot, sign, factor, partner, left_ref, tall_ref, stage_ref, out_ref, sem):
+def correlate(slot, sign, factor, partner, left_ref, tall_ref, stage_ref, out_ref, sems):
     half_rows, channels = stage_ref.shape[1:]
     amounts = [sign * FINE * place for place in range(COARSE)]
-    steps = list(range(FINE + 1) if sign > 0 else range(-FINE, 0))
-    result = jnp.dot(
-        left_ref[: len(steps) * half_rows, :], coarse_columns(tall_ref, partner, amounts),
-        preferred_element_type=jnp.float32,
-    )
-    lags = []
-    for column, amount in enumerate(amounts):
-        for row, step in enumerate(steps):
-            if step == FINE and column < COARSE - 1:
-                continue
-            lags.append(LAG + amount + step)
-            stage_ref[lags[-1]] = factor * result[
-                row * half_rows : (row + 1) * half_rows,
-                column * channels : (column + 1) * channels,
-            ]
-    span = pl.ds(min(lags), len(lags))
-    copy = pltpu.make_async_copy(stage_ref.at[span], out_ref.at[slot, span], sem)
-    copy.start()
-    return copy
+    first = 0 if sign > 0 else -FINE
+    copies = []
+
+    def product(steps, amounts):
+        low = steps[0] - first
+        result = jnp.dot(
+            left_ref[low * half_rows : (low + len(steps)) * half_rows, :],
+            coarse_columns(tall_ref, partner, amounts), preferred_element_type=jnp.float32,
+        )
+        for column, amount in enumerate(amounts):
+            for row, step in enumerate(steps):
+                stage_ref[LAG + amount + step] = factor * result[
+                    row * half_rows : (row + 1) * half_rows,
+                    column * channels : (column + 1) * channels,
+                ]
+            span = pl.ds(LAG + amount + steps[0], len(steps))
+            copy = pltpu.make_async_copy(
+                stage_ref.at[span], out_ref.at[slot, span], sems.at[len(copies)]
+            )
+            copy.start()
+            copies.append(copy)
+
+    if sign > 0:
+        product([FINE], amounts[-1:])
+    for part in range(0, FINE, CHUNK):
+        product(range(first + part, first + part + CHUNK), amounts)
+    return copies
 
 
 def early_kernel(pairs_ref, count_ref, taps_ref, *refs):
@@ -180,7 +190,7 @@
         ready(number + 1)
         factor = jnp.where(slot < count_ref[0], scale, 0.0)
         partner = place_of(pairs_ref[1, slot], owner)
-        copies.append(
+        copies += (
             correlate(
                 slot, sign, factor, partner, left_ref.at[number % 2], tall_ref,
                 stage_ref.at[slot], out_ref, sems.at[number],
@@ -247,10 +257,10 @@
     mine, other = 0, 1
     sent, band = lax.optimization_barrier((diagonal, band))
     unit, tall = more(
-        ((ABOVE, mine), (BELOW, mine), (PARTNER, mine), (DIAGONAL, other)),
-        (above, below, partner, swap(sent)), unit, tall,
-    )
-    units = ((ABOVE, other), (BELOW, other), (PARTNER, other))
+        ((BELOW, mine), (ABOVE, mine), (PARTNER, mine), (DIAGONAL, other)),
+        (below, above, partner, swap(sent)), unit, tall,
+    )
+    units = ((BELOW, other), (ABOVE, other), (PARTNER, other))
     _, _, out = pl.pallas_call(
         functools.partial(stack_kernel, scale, units),
         out_shape=(unit_shape, tall_shape, out_shape),
@@ -260,11 +270,11 @@
         scratch_shapes=[
             pltpu.VMEM((2, (FINE + 1) * half_rows, halves * length), jnp.bfloat16),
             pltpu.VMEM((cap, lags, half_rows, rows), jnp.float32),
-            pltpu.SemaphoreType.DMA((2 * cap,)),
+            pltpu.SemaphoreType.DMA((2 * cap, COPIES)),
         ],
         compiler_params=params,
         cost_estimate=heavy,
-    )(pairs, count, band, swap(above), swap(below), swap(partner), unit, tall)
+    )(pairs, count, band, swap(below), swap(above), swap(partner), unit, tall)
     return jnp.transpose(out, (0, 2, 1, 3))
 
 

time: 33.8 us -> 33.8 us (level)
  waiting for transfers between devices: 4.05 us -> 2.27 us
  starting transfers between devices: 12 us -> 13.1 us
  Pallas kernels: 14.5 us -> 15.2 us
    ppermute x9, waiting for transfers between devices: 4.05 us -> 2.27 us  [passed(): return lax.ppermute(block, axis, route)]
    ppermute x9, starting transfers between devices: 12 us -> 13.1 us  [passed(): return lax.ppermute(block, axis, route)]
    pallas_call x1, Pallas kernels: 12.1 us -> 12.8 us  [body(): pl.pallas_call(functools.partial(stack_kernel, scale, units), out_shape=(...]
where the time goes in v8:
time: 33.8 us; the launch traced here: 33.6 us
  Pallas kernels  15.2 us (45%)
  starting transfers between devices  13.1 us (39%)
  waiting for transfers between devices  2.27 us (7%)
  local copies, waits for them, and re-layouts  1.63 us (5%)
  between operations  0.72 us (2%)
  other arithmetic  0.66 us (2%)
    ppermute x9, starting transfers between devices, passed(): return lax.ppermute(block, axis, route)  13.1 us
    pallas_call x1, Pallas kernels, body(): pl.pallas_call(functools.partial(stack_kernel, scale, units), out_shape=(...  12.8 us
    ppermute x9, waiting for transfers between devices, passed(): return lax.ppermute(block, axis, route)  2.27 us
    unnamed x6, local copies, waits for them, and re-layouts  1.63 us
    pallas_call x1, Pallas kernels, body(): pl.pallas_call(early_kernel, out_shape=(band_shape, unit_shape, tall_shap...  1.46 us
    pallas_call x1, Pallas kernels, more(): pl.pallas_call(functools.partial(filter_kernel, units), out_shape=(unit_s...  1 us
  transfers between devices with their start and end apart: 9, of which 3 were waited for; matrix products, arithmetic and copies ran while one was open for 2% of the time, Pallas kernels for 7%

profile of v8, /device:TPU:0, one launch (start us, length us, event | category | flops | bytes accessed | tf_op | source)
XLA Modules:
  0.0 33.6 jit_solution(17339160309965078369)
XLA Ops:
  0.0 0.0 copy-start.2
  0.0 0.5 %collective-permute-start.1 = (bf16[128,1024]{1,0:T(8,128)(2,1)}, bf16[128,1024]{1,0:T(8,128)(2,1)S(1)}, u32[]{:S(2)}, u32[]{:S(2)}) collective-permute-start(bf16[128,1024]{1,0:T(8,128)(2,1)} %bitcast.6), channel_id=1, source_target_pairs={{0,1},{1,0},{2,3},{3,2},{4,5},{5,4},{6,7},{7,6},{8,9},{9,8},{10,11... | collective-permute-start | bytes 786440 | tf_op jit(solution)/shard_map/ppermute | solution.py:26
  0.5 0.7 %collective-permute-start = (bf16[128,1024]{1,0:T(8,128)(2,1)}, bf16[128,1024]{1,0:T(8,128)(2,1)S(1)}, u32[]{:S(2)}, u32[]{:S(2)}) collective-permute-start(bf16[128,1024]{1,0:T(8,128)(2,1)} %bitcast.7), channel_id=1, source_target_pairs={{2,4},{4,2},{6,8},{8,6},{10,12},{12,10},{3,5},{5,3},{7,9},{9,7},{1... | collective-permute-start | bytes 786440 | tf_op jit(solution)/shard_map/ppermute | solution.py:26
  1.1 5.5 %collective-permute-start.6 = (bf16[128,1024]{1,0:T(8,128)(2,1)}, bf16[128,1024]{1,0:T(8,128)(2,1)S(1)}, u32[]{:S(2)}, u32[]{:S(2)}) collective-permute-start(bf16[128,1024]{1,0:T(8,128)(2,1)} %bitcast.8), channel_id=1, source_target_pairs={{0,2},{2,0},{4,6},{6,4},{8,10},{10,8},{12,14},{14,12},{1,3},{3,1},... | collective-permute-start | bytes 786440 | tf_op jit(solution)/shard_map/ppermute | solution.py:26
  6.6 1.3 %collective-permute-start.4 = (bf16[128,1024]{1,0:T(8,128)(2,1)}, bf16[128,1024]{1,0:T(8,128)(2,1)S(1)}, u32[]{:S(2)}, u32[]{:S(2)}) collective-permute-start(bf16[128,1024]{1,0:T(8,128)(2,1)} %bitcast.9), channel_id=1, source_target_pairs={{4,0},{6,2},{8,4},{10,6},{12,8},{14,10},{5,1},{7,3},{9,5},{11,7},{... | collective-permute-start | bytes 786440 | tf_op jit(solution)/shard_map/ppermute | solution.py:26
  7.9 4.6 %collective-permute-start.2 = (bf16[128,1024]{1,0:T(8,128)(2,1)}, bf16[128,1024]{1,0:T(8,128)(2,1)S(1)}, u32[]{:S(2)}, u32[]{:S(2)}) collective-permute-start(bf16[128,1024]{1,0:T(8,128)(2,1)} %bitcast.10), channel_id=1, source_target_pairs={{0,4},{2,6},{4,8},{6,10},{8,12},{10,14},{1,5},{3,7},{5,9},{7,11},{... | collective-permute-start | bytes 786440 | tf_op jit(solution)/shard_map/ppermute | solution.py:26
  13.1 0.7 %bitcast_convert_fusion.taps_ref = f32[1,64]{1,0:T(1,128)S(1)} fusion(bf16[64]{0:T(256)(128)(2,1)} %param.5), kind=kLoop, calls=%fused_computation | loop fusion | flops 64 | bytes 384 | tf_op jit(solution)/shard_map/broadcast_in_dim | solution.py:218
  13.8 0.0 collective-permute-done.1.refs_1_
  13.8 0.0 collective-permute-done.refs_2_
  13.8 0.0 copy-start
  13.8 0.9 %copy-done = bf16[128,1,1024]{2,0,1:T(8,128)(2,1)S(1)} copy-done((bf16[128,1,1024]{2,0,1:T(8,128)(2,1)S(1)}, bf16[128,1,1024]{2,0,1:T(8,128)(2,1)}, u32[]{:S(2)}) %copy-start) | copy-done | bytes 262168
  14.7 0.0 copy-start.1
  14.7 0.7 %copy-done.1 = s32[4,2]{0,1:T(2,128)S(1)} copy-done((s32[4,2]{0,1:T(2,128)S(1)}, s32[4,2]{0,1:T(2,128)}, u32[]{:S(2)}) %copy-start.1) | copy-done | bytes 56
  15.4 1.5 %shard_map.46 = (bf16[2,256,256]{2,1,0:T(8,128)(2,1)S(1)}, bf16[5,128,2048]{2,1,0:T(8,128)(2,1)S(1)}, bf16[5,2,2,1088,128]{4,3,2,1,0:T(8,128)(2,1)S(1)}) custom-call(s32[2,4]{1,0:T(2,128)S(1)} %bitcast.12, s32[1]{0:T(128)S(6)} %copy.13.count_ref, f32[1,64]{1,0:T(1,128)S(1)} %bitcast_convert_fusion.taps_ref, bf16[128,1024]{1,0:T(8,128)(2,1)S(1)} %bitcast.11, ...), custom_call_target="tpu_custom_call" | custom-call | flops 1 | bytes 1 | tf_op jit(solution)/shard_map/pallas_call | solution.py:237
  16.9 0.1 collective-permute-start.8
  17.0 1.0 %collective-permute-done.6.refs_2_ = bf16[128,1024]{1,0:T(8,128)(2,1)S(1)} collective-permute-done((bf16[128,1024]{1,0:T(8,128)(2,1)}, bf16[128,1024]{1,0:T(8,128)(2,1)S(1)}, u32[]{:S(2)}, u32[]{:S(2)}) %collective-permute-start.6) | collective-permute-done | bytes 262176 | tf_op jit(solution)/shard_map/ppermute | solution.py:26
  17.9 0.0 collective-permute-start.7
  18.0 0.9 %collective-permute-done.4.refs_1_ = bf16[128,1024]{1,0:T(8,128)(2,1)S(1)} collective-permute-done((bf16[128,1024]{1,0:T(8,128)(2,1)}, bf16[128,1024]{1,0:T(8,128)(2,1)S(1)}, u32[]{:S(2)}, u32[]{:S(2)}) %collective-permute-start.4) | collective-permute-done | bytes 262176 | tf_op jit(solution)/shard_map/ppermute | solution.py:26
  18.9 0.0 collective-permute-start.5
  18.9 0.0 collective-permute-done.2.refs_0_
  18.9 0.5 %collective-permute-start.3 = (bf16[128,1024]{1,0:T(8,128)(2,1)S(1)}, bf16[128,1024]{1,0:T(8,128)(2,1)S(1)}, u32[]{:S(2)}, u32[]{:S(2)}) collective-permute-start(bf16[128,1024]{1,0:T(8,128)(2,1)S(1)} %collective-permute-done.2.refs_0_), channel_id=1, source_target_pairs={{0,1},{1,0},{2,3},{3,2},{4,5},{5,4},{6,7},{7,6},{8,9},{9,8},{10,11... | collective-permute-start | bytes 786440 | tf_op jit(solution)/shard_map/ppermute | solution.py:26
  19.4 0.0 collective-permute-done.8.refs_3_
  19.4 1.0 %shard_map.47 = (bf16[5,128,2048]{2,1,0:T(8,128)(2,1)S(1)}, bf16[5,2,2,1088,128]{4,3,2,1,0:T(8,128)(2,1)S(1)}) custom-call(bf16[2,256,256]{2,1,0:T(8,128)(2,1)S(1)} %get-tuple-element.14.band_ref, bf16[128,1024]{1,0:T(8,128)(2,1)S(1)} %collective-permute-done.2.refs_0_, ...), custom_call_target="tpu_custom_call", output_to_operand_aliasing={{0}: (5, {}), {1}: (6, {})} | custom-call | flops 1 | bytes 1 | tf_op jit(solution)/shard_map/pallas_call | solution.py:247
  20.4 0.0 collective-permute-done.7.refs_2_
  20.4 0.0 collective-permute-done.5.refs_1_
  20.4 0.4 %collective-permute-done.3.refs_0_ = bf16[128,1024]{1,0:T(8,128)(2,1)S(1)} collective-permute-done((bf16[128,1024]{1,0:T(8,128)(2,1)S(1)}, bf16[128,1024]{1,0:T(8,128)(2,1)S(1)}, u32[]{:S(2)}, u32[]{:S(2)}) %collective-permute-start.3) | collective-permute-done | bytes 262176 | tf_op jit(solution)/shard_map/ppermute | solution.py:26
  20.8 0.0 copy-done.2
  20.8 12.8 %shard_map.48 = (bf16[5,128,2048]{2,1,0:T(8,128)(2,1)S(1)}, bf16[5,2,2,1088,128]{4,3,2,1,0:T(8,128)(2,1)S(1)}, f32[4,65,64,128]{3,2,1,0:T(8,128)}) custom-call(s32[2,4]{1,0:T(2,128)S(1)} %bitcast.13, s32[1]{0:T(128)S(6)} %copy.13.count_ref, bf16[2,256,256]{2,1,0:T(8,128)(2,1)S(1)} %get-tuple-element.14.band_ref, ...), custom_call_target="tpu_custom_call", output_to_operand_aliasing={{0}: (6, {}), {1}: (7, {})} | custom-call | flops 8724152320 | bytes 8519680 | tf_op jit(solution)/shard_map/pallas_call | solution.py:264
Async XLA Ops:
  0.0 20.8 %copy-start.2 = (s32[4,2]{0,1:T(2,128)S(1)}, s32[4,2]{0,1:T(2,128)}, u32[]{:S(2)}) copy-start(s32[4,2]{0,1:T(2,128)} %param.6) | copy-start | bytes 100
  0.0 13.8 %collective-permute-start.1 = (bf16[128,1024]{1,0:T(8,128)(2,1)}, bf16[128,1024]{1,0:T(8,128)(2,1)S(1)}, u32[]{:S(2)}, u32[]{:S(2)}) collective-permute-start(bf16[128,1024]{1,0:T(8,128)(2,1)} %bitcast.6), channel_id=1, source_target_pairs={{0,1},{1,0},{2,3},{3,2},{4,5},{5,4},{6,7},{7,6},{8,9},{9,8},{10,11... | collective-permute-start | bytes 786440 | tf_op jit(solution)/shard_map/ppermute | solution.py:26
  0.5 13.3 %collective-permute-start = (bf16[128,1024]{1,0:T(8,128)(2,1)}, bf16[128,1024]{1,0:T(8,128)(2,1)S(1)}, u32[]{:S(2)}, u32[]{:S(2)}) collective-permute-start(bf16[128,1024]{1,0:T(8,128)(2,1)} %bitcast.7), channel_id=1, source_target_pairs={{2,4},{4,2},{6,8},{8,6},{10,12},{12,10},{3,5},{5,3},{7,9},{9,7},{1... | collective-permute-start | bytes 786440 | tf_op jit(solution)/shard_map/ppermute | solution.py:26
  1.1 16.8 %collective-permute-start.6 = (bf16[128,1024]{1,0:T(8,128)(2,1)}, bf16[128,1024]{1,0:T(8,128)(2,1)S(1)}, u32[]{:S(2)}, u32[]{:S(2)}) collective-permute-start(bf16[128,1024]{1,0:T(8,128)(2,1)} %bitcast.8), channel_id=1, source_target_pairs={{0,2},{2,0},{4,6},{6,4},{8,10},{10,8},{12,14},{14,12},{1,3},{3,1},... | collective-permute-start | bytes 786440 | tf_op jit(solution)/shard_map/ppermute | solution.py:26
  6.6 12.3 %collective-permute-start.4 = (bf16[128,1024]{1,0:T(8,128)(2,1)}, bf16[128,1024]{1,0:T(8,128)(2,1)S(1)}, u32[]{:S(2)}, u32[]{:S(2)}) collective-permute-start(bf16[128,1024]{1,0:T(8,128)(2,1)} %bitcast.9), channel_id=1, source_target_pairs={{4,0},{6,2},{8,4},{10,6},{12,8},{14,10},{5,1},{7,3},{9,5},{11,7},{... | collective-permute-start | bytes 786440 | tf_op jit(solution)/shard_map/ppermute | solution.py:26
  7.9 11.0 %collective-permute-start.2 = (bf16[128,1024]{1,0:T(8,128)(2,1)}, bf16[128,1024]{1,0:T(8,128)(2,1)S(1)}, u32[]{:S(2)}, u32[]{:S(2)}) collective-permute-start(bf16[128,1024]{1,0:T(8,128)(2,1)} %bitcast.10), channel_id=1, source_target_pairs={{0,4},{2,6},{4,8},{6,10},{8,12},{10,14},{1,5},{3,7},{5,9},{7,11},{... | collective-permute-start | bytes 786440 | tf_op jit(solution)/shard_map/ppermute | solution.py:26
  13.8 1.0 %copy-start = (bf16[128,1,1024]{2,0,1:T(8,128)(2,1)S(1)}, bf16[128,1,1024]{2,0,1:T(8,128)(2,1)}, u32[]{:S(2)}) copy-start(bf16[128,1,1024]{2,0,1:T(8,128)(2,1)} %param.4) | copy-start | bytes 786436
  14.7 0.7 %copy-start.1 = (s32[4,2]{0,1:T(2,128)S(1)}, s32[4,2]{0,1:T(2,128)}, u32[]{:S(2)}) copy-start(s32[4,2]{0,1:T(2,128)} %param.6) | copy-start | bytes 100
  16.9 2.5 %collective-permute-start.8 = (bf16[128,1024]{1,0:T(8,128)(2,1)S(1)}, bf16[128,1024]{1,0:T(8,128)(2,1)S(1)}, u32[]{:S(2)}, u32[]{:S(2)}) collective-permute-start(bf16[128,1024]{1,0:T(8,128)(2,1)S(1)} %collective-permute-done.refs_2_), channel_id=1, source_target_pairs={{0,1},{1,0},{2,3},{3,2},{4,5},{5,4},{6,7},{7,6},{8,9},{9,8},{10,11... | collective-permute-start | bytes 786440 | tf_op jit(solution)/shard_map/ppermute | solution.py:26
  17.9 2.5 %collective-permute-start.7 = (bf16[128,1024]{1,0:T(8,128)(2,1)S(1)}, bf16[128,1024]{1,0:T(8,128)(2,1)S(1)}, u32[]{:S(2)}, u32[]{:S(2)}) collective-permute-start(bf16[128,1024]{1,0:T(8,128)(2,1)S(1)} %collective-permute-done.6.refs_2_), channel_id=1, source_target_pairs={{0,1},{1,0},{2,3},{3,2},{4,5},{5,4},{6,7},{7,6},{8,9},{9,8},{10,11... | collective-permute-start | bytes 786440 | tf_op jit(solution)/shard_map/ppermute | solution.py:26
  18.9 1.5 %collective-permute-start.5 = (bf16[128,1024]{1,0:T(8,128)(2,1)S(1)}, bf16[128,1024]{1,0:T(8,128)(2,1)S(1)}, u32[]{:S(2)}, u32[]{:S(2)}) collective-permute-start(bf16[128,1024]{1,0:T(8,128)(2,1)S(1)} %collective-permute-done.4.refs_1_), channel_id=1, source_target_pairs={{0,1},{1,0},{2,3},{3,2},{4,5},{5,4},{6,7},{7,6},{8,9},{9,8},{10,11... | collective-permute-start | bytes 786440 | tf_op jit(solution)/shard_map/ppermute | solution.py:26
  18.9 1.9 %collective-permute-start.3 = (bf16[128,1024]{1,0:T(8,128)(2,1)S(1)}, bf16[128,1024]{1,0:T(8,128)(2,1)S(1)}, u32[]{:S(2)}, u32[]{:S(2)}) collective-permute-start(bf16[128,1024]{1,0:T(8,128)(2,1)S(1)} %collective-permute-done.2.refs_0_), channel_id=1, source_target_pairs={{0,1},{1,0},{2,3},{3,2},{4,5},{5,4},{6,7},{7,6},{8,9},{9,8},{10,11... | collective-permute-start | bytes 786440 | tf_op jit(solution)/shard_map/ppermute | solution.py:26

commit v9 on v8

--- a/solution.py
+++ b/solution.py
@@ -12,7 +12,7 @@
 NEAR = 2 * REACH + 1
 FINE = 8
 COARSE = LAG // FINE
-CHUNK = 4
+CHUNK = 8
 COPIES = COARSE * (FINE // CHUNK) + 1
 LANES = 128
 TILE = 256
@@ -257,10 +257,10 @@
     mine, other = 0, 1
     sent, band = lax.optimization_barrier((diagonal, band))
     unit, tall = more(
-        ((BELOW, mine), (ABOVE, mine), (PARTNER, mine), (DIAGONAL, other)),
-        (below, above, partner, swap(sent)), unit, tall,
-    )
-    units = ((BELOW, other), (ABOVE, other), (PARTNER, other))
+        ((BELOW, mine), (PARTNER, mine), (ABOVE, mine), (DIAGONAL, other)),
+        (below, partner, above, swap(sent)), unit, tall,
+    )
+    units = ((BELOW, other), (PARTNER, other), (ABOVE, other))
     _, _, out = pl.pallas_call(
         functools.partial(stack_kernel, scale, units),
         out_shape=(unit_shape, tall_shape, out_shape),
@@ -274,7 +274,7 @@
         ],
         compiler_params=params,
         cost_estimate=heavy,
-    )(pairs, count, band, swap(below), swap(above), swap(partner), unit, tall)
+    )(pairs, count, band, swap(below), swap(partner), swap(above), unit, tall)
     return jnp.transpose(out, (0, 2, 1, 3))
 
 

time: 33.8 us -> 34.2 us (1.012)
  no operation moved by 1% of the time
where the time goes in v9:
time: 34.2 us; the launch traced here: 34 us
  Pallas kernels  15.3 us (45%)
  starting transfers between devices  13.1 us (38%)
  waiting for transfers between devices  2.61 us (8%)
  local copies, waits for them, and re-layouts  1.63 us (5%)
  between operations  0.72 us (2%)
  other arithmetic  0.66 us (2%)
    ppermute x9, starting transfers between devices, passed(): return lax.ppermute(block, axis, route)  13.1 us
    pallas_call x1, Pallas kernels, body(): pl.pallas_call(functools.partial(stack_kernel, scale, units), out_shape=(...  12.8 us
    ppermute x9, waiting for transfers between devices, passed(): return lax.ppermute(block, axis, route)  2.61 us
    unnamed x6, local copies, waits for them, and re-layouts  1.63 us
    pallas_call x1, Pallas kernels, body(): pl.pallas_call(early_kernel, out_shape=(band_shape, unit_shape, tall_shap...  1.46 us
    pallas_call x1, Pallas kernels, more(): pl.pallas_call(functools.partial(filter_kernel, units), out_shape=(unit_s...  1 us
  transfers between devices with their start and end apart: 9, of which 3 were waited for; matrix products, arithmetic and copies ran while one was open for 2% of the time, Pallas kernels for 7%

profile of v9, /device:TPU:0, one launch (start us, length us, event | category | flops | bytes accessed | tf_op | source)
XLA Modules:
  0.0 34.0 jit_solution(16675189939521081693)
XLA Ops:
  0.0 0.0 copy-start.2
  0.0 0.5 %collective-permute-start.1 = (bf16[128,1024]{1,0:T(8,128)(2,1)}, bf16[128,1024]{1,0:T(8,128)(2,1)S(1)}, u32[]{:S(2)}, u32[]{:S(2)}) collective-permute-start(bf16[128,1024]{1,0:T(8,128)(2,1)} %bitcast.6), channel_id=1, source_target_pairs={{0,1},{1,0},{2,3},{3,2},{4,5},{5,4},{6,7},{7,6},{8,9},{9,8},{10,11... | collective-permute-start | bytes 786440 | tf_op jit(solution)/shard_map/ppermute | solution.py:26
  0.5 0.7 %collective-permute-start = (bf16[128,1024]{1,0:T(8,128)(2,1)}, bf16[128,1024]{1,0:T(8,128)(2,1)S(1)}, u32[]{:S(2)}, u32[]{:S(2)}) collective-permute-start(bf16[128,1024]{1,0:T(8,128)(2,1)} %bitcast.7), channel_id=1, source_target_pairs={{2,4},{4,2},{6,8},{8,6},{10,12},{12,10},{3,5},{5,3},{7,9},{9,7},{1... | collective-permute-start | bytes 786440 | tf_op jit(solution)/shard_map/ppermute | solution.py:26
  1.1 1.3 %collective-permute-start.6 = (bf16[128,1024]{1,0:T(8,128)(2,1)}, bf16[128,1024]{1,0:T(8,128)(2,1)S(1)}, u32[]{:S(2)}, u32[]{:S(2)}) collective-permute-start(bf16[128,1024]{1,0:T(8,128)(2,1)} %bitcast.8), channel_id=1, source_target_pairs={{4,0},{6,2},{8,4},{10,6},{12,8},{14,10},{5,1},{7,3},{9,5},{11,7},{... | collective-permute-start | bytes 786440 | tf_op jit(solution)/shard_map/ppermute | solution.py:26
  2.4 5.5 %collective-permute-start.4 = (bf16[128,1024]{1,0:T(8,128)(2,1)}, bf16[128,1024]{1,0:T(8,128)(2,1)S(1)}, u32[]{:S(2)}, u32[]{:S(2)}) collective-permute-start(bf16[128,1024]{1,0:T(8,128)(2,1)} %bitcast.9), channel_id=1, source_target_pairs={{0,2},{2,0},{4,6},{6,4},{8,10},{10,8},{12,14},{14,12},{1,3},{3,1},... | collective-permute-start | bytes 786440 | tf_op jit(solution)/shard_map/ppermute | solution.py:26
  7.9 4.6 %collective-permute-start.2 = (bf16[128,1024]{1,0:T(8,128)(2,1)}, bf16[128,1024]{1,0:T(8,128)(2,1)S(1)}, u32[]{:S(2)}, u32[]{:S(2)}) collective-permute-start(bf16[128,1024]{1,0:T(8,128)(2,1)} %bitcast.10), channel_id=1, source_target_pairs={{0,4},{2,6},{4,8},{6,10},{8,12},{10,14},{1,5},{3,7},{5,9},{7,11},{... | collective-permute-start | bytes 786440 | tf_op jit(solution)/shard_map/ppermute | solution.py:26
  13.1 0.7 %bitcast_convert_fusion.taps_ref = f32[1,64]{1,0:T(1,128)S(1)} fusion(bf16[64]{0:T(256)(128)(2,1)} %param.5), kind=kLoop, calls=%fused_computation | loop fusion | flops 64 | bytes 384 | tf_op jit(solution)/shard_map/broadcast_in_dim | solution.py:218
  13.8 0.0 collective-permute-done.1.refs_1_
  13.8 0.0 collective-permute-done.refs_2_
  13.8 0.0 copy-start
  13.8 0.9 %copy-done = bf16[128,1,1024]{2,0,1:T(8,128)(2,1)S(1)} copy-done((bf16[128,1,1024]{2,0,1:T(8,128)(2,1)S(1)}, bf16[128,1,1024]{2,0,1:T(8,128)(2,1)}, u32[]{:S(2)}) %copy-start) | copy-done | bytes 262168
  14.7 0.0 copy-start.1
  14.7 0.7 %copy-done.1 = s32[4,2]{0,1:T(2,128)S(1)} copy-done((s32[4,2]{0,1:T(2,128)S(1)}, s32[4,2]{0,1:T(2,128)}, u32[]{:S(2)}) %copy-start.1) | copy-done | bytes 56
  15.4 1.5 %shard_map.46 = (bf16[2,256,256]{2,1,0:T(8,128)(2,1)S(1)}, bf16[5,128,2048]{2,1,0:T(8,128)(2,1)S(1)}, bf16[5,2,2,1088,128]{4,3,2,1,0:T(8,128)(2,1)S(1)}) custom-call(s32[2,4]{1,0:T(2,128)S(1)} %bitcast.12, s32[1]{0:T(128)S(6)} %copy.13.count_ref, f32[1,64]{1,0:T(1,128)S(1)} %bitcast_convert_fusion.taps_ref, bf16[128,1024]{1,0:T(8,128)(2,1)S(1)} %bitcast.11, ...), custom_call_target="tpu_custom_call" | custom-call | flops 1 | bytes 1 | tf_op jit(solution)/shard_map/pallas_call | solution.py:237
  16.9 0.1 collective-permute-start.8
  17.0 1.9 %collective-permute-done.6.refs_2_ = bf16[128,1024]{1,0:T(8,128)(2,1)S(1)} collective-permute-done((bf16[128,1024]{1,0:T(8,128)(2,1)}, bf16[128,1024]{1,0:T(8,128)(2,1)S(1)}, u32[]{:S(2)}, u32[]{:S(2)}) %collective-permute-start.6) | collective-permute-done | bytes 262176 | tf_op jit(solution)/shard_map/ppermute | solution.py:26
  18.9 0.0 collective-permute-start.7
  18.9 0.0 collective-permute-done.4.refs_1_
  18.9 0.5 %collective-permute-start.5 = (bf16[128,1024]{1,0:T(8,128)(2,1)S(1)}, bf16[128,1024]{1,0:T(8,128)(2,1)S(1)}, u32[]{:S(2)}, u32[]{:S(2)}) collective-permute-start(bf16[128,1024]{1,0:T(8,128)(2,1)S(1)} %collective-permute-done.4.refs_1_), channel_id=1, source_target_pairs={{0,1},{1,0},{2,3},{3,2},{4,5},{5,4},{6,7},{7,6},{8,9},{9,8},{10,11... | collective-permute-start | bytes 786440 | tf_op jit(solution)/shard_map/ppermute | solution.py:26
  19.4 0.0 collective-permute-done.2.refs_0_
  19.4 0.1 collective-permute-start.3
  19.5 0.0 collective-permute-done.8.refs_3_
  19.5 1.0 %shard_map.47 = (bf16[5,128,2048]{2,1,0:T(8,128)(2,1)S(1)}, bf16[5,2,2,1088,128]{4,3,2,1,0:T(8,128)(2,1)S(1)}) custom-call(bf16[2,256,256]{2,1,0:T(8,128)(2,1)S(1)} %get-tuple-element.14.band_ref, bf16[128,1024]{1,0:T(8,128)(2,1)S(1)} %collective-permute-done.2.refs_0_, ...), custom_call_target="tpu_custom_call", output_to_operand_aliasing={{0}: (5, {}), {1}: (6, {})} | custom-call | flops 1 | bytes 1 | tf_op jit(solution)/shard_map/pallas_call | solution.py:247
  20.5 0.0 collective-permute-done.7.refs_2_
  20.5 0.3 collective-permute-done.5.refs_1_
  20.8 0.4 %collective-permute-done.3.refs_0_ = bf16[128,1024]{1,0:T(8,128)(2,1)S(1)} collective-permute-done((bf16[128,1024]{1,0:T(8,128)(2,1)S(1)}, bf16[128,1024]{1,0:T(8,128)(2,1)S(1)}, u32[]{:S(2)}, u32[]{:S(2)}) %collective-permute-start.3) | collective-permute-done | bytes 262176 | tf_op jit(solution)/shard_map/ppermute | solution.py:26
  21.2 0.0 copy-done.2
  21.2 12.8 %shard_map.48 = (bf16[5,128,2048]{2,1,0:T(8,128)(2,1)S(1)}, bf16[5,2,2,1088,128]{4,3,2,1,0:T(8,128)(2,1)S(1)}, f32[4,65,64,128]{3,2,1,0:T(8,128)}) custom-call(s32[2,4]{1,0:T(2,128)S(1)} %bitcast.13, s32[1]{0:T(128)S(6)} %copy.13.count_ref, bf16[2,256,256]{2,1,0:T(8,128)(2,1)S(1)} %get-tuple-element.14.band_ref, ...), custom_call_target="tpu_custom_call", output_to_operand_aliasing={{0}: (6, {}), {1}: (7, {})} | custom-call | flops 8724152320 | bytes 8519680 | tf_op jit(solution)/shard_map/pallas_call | solution.py:264
Async XLA Ops:
  0.0 21.2 %copy-start.2 = (s32[4,2]{0,1:T(2,128)S(1)}, s32[4,2]{0,1:T(2,128)}, u32[]{:S(2)}) copy-start(s32[4,2]{0,1:T(2,128)} %param.6) | copy-start | bytes 100
  0.0 13.8 %collective-permute-start.1 = (bf16[128,1024]{1,0:T(8,128)(2,1)}, bf16[128,1024]{1,0:T(8,128)(2,1)S(1)}, u32[]{:S(2)}, u32[]{:S(2)}) collective-permute-start(bf16[128,1024]{1,0:T(8,128)(2,1)} %bitcast.6), channel_id=1, source_target_pairs={{0,1},{1,0},{2,3},{3,2},{4,5},{5,4},{6,7},{7,6},{8,9},{9,8},{10,11... | collective-permute-start | bytes 786440 | tf_op jit(solution)/shard_map/ppermute | solution.py:26
  0.5 13.3 %collective-permute-start = (bf16[128,1024]{1,0:T(8,128)(2,1)}, bf16[128,1024]{1,0:T(8,128)(2,1)S(1)}, u32[]{:S(2)}, u32[]{:S(2)}) collective-permute-start(bf16[128,1024]{1,0:T(8,128)(2,1)} %bitcast.7), channel_id=1, source_target_pairs={{2,4},{4,2},{6,8},{8,6},{10,12},{12,10},{3,5},{5,3},{7,9},{9,7},{1... | collective-permute-start | bytes 786440 | tf_op jit(solution)/shard_map/ppermute | solution.py:26
  1.1 17.8 %collective-permute-start.6 = (bf16[128,1024]{1,0:T(8,128)(2,1)}, bf16[128,1024]{1,0:T(8,128)(2,1)S(1)}, u32[]{:S(2)}, u32[]{:S(2)}) collective-permute-start(bf16[128,1024]{1,0:T(8,128)(2,1)} %bitcast.8), channel_id=1, source_target_pairs={{4,0},{6,2},{8,4},{10,6},{12,8},{14,10},{5,1},{7,3},{9,5},{11,7},{... | collective-permute-start | bytes 786440 | tf_op jit(solution)/shard_map/ppermute | solution.py:26
  2.4 16.5 %collective-permute-start.4 = (bf16[128,1024]{1,0:T(8,128)(2,1)}, bf16[128,1024]{1,0:T(8,128)(2,1)S(1)}, u32[]{:S(2)}, u32[]{:S(2)}) collective-permute-start(bf16[128,1024]{1,0:T(8,128)(2,1)} %bitcast.9), channel_id=1, source_target_pairs={{0,2},{2,0},{4,6},{6,4},{8,10},{10,8},{12,14},{14,12},{1,3},{3,1},... | collective-permute-start | bytes 786440 | tf_op jit(solution)/shard_map/ppermute | solution.py:26
  7.9 11.5 %collective-permute-start.2 = (bf16[128,1024]{1,0:T(8,128)(2,1)}, bf16[128,1024]{1,0:T(8,128)(2,1)S(1)}, u32[]{:S(2)}, u32[]{:S(2)}) collective-permute-start(bf16[128,1024]{1,0:T(8,128)(2,1)} %bitcast.10), channel_id=1, source_target_pairs={{0,4},{2,6},{4,8},{6,10},{8,12},{10,14},{1,5},{3,7},{5,9},{7,11},{... | collective-permute-start | bytes 786440 | tf_op jit(solution)/shard_map/ppermute | solution.py:26
  13.8 1.0 %copy-start = (bf16[128,1,1024]{2,0,1:T(8,128)(2,1)S(1)}, bf16[128,1,1024]{2,0,1:T(8,128)(2,1)}, u32[]{:S(2)}) copy-start(bf16[128,1,1024]{2,0,1:T(8,128)(2,1)} %param.4) | copy-start | bytes 786436
  14.7 0.7 %copy-start.1 = (s32[4,2]{0,1:T(2,128)S(1)}, s32[4,2]{0,1:T(2,128)}, u32[]{:S(2)}) copy-start(s32[4,2]{0,1:T(2,128)} %param.6) | copy-start | bytes 100
  16.9 2.6 %collective-permute-start.8 = (bf16[128,1024]{1,0:T(8,128)(2,1)S(1)}, bf16[128,1024]{1,0:T(8,128)(2,1)S(1)}, u32[]{:S(2)}, u32[]{:S(2)}) collective-permute-start(bf16[128,1024]{1,0:T(8,128)(2,1)S(1)} %collective-permute-done.refs_2_), channel_id=1, source_target_pairs={{0,1},{1,0},{2,3},{3,2},{4,5},{5,4},{6,7},{7,6},{8,9},{9,8},{10,11... | collective-permute-start | bytes 786440 | tf_op jit(solution)/shard_map/ppermute | solution.py:26
  18.9 1.6 %collective-permute-start.7 = (bf16[128,1024]{1,0:T(8,128)(2,1)S(1)}, bf16[128,1024]{1,0:T(8,128)(2,1)S(1)}, u32[]{:S(2)}, u32[]{:S(2)}) collective-permute-start(bf16[128,1024]{1,0:T(8,128)(2,1)S(1)} %collective-permute-done.6.refs_2_), channel_id=1, source_target_pairs={{0,1},{1,0},{2,3},{3,2},{4,5},{5,4},{6,7},{7,6},{8,9},{9,8},{10,11... | collective-permute-start | bytes 786440 | tf_op jit(solution)/shard_map/ppermute | solution.py:26
  18.9 1.9 %collective-permute-start.5 = (bf16[128,1024]{1,0:T(8,128)(2,1)S(1)}, bf16[128,1024]{1,0:T(8,128)(2,1)S(1)}, u32[]{:S(2)}, u32[]{:S(2)}) collective-permute-start(bf16[128,1024]{1,0:T(8,128)(2,1)S(1)} %collective-permute-done.4.refs_1_), channel_id=1, source_target_pairs={{0,1},{1,0},{2,3},{3,2},{4,5},{5,4},{6,7},{7,6},{8,9},{9,8},{10,11... | collective-permute-start | bytes 786440 | tf_op jit(solution)/shard_map/ppermute | solution.py:26
  19.4 1.8 %collective-permute-start.3 = (bf16[128,1024]{1,0:T(8,128)(2,1)S(1)}, bf16[128,1024]{1,0:T(8,128)(2,1)S(1)}, u32[]{:S(2)}, u32[]{:S(2)}) collective-permute-start(bf16[128,1024]{1,0:T(8,128)(2,1)S(1)} %collective-permute-done.2.refs_0_), channel_id=1, source_target_pairs={{0,1},{1,0},{2,3},{3,2},{4,5},{5,4},{6,7},{7,6},{8,9},{9,8},{10,11... | collective-permute-start | bytes 786440 | tf_op jit(solution)/shard_map/ppermute | solution.py:26

commit v10 on v7

--- a/solution.py
+++ b/solution.py
@@ -92,15 +92,22 @@
     ).astype(jnp.bfloat16)
 
 
+def own_rows(source, unit_ref, half_rows, span):
+    first = pl.multiple_of(lax.axis_index("tm") * half_rows, half_rows)
+    return unit_ref[source, pl.ds(first, half_rows), span]
+
+
+def fine_steps(sign):
+    return range(1, FINE + 1) if sign > 0 else range(-FINE, 0)
+
+
 def prepare(source, sign, unit_ref, left_ref, half_rows):
     length = unit_ref.shape[2] // 2
-    first_row = pl.multiple_of(lax.axis_index("tm") * half_rows, half_rows)
     for window in range(2):
         span = slice(window * length, (window + 1) * length)
-        rows = unit_ref[source, pl.ds(first_row, half_rows), span]
-        for place in range(FINE + 1 if sign > 0 else FINE):
-            step = place if sign > 0 else place - FINE
-            left_ref[place * half_rows : (place + 1) * half_rows, span] = shifted(rows, step)
+        rows = own_rows(source, unit_ref, half_rows, span)
+        for row, step in enumerate(fine_steps(sign)):
+            left_ref[row * half_rows : (row + 1) * half_rows, span] = shifted(rows, step)
 
 
 def coarse_rows(tall_ref, partner, window, amount):
@@ -122,28 +129,19 @@
     )
 
 
-def correlate(slot, sign, factor, partner, left_ref, tall_ref, stage_ref, out_ref, sem):
+def correlate(sign, factor, partner, left_ref, tall_ref, stage_ref):
     half_rows, channels = stage_ref.shape[1:]
     amounts = [sign * FINE * place for place in range(COARSE)]
-    steps = list(range(FINE + 1) if sign > 0 else range(-FINE, 0))
     result = jnp.dot(
-        left_ref[: len(steps) * half_rows, :], coarse_columns(tall_ref, partner, amounts),
+        left_ref[...], coarse_columns(tall_ref, partner, amounts),
         preferred_element_type=jnp.float32,
     )
-    lags = []
     for column, amount in enumerate(amounts):
-        for row, step in enumerate(steps):
-            if step == FINE and column < COARSE - 1:
-                continue
-            lags.append(LAG + amount + step)
-            stage_ref[lags[-1]] = factor * result[
+        for row, step in enumerate(fine_steps(sign)):
+            stage_ref[LAG + amount + step] = factor * result[
                 row * half_rows : (row + 1) * half_rows,
                 column * channels : (column + 1) * channels,
             ]
-    span = pl.ds(min(lags), len(lags))
-    copy = pltpu.make_async_copy(stage_ref.at[span], out_ref.at[slot, span], sem)
-    copy.start()
-    return copy
 
 
 def early_kernel(pairs_ref, count_ref, taps_ref, *refs):
@@ -164,28 +162,46 @@
     unit_ref, tall_ref, out_ref, left_ref, stage_ref, sems = refs
     for block, (place, window) in zip(blocks, units):
         normalise(block, band_ref, unit_ref, tall_ref, place, window)
-    slots = out_ref.shape[0]
-    steps = [(slot, sign) for slot in range(slots) for sign in (1, -1)]
+    slots, lags, half_rows, _ = out_ref.shape
     owner = lax.axis_index("chan")
 
-    def ready(number):
-        if number < len(steps):
-            slot, sign = steps[number]
+    def ready(slot):
+        if slot < slots:
             source = place_of(pairs_ref[0, slot], owner)
-            prepare(source, sign, unit_ref, left_ref.at[number % 2], stage_ref.shape[2])
+            for side, sign in enumerate((1, -1)):
+                prepare(source, sign, unit_ref, left_ref.at[slot % 2, side], half_rows)
 
     copies = []
+
+    def send(slot, first, count):
+        span = pl.ds(first, count)
+        copy = pltpu.make_async_copy(
+            stage_ref.at[slot, span], out_ref.at[slot, span], sems.at[len(copies)]
+        )
+        copy.start()
+        copies.append(copy)
+
     ready(0)
-    for number, (slot, sign) in enumerate(steps):
-        ready(number + 1)
+    for slot in range(slots):
+        ready(slot + 1)
         factor = jnp.where(slot < count_ref[0], scale, 0.0)
+        source = place_of(pairs_ref[0, slot], owner)
         partner = place_of(pairs_ref[1, slot], owner)
-        copies.append(
+        for side, sign in enumerate((1, -1)):
             correlate(
-                slot, sign, factor, partner, left_ref.at[number % 2], tall_ref,
-                stage_ref.at[slot], out_ref, sems.at[number],
+                sign, factor, partner, left_ref.at[slot % 2, side], tall_ref, stage_ref.at[slot]
             )
-        )
+            if sign > 0:
+                stage_ref[slot, LAG] = factor * jnp.dot(
+                    own_rows(source, unit_ref, half_rows, slice(None)),
+                    coarse_columns(tall_ref, partner, [0]), preferred_element_type=jnp.float32,
+                )
+                if slot == slots - 1:
+                    send(slot, LAG, lags - LAG)
+        if slot == slots - 1:
+            send(slot, 0, LAG)
+        else:
+            send(slot, 0, lags)
     for copy in copies:
         copy.wait()
 
@@ -247,10 +263,10 @@
     mine, other = 0, 1
     sent, band = lax.optimization_barrier((diagonal, band))
     unit, tall = more(
-        ((ABOVE, mine), (BELOW, mine), (PARTNER, mine), (DIAGONAL, other)),
-        (above, below, partner, swap(sent)), unit, tall,
-    )
-    units = ((ABOVE, other), (BELOW, other), (PARTNER, other))
+        ((BELOW, mine), (ABOVE, mine), (PARTNER, mine), (DIAGONAL, other)),
+        (below, above, partner, swap(sent)), unit, tall,
+    )
+    units = ((BELOW, other), (ABOVE, other), (PARTNER, other))
     _, _, out = pl.pallas_call(
         functools.partial(stack_kernel, scale, units),
         out_shape=(unit_shape, tall_shape, out_shape),
@@ -258,13 +274,13 @@
         out_specs=(vmem, vmem, hbm),
         input_output_aliases={len(units) + 3: 0, len(units) + 4: 1},
         scratch_shapes=[
-            pltpu.VMEM((2, (FINE + 1) * half_rows, halves * length), jnp.bfloat16),
+            pltpu.VMEM((2, 2, FINE * half_rows, halves * length), jnp.bfloat16),
             pltpu.VMEM((cap, lags, half_rows, rows), jnp.float32),
-            pltpu.SemaphoreType.DMA((2 * cap,)),
+            pltpu.SemaphoreType.DMA((cap + 1,)),
         ],
         compiler_params=params,
         cost_estimate=heavy,
-    )(pairs, count, band, swap(above), swap(below), swap(partner), unit, tall)
+    )(pairs, count, band, swap(below), swap(above), swap(partner), unit, tall)
     return jnp.transpose(out, (0, 2, 1, 3))
 
 

time: 33.8 us -> 33 us (0.976)
  waiting for transfers between devices: 4.05 us -> 2.27 us
  starting transfers between devices: 12 us -> 13.1 us
    ppermute x9, waiting for transfers between devices: 4.05 us -> 2.27 us  [passed(): return lax.ppermute(block, axis, route)]
    ppermute x9, starting transfers between devices: 12 us -> 13.1 us  [passed(): return lax.ppermute(block, axis, route)]
where the time goes in v10:
time: 33 us; the launch traced here: 32.8 us
  Pallas kernels  14.4 us (44%)
  starting transfers between devices  13.1 us (40%)
  waiting for transfers between devices  2.27 us (7%)
  local copies, waits for them, and re-layouts  1.63 us (5%)
  between operations  0.72 us (2%)
  other arithmetic  0.66 us (2%)
    ppermute x9, starting transfers between devices, passed(): return lax.ppermute(block, axis, route)  13.1 us
    pallas_call x1, Pallas kernels, body(): pl.pallas_call(functools.partial(stack_kernel, scale, units), out_shape=(...  12 us
    ppermute x9, waiting for transfers between devices, passed(): return lax.ppermute(block, axis, route)  2.27 us
    unnamed x6, local copies, waits for them, and re-layouts  1.63 us
    pallas_call x1, Pallas kernels, body(): pl.pallas_call(early_kernel, out_shape=(band_shape, unit_shape, tall_shap...  1.46 us
    pallas_call x1, Pallas kernels, more(): pl.pallas_call(functools.partial(filter_kernel, units), out_shape=(unit_s...  1 us
  transfers between devices with their start and end apart: 9, of which 3 were waited for; matrix products, arithmetic and copies ran while one was open for 2% of the time, Pallas kernels for 7%

profile of v10, /device:TPU:0, one launch (start us, length us, event | category | flops | bytes accessed | tf_op | source)
XLA Modules:
  0.0 32.8 jit_solution(9206772426242672138)
XLA Ops:
  0.0 0.0 copy-start.2
  0.0 0.5 %collective-permute-start.1 = (bf16[128,1024]{1,0:T(8,128)(2,1)}, bf16[128,1024]{1,0:T(8,128)(2,1)S(1)}, u32[]{:S(2)}, u32[]{:S(2)}) collective-permute-start(bf16[128,1024]{1,0:T(8,128)(2,1)} %bitcast.6), channel_id=1, source_target_pairs={{0,1},{1,0},{2,3},{3,2},{4,5},{5,4},{6,7},{7,6},{8,9},{9,8},{10,11... | collective-permute-start | bytes 786440 | tf_op jit(solution)/shard_map/ppermute | solution.py:24
  0.5 0.7 %collective-permute-start = (bf16[128,1024]{1,0:T(8,128)(2,1)}, bf16[128,1024]{1,0:T(8,128)(2,1)S(1)}, u32[]{:S(2)}, u32[]{:S(2)}) collective-permute-start(bf16[128,1024]{1,0:T(8,128)(2,1)} %bitcast.7), channel_id=1, source_target_pairs={{2,4},{4,2},{6,8},{8,6},{10,12},{12,10},{3,5},{5,3},{7,9},{9,7},{1... | collective-permute-start | bytes 786440 | tf_op jit(solution)/shard_map/ppermute | solution.py:24
  1.1 5.5 %collective-permute-start.6 = (bf16[128,1024]{1,0:T(8,128)(2,1)}, bf16[128,1024]{1,0:T(8,128)(2,1)S(1)}, u32[]{:S(2)}, u32[]{:S(2)}) collective-permute-start(bf16[128,1024]{1,0:T(8,128)(2,1)} %bitcast.8), channel_id=1, source_target_pairs={{0,2},{2,0},{4,6},{6,4},{8,10},{10,8},{12,14},{14,12},{1,3},{3,1},... | collective-permute-start | bytes 786440 | tf_op jit(solution)/shard_map/ppermute | solution.py:24
  6.6 1.3 %collective-permute-start.4 = (bf16[128,1024]{1,0:T(8,128)(2,1)}, bf16[128,1024]{1,0:T(8,128)(2,1)S(1)}, u32[]{:S(2)}, u32[]{:S(2)}) collective-permute-start(bf16[128,1024]{1,0:T(8,128)(2,1)} %bitcast.9), channel_id=1, source_target_pairs={{4,0},{6,2},{8,4},{10,6},{12,8},{14,10},{5,1},{7,3},{9,5},{11,7},{... | collective-permute-start | bytes 786440 | tf_op jit(solution)/shard_map/ppermute | solution.py:24
  7.9 4.6 %collective-permute-start.2 = (bf16[128,1024]{1,0:T(8,128)(2,1)}, bf16[128,1024]{1,0:T(8,128)(2,1)S(1)}, u32[]{:S(2)}, u32[]{:S(2)}) collective-permute-start(bf16[128,1024]{1,0:T(8,128)(2,1)} %bitcast.10), channel_id=1, source_target_pairs={{0,4},{2,6},{4,8},{6,10},{8,12},{10,14},{1,5},{3,7},{5,9},{7,11},{... | collective-permute-start | bytes 786440 | tf_op jit(solution)/shard_map/ppermute | solution.py:24
  13.1 0.7 %bitcast_convert_fusion.taps_ref = f32[1,64]{1,0:T(1,128)S(1)} fusion(bf16[64]{0:T(256)(128)(2,1)} %param.5), kind=kLoop, calls=%fused_computation | loop fusion | flops 64 | bytes 384 | tf_op jit(solution)/shard_map/broadcast_in_dim | solution.py:224
  13.8 0.0 collective-permute-done.1.refs_1_
  13.8 0.0 collective-permute-done.refs_2_
  13.8 0.0 copy-start
  13.8 0.9 %copy-done = bf16[128,1,1024]{2,0,1:T(8,128)(2,1)S(1)} copy-done((bf16[128,1,1024]{2,0,1:T(8,128)(2,1)S(1)}, bf16[128,1,1024]{2,0,1:T(8,128)(2,1)}, u32[]{:S(2)}) %copy-start) | copy-done | bytes 262168
  14.7 0.0 copy-start.1
  14.7 0.7 %copy-done.1 = s32[4,2]{0,1:T(2,128)S(1)} copy-done((s32[4,2]{0,1:T(2,128)S(1)}, s32[4,2]{0,1:T(2,128)}, u32[]{:S(2)}) %copy-start.1) | copy-done | bytes 56
  15.4 1.5 %shard_map.46 = (bf16[2,256,256]{2,1,0:T(8,128)(2,1)S(1)}, bf16[5,128,2048]{2,1,0:T(8,128)(2,1)S(1)}, bf16[5,2,2,1088,128]{4,3,2,1,0:T(8,128)(2,1)S(1)}) custom-call(s32[2,4]{1,0:T(2,128)S(1)} %bitcast.12, s32[1]{0:T(128)S(6)} %copy.13.count_ref, f32[1,64]{1,0:T(1,128)S(1)} %bitcast_convert_fusion.taps_ref, bf16[128,1024]{1,0:T(8,128)(2,1)S(1)} %bitcast.11, ...), custom_call_target="tpu_custom_call" | custom-call | flops 1 | bytes 1 | tf_op jit(solution)/shard_map/pallas_call | solution.py:243
  16.9 0.1 collective-permute-start.8
  17.0 1.0 %collective-permute-done.6.refs_2_ = bf16[128,1024]{1,0:T(8,128)(2,1)S(1)} collective-permute-done((bf16[128,1024]{1,0:T(8,128)(2,1)}, bf16[128,1024]{1,0:T(8,128)(2,1)S(1)}, u32[]{:S(2)}, u32[]{:S(2)}) %collective-permute-start.6) | collective-permute-done | bytes 262176 | tf_op jit(solution)/shard_map/ppermute | solution.py:24
  17.9 0.0 collective-permute-start.7
  18.0 0.9 %collective-permute-done.4.refs_1_ = bf16[128,1024]{1,0:T(8,128)(2,1)S(1)} collective-permute-done((bf16[128,1024]{1,0:T(8,128)(2,1)}, bf16[128,1024]{1,0:T(8,128)(2,1)S(1)}, u32[]{:S(2)}, u32[]{:S(2)}) %collective-permute-start.4) | collective-permute-done | bytes 262176 | tf_op jit(solution)/shard_map/ppermute | solution.py:24
  18.9 0.0 collective-permute-start.5
  18.9 0.0 collective-permute-done.2.refs_0_
  18.9 0.5 %collective-permute-start.3 = (bf16[128,1024]{1,0:T(8,128)(2,1)S(1)}, bf16[128,1024]{1,0:T(8,128)(2,1)S(1)}, u32[]{:S(2)}, u32[]{:S(2)}) collective-permute-start(bf16[128,1024]{1,0:T(8,128)(2,1)S(1)} %collective-permute-done.2.refs_0_), channel_id=1, source_target_pairs={{0,1},{1,0},{2,3},{3,2},{4,5},{5,4},{6,7},{7,6},{8,9},{9,8},{10,11... | collective-permute-start | bytes 786440 | tf_op jit(solution)/shard_map/ppermute | solution.py:24
  19.4 0.0 collective-permute-done.8.refs_3_
  19.4 1.0 %shard_map.47 = (bf16[5,128,2048]{2,1,0:T(8,128)(2,1)S(1)}, bf16[5,2,2,1088,128]{4,3,2,1,0:T(8,128)(2,1)S(1)}) custom-call(bf16[2,256,256]{2,1,0:T(8,128)(2,1)S(1)} %get-tuple-element.14.band_ref, bf16[128,1024]{1,0:T(8,128)(2,1)S(1)} %collective-permute-done.2.refs_0_, ...), custom_call_target="tpu_custom_call", output_to_operand_aliasing={{0}: (5, {}), {1}: (6, {})} | custom-call | flops 1 | bytes 1 | tf_op jit(solution)/shard_map/pallas_call | solution.py:253
  20.4 0.0 collective-permute-done.7.refs_2_
  20.4 0.0 collective-permute-done.5.refs_1_
  20.4 0.4 %collective-permute-done.3.refs_0_ = bf16[128,1024]{1,0:T(8,128)(2,1)S(1)} collective-permute-done((bf16[128,1024]{1,0:T(8,128)(2,1)S(1)}, bf16[128,1024]{1,0:T(8,128)(2,1)S(1)}, u32[]{:S(2)}, u32[]{:S(2)}) %collective-permute-start.3) | collective-permute-done | bytes 262176 | tf_op jit(solution)/shard_map/ppermute | solution.py:24
  20.8 0.0 copy-done.2
  20.8 12.0 %shard_map.48 = (bf16[5,128,2048]{2,1,0:T(8,128)(2,1)S(1)}, bf16[5,2,2,1088,128]{4,3,2,1,0:T(8,128)(2,1)S(1)}, f32[4,65,64,128]{3,2,1,0:T(8,128)}) custom-call(s32[2,4]{1,0:T(2,128)S(1)} %bitcast.13, s32[1]{0:T(128)S(6)} %copy.13.count_ref, bf16[2,256,256]{2,1,0:T(8,128)(2,1)S(1)} %get-tuple-element.14.band_ref, ...), custom_call_target="tpu_custom_call", output_to_operand_aliasing={{0}: (6, {}), {1}: (7, {})} | custom-call | flops 8724152320 | bytes 8519680 | tf_op jit(solution)/shard_map/pallas_call | solution.py:270
Async XLA Ops:
  0.0 20.8 %copy-start.2 = (s32[4,2]{0,1:T(2,128)S(1)}, s32[4,2]{0,1:T(2,128)}, u32[]{:S(2)}) copy-start(s32[4,2]{0,1:T(2,128)} %param.6) | copy-start | bytes 100
  0.0 13.8 %collective-permute-start.1 = (bf16[128,1024]{1,0:T(8,128)(2,1)}, bf16[128,1024]{1,0:T(8,128)(2,1)S(1)}, u32[]{:S(2)}, u32[]{:S(2)}) collective-permute-start(bf16[128,1024]{1,0:T(8,128)(2,1)} %bitcast.6), channel_id=1, source_target_pairs={{0,1},{1,0},{2,3},{3,2},{4,5},{5,4},{6,7},{7,6},{8,9},{9,8},{10,11... | collective-permute-start | bytes 786440 | tf_op jit(solution)/shard_map/ppermute | solution.py:24
  0.5 13.3 %collective-permute-start = (bf16[128,1024]{1,0:T(8,128)(2,1)}, bf16[128,1024]{1,0:T(8,128)(2,1)S(1)}, u32[]{:S(2)}, u32[]{:S(2)}) collective-permute-start(bf16[128,1024]{1,0:T(8,128)(2,1)} %bitcast.7), channel_id=1, source_target_pairs={{2,4},{4,2},{6,8},{8,6},{10,12},{12,10},{3,5},{5,3},{7,9},{9,7},{1... | collective-permute-start | bytes 786440 | tf_op jit(solution)/shard_map/ppermute | solution.py:24
  1.1 16.8 %collective-permute-start.6 = (bf16[128,1024]{1,0:T(8,128)(2,1)}, bf16[128,1024]{1,0:T(8,128)(2,1)S(1)}, u32[]{:S(2)}, u32[]{:S(2)}) collective-permute-start(bf16[128,1024]{1,0:T(8,128)(2,1)} %bitcast.8), channel_id=1, source_target_pairs={{0,2},{2,0},{4,6},{6,4},{8,10},{10,8},{12,14},{14,12},{1,3},{3,1},... | collective-permute-start | bytes 786440 | tf_op jit(solution)/shard_map/ppermute | solution.py:24
  6.6 12.3 %collective-permute-start.4 = (bf16[128,1024]{1,0:T(8,128)(2,1)}, bf16[128,1024]{1,0:T(8,128)(2,1)S(1)}, u32[]{:S(2)}, u32[]{:S(2)}) collective-permute-start(bf16[128,1024]{1,0:T(8,128)(2,1)} %bitcast.9), channel_id=1, source_target_pairs={{4,0},{6,2},{8,4},{10,6},{12,8},{14,10},{5,1},{7,3},{9,5},{11,7},{... | collective-permute-start | bytes 786440 | tf_op jit(solution)/shard_map/ppermute | solution.py:24
  7.9 11.0 %collective-permute-start.2 = (bf16[128,1024]{1,0:T(8,128)(2,1)}, bf16[128,1024]{1,0:T(8,128)(2,1)S(1)}, u32[]{:S(2)}, u32[]{:S(2)}) collective-permute-start(bf16[128,1024]{1,0:T(8,128)(2,1)} %bitcast.10), channel_id=1, source_target_pairs={{0,4},{2,6},{4,8},{6,10},{8,12},{10,14},{1,5},{3,7},{5,9},{7,11},{... | collective-permute-start | bytes 786440 | tf_op jit(solution)/shard_map/ppermute | solution.py:24
  13.8 1.0 %copy-start = (bf16[128,1,1024]{2,0,1:T(8,128)(2,1)S(1)}, bf16[128,1,1024]{2,0,1:T(8,128)(2,1)}, u32[]{:S(2)}) copy-start(bf16[128,1,1024]{2,0,1:T(8,128)(2,1)} %param.4) | copy-start | bytes 786436
  14.7 0.7 %copy-start.1 = (s32[4,2]{0,1:T(2,128)S(1)}, s32[4,2]{0,1:T(2,128)}, u32[]{:S(2)}) copy-start(s32[4,2]{0,1:T(2,128)} %param.6) | copy-start | bytes 100
  16.9 2.5 %collective-permute-start.8 = (bf16[128,1024]{1,0:T(8,128)(2,1)S(1)}, bf16[128,1024]{1,0:T(8,128)(2,1)S(1)}, u32[]{:S(2)}, u32[]{:S(2)}) collective-permute-start(bf16[128,1024]{1,0:T(8,128)(2,1)S(1)} %collective-permute-done.refs_2_), channel_id=1, source_target_pairs={{0,1},{1,0},{2,3},{3,2},{4,5},{5,4},{6,7},{7,6},{8,9},{9,8},{10,11... | collective-permute-start | bytes 786440 | tf_op jit(solution)/shard_map/ppermute | solution.py:24
  17.9 2.5 %collective-permute-start.7 = (bf16[128,1024]{1,0:T(8,128)(2,1)S(1)}, bf16[128,1024]{1,0:T(8,128)(2,1)S(1)}, u32[]{:S(2)}, u32[]{:S(2)}) collective-permute-start(bf16[128,1024]{1,0:T(8,128)(2,1)S(1)} %collective-permute-done.6.refs_2_), channel_id=1, source_target_pairs={{0,1},{1,0},{2,3},{3,2},{4,5},{5,4},{6,7},{7,6},{8,9},{9,8},{10,11... | collective-permute-start | bytes 786440 | tf_op jit(solution)/shard_map/ppermute | solution.py:24
  18.9 1.5 %collective-permute-start.5 = (bf16[128,1024]{1,0:T(8,128)(2,1)S(1)}, bf16[128,1024]{1,0:T(8,128)(2,1)S(1)}, u32[]{:S(2)}, u32[]{:S(2)}) collective-permute-start(bf16[128,1024]{1,0:T(8,128)(2,1)S(1)} %collective-permute-done.4.refs_1_), channel_id=1, source_target_pairs={{0,1},{1,0},{2,3},{3,2},{4,5},{5,4},{6,7},{7,6},{8,9},{9,8},{10,11... | collective-permute-start | bytes 786440 | tf_op jit(solution)/shard_map/ppermute | solution.py:24
  18.9 1.9 %collective-permute-start.3 = (bf16[128,1024]{1,0:T(8,128)(2,1)S(1)}, bf16[128,1024]{1,0:T(8,128)(2,1)S(1)}, u32[]{:S(2)}, u32[]{:S(2)}) collective-permute-start(bf16[128,1024]{1,0:T(8,128)(2,1)S(1)} %collective-permute-done.2.refs_0_), channel_id=1, source_target_pairs={{0,1},{1,0},{2,3},{3,2},{4,5},{5,4},{6,7},{7,6},{8,9},{9,8},{10,11... | collective-permute-start | bytes 786440 | tf_op jit(solution)/shard_map/ppermute | solution.py:24

commit v11 on v10

--- a/solution.py
+++ b/solution.py
@@ -12,6 +12,8 @@
 NEAR = 2 * REACH + 1
 FINE = 8
 COARSE = LAG // FINE
+TALL = 2
+WIDE = 2
 LANES = 128
 TILE = 256
 MARGIN = 32
@@ -132,16 +134,19 @@
 def correlate(sign, factor, partner, left_ref, tall_ref, stage_ref):
     half_rows, channels = stage_ref.shape[1:]
     amounts = [sign * FINE * place for place in range(COARSE)]
-    result = jnp.dot(
-        left_ref[...], coarse_columns(tall_ref, partner, amounts),
-        preferred_element_type=jnp.float32,
-    )
-    for column, amount in enumerate(amounts):
-        for row, step in enumerate(fine_steps(sign)):
-            stage_ref[LAG + amount + step] = factor * result[
-                row * half_rows : (row + 1) * half_rows,
-                column * channels : (column + 1) * channels,
-            ]
+    steps = fine_steps(sign)
+    for column in range(0, COARSE, WIDE):
+        right = coarse_columns(tall_ref, partner, amounts[column : column + WIDE])
+        for row in range(0, FINE, TALL):
+            result = jnp.dot(
+                left_ref[row * half_rows : (row + TALL) * half_rows, :], right,
+                preferred_element_type=jnp.float32,
+            )
+            for i, amount in enumerate(amounts[column : column + WIDE]):
+                for j, step in enumerate(steps[row : row + TALL]):
+                    stage_ref[LAG + amount + step] = factor * result[
+                        j * half_rows : (j + 1) * half_rows, i * channels : (i + 1) * channels
+                    ]
 
 
 def early_kernel(pairs_ref, count_ref, taps_ref, *refs):

time: 33 us -> 33.3 us (level)
  no operation moved by 1% of the time
where the time goes in v11:
time: 33.3 us; the launch traced here: 33.1 us
  Pallas kernels  14.7 us (44%)
  starting transfers between devices  13.1 us (39%)
  waiting for transfers between devices  2.27 us (7%)
  local copies, waits for them, and re-layouts  1.63 us (5%)
  between operations  0.72 us (2%)
  other arithmetic  0.66 us (2%)
    ppermute x9, starting transfers between devices, passed(): return lax.ppermute(block, axis, route)  13.1 us
    pallas_call x1, Pallas kernels, body(): pl.pallas_call(functools.partial(stack_kernel, scale, units), out_shape=(...  12.3 us
    ppermute x9, waiting for transfers between devices, passed(): return lax.ppermute(block, axis, route)  2.27 us
    unnamed x6, local copies, waits for them, and re-layouts  1.63 us
    pallas_call x1, Pallas kernels, body(): pl.pallas_call(early_kernel, out_shape=(band_shape, unit_shape, tall_shap...  1.46 us
    pallas_call x1, Pallas kernels, more(): pl.pallas_call(functools.partial(filter_kernel, units), out_shape=(unit_s...  1 us
  transfers between devices with their start and end apart: 9, of which 3 were waited for; matrix products, arithmetic and copies ran while one was open for 2% of the time, Pallas kernels for 7%

profile of v11, /device:TPU:0, one launch (start us, length us, event | category | flops | bytes accessed | tf_op | source)
XLA Modules:
  0.0 33.1 jit_solution(38092255186429699)
XLA Ops:
  0.0 0.0 copy-start.2
  0.0 0.5 %collective-permute-start.1 = (bf16[128,1024]{1,0:T(8,128)(2,1)}, bf16[128,1024]{1,0:T(8,128)(2,1)S(1)}, u32[]{:S(2)}, u32[]{:S(2)}) collective-permute-start(bf16[128,1024]{1,0:T(8,128)(2,1)} %bitcast.6), channel_id=1, source_target_pairs={{0,1},{1,0},{2,3},{3,2},{4,5},{5,4},{6,7},{7,6},{8,9},{9,8},{10,11... | collective-permute-start | bytes 786440 | tf_op jit(solution)/shard_map/ppermute | solution.py:26
  0.5 0.7 %collective-permute-start = (bf16[128,1024]{1,0:T(8,128)(2,1)}, bf16[128,1024]{1,0:T(8,128)(2,1)S(1)}, u32[]{:S(2)}, u32[]{:S(2)}) collective-permute-start(bf16[128,1024]{1,0:T(8,128)(2,1)} %bitcast.7), channel_id=1, source_target_pairs={{2,4},{4,2},{6,8},{8,6},{10,12},{12,10},{3,5},{5,3},{7,9},{9,7},{1... | collective-permute-start | bytes 786440 | tf_op jit(solution)/shard_map/ppermute | solution.py:26
  1.1 5.5 %collective-permute-start.6 = (bf16[128,1024]{1,0:T(8,128)(2,1)}, bf16[128,1024]{1,0:T(8,128)(2,1)S(1)}, u32[]{:S(2)}, u32[]{:S(2)}) collective-permute-start(bf16[128,1024]{1,0:T(8,128)(2,1)} %bitcast.8), channel_id=1, source_target_pairs={{0,2},{2,0},{4,6},{6,4},{8,10},{10,8},{12,14},{14,12},{1,3},{3,1},... | collective-permute-start | bytes 786440 | tf_op jit(solution)/shard_map/ppermute | solution.py:26
  6.6 1.3 %collective-permute-start.4 = (bf16[128,1024]{1,0:T(8,128)(2,1)}, bf16[128,1024]{1,0:T(8,128)(2,1)S(1)}, u32[]{:S(2)}, u32[]{:S(2)}) collective-permute-start(bf16[128,1024]{1,0:T(8,128)(2,1)} %bitcast.9), channel_id=1, source_target_pairs={{4,0},{6,2},{8,4},{10,6},{12,8},{14,10},{5,1},{7,3},{9,5},{11,7},{... | collective-permute-start | bytes 786440 | tf_op jit(solution)/shard_map/ppermute | solution.py:26
  7.9 4.6 %collective-permute-start.2 = (bf16[128,1024]{1,0:T(8,128)(2,1)}, bf16[128,1024]{1,0:T(8,128)(2,1)S(1)}, u32[]{:S(2)}, u32[]{:S(2)}) collective-permute-start(bf16[128,1024]{1,0:T(8,128)(2,1)} %bitcast.10), channel_id=1, source_target_pairs={{0,4},{2,6},{4,8},{6,10},{8,12},{10,14},{1,5},{3,7},{5,9},{7,11},{... | collective-permute-start | bytes 786440 | tf_op jit(solution)/shard_map/ppermute | solution.py:26
  13.1 0.7 %bitcast_convert_fusion.taps_ref = f32[1,64]{1,0:T(1,128)S(1)} fusion(bf16[64]{0:T(256)(128)(2,1)} %param.5), kind=kLoop, calls=%fused_computation | loop fusion | flops 64 | bytes 384 | tf_op jit(solution)/shard_map/broadcast_in_dim | solution.py:229
  13.8 0.0 collective-permute-done.1.refs_1_
  13.8 0.0 collective-permute-done.refs_2_
  13.8 0.0 copy-start
  13.8 0.9 %copy-done = bf16[128,1,1024]{2,0,1:T(8,128)(2,1)S(1)} copy-done((bf16[128,1,1024]{2,0,1:T(8,128)(2,1)S(1)}, bf16[128,1,1024]{2,0,1:T(8,128)(2,1)}, u32[]{:S(2)}) %copy-start) | copy-done | bytes 262168
  14.7 0.0 copy-start.1
  14.7 0.7 %copy-done.1 = s32[4,2]{0,1:T(2,128)S(1)} copy-done((s32[4,2]{0,1:T(2,128)S(1)}, s32[4,2]{0,1:T(2,128)}, u32[]{:S(2)}) %copy-start.1) | copy-done | bytes 56
  15.4 1.5 %shard_map.46 = (bf16[2,256,256]{2,1,0:T(8,128)(2,1)S(1)}, bf16[5,128,2048]{2,1,0:T(8,128)(2,1)S(1)}, bf16[5,2,2,1088,128]{4,3,2,1,0:T(8,128)(2,1)S(1)}) custom-call(s32[2,4]{1,0:T(2,128)S(1)} %bitcast.12, s32[1]{0:T(128)S(6)} %copy.13.count_ref, f32[1,64]{1,0:T(1,128)S(1)} %bitcast_convert_fusion.taps_ref, bf16[128,1024]{1,0:T(8,128)(2,1)S(1)} %bitcast.11, ...), custom_call_target="tpu_custom_call" | custom-call | flops 1 | bytes 1 | tf_op jit(solution)/shard_map/pallas_call | solution.py:248
  16.9 0.1 collective-permute-start.8
  17.0 1.0 %collective-permute-done.6.refs_2_ = bf16[128,1024]{1,0:T(8,128)(2,1)S(1)} collective-permute-done((bf16[128,1024]{1,0:T(8,128)(2,1)}, bf16[128,1024]{1,0:T(8,128)(2,1)S(1)}, u32[]{:S(2)}, u32[]{:S(2)}) %collective-permute-start.6) | collective-permute-done | bytes 262176 | tf_op jit(solution)/shard_map/ppermute | solution.py:26
  17.9 0.0 collective-permute-start.7
  18.0 0.9 %collective-permute-done.4.refs_1_ = bf16[128,1024]{1,0:T(8,128)(2,1)S(1)} collective-permute-done((bf16[128,1024]{1,0:T(8,128)(2,1)}, bf16[128,1024]{1,0:T(8,128)(2,1)S(1)}, u32[]{:S(2)}, u32[]{:S(2)}) %collective-permute-start.4) | collective-permute-done | bytes 262176 | tf_op jit(solution)/shard_map/ppermute | solution.py:26
  18.9 0.0 collective-permute-start.5
  18.9 0.0 collective-permute-done.2.refs_0_
  18.9 0.5 %collective-permute-start.3 = (bf16[128,1024]{1,0:T(8,128)(2,1)S(1)}, bf16[128,1024]{1,0:T(8,128)(2,1)S(1)}, u32[]{:S(2)}, u32[]{:S(2)}) collective-permute-start(bf16[128,1024]{1,0:T(8,128)(2,1)S(1)} %collective-permute-done.2.refs_0_), channel_id=1, source_target_pairs={{0,1},{1,0},{2,3},{3,2},{4,5},{5,4},{6,7},{7,6},{8,9},{9,8},{10,11... | collective-permute-start | bytes 786440 | tf_op jit(solution)/shard_map/ppermute | solution.py:26
  19.4 0.0 collective-permute-done.8.refs_3_
  19.4 1.0 %shard_map.47 = (bf16[5,128,2048]{2,1,0:T(8,128)(2,1)S(1)}, bf16[5,2,2,1088,128]{4,3,2,1,0:T(8,128)(2,1)S(1)}) custom-call(bf16[2,256,256]{2,1,0:T(8,128)(2,1)S(1)} %get-tuple-element.14.band_ref, bf16[128,1024]{1,0:T(8,128)(2,1)S(1)} %collective-permute-done.2.refs_0_, ...), custom_call_target="tpu_custom_call", output_to_operand_aliasing={{0}: (5, {}), {1}: (6, {})} | custom-call | flops 1 | bytes 1 | tf_op jit(solution)/shard_map/pallas_call | solution.py:258
  20.4 0.0 collective-permute-done.7.refs_2_
  20.4 0.0 collective-permute-done.5.refs_1_
  20.4 0.4 %collective-permute-done.3.refs_0_ = bf16[128,1024]{1,0:T(8,128)(2,1)S(1)} collective-permute-done((bf16[128,1024]{1,0:T(8,128)(2,1)S(1)}, bf16[128,1024]{1,0:T(8,128)(2,1)S(1)}, u32[]{:S(2)}, u32[]{:S(2)}) %collective-permute-start.3) | collective-permute-done | bytes 262176 | tf_op jit(solution)/shard_map/ppermute | solution.py:26
  20.8 0.0 copy-done.2
  20.8 12.3 %shard_map.48 = (bf16[5,128,2048]{2,1,0:T(8,128)(2,1)S(1)}, bf16[5,2,2,1088,128]{4,3,2,1,0:T(8,128)(2,1)S(1)}, f32[4,65,64,128]{3,2,1,0:T(8,128)}) custom-call(s32[2,4]{1,0:T(2,128)S(1)} %bitcast.13, s32[1]{0:T(128)S(6)} %copy.13.count_ref, bf16[2,256,256]{2,1,0:T(8,128)(2,1)S(1)} %get-tuple-element.14.band_ref, ...), custom_call_target="tpu_custom_call", output_to_operand_aliasing={{0}: (6, {}), {1}: (7, {})} | custom-call | flops 8724152320 | bytes 8519680 | tf_op jit(solution)/shard_map/pallas_call | solution.py:275
Async XLA Ops:
  0.0 20.8 %copy-start.2 = (s32[4,2]{0,1:T(2,128)S(1)}, s32[4,2]{0,1:T(2,128)}, u32[]{:S(2)}) copy-start(s32[4,2]{0,1:T(2,128)} %param.6) | copy-start | bytes 100
  0.0 13.8 %collective-permute-start.1 = (bf16[128,1024]{1,0:T(8,128)(2,1)}, bf16[128,1024]{1,0:T(8,128)(2,1)S(1)}, u32[]{:S(2)}, u32[]{:S(2)}) collective-permute-start(bf16[128,1024]{1,0:T(8,128)(2,1)} %bitcast.6), channel_id=1, source_target_pairs={{0,1},{1,0},{2,3},{3,2},{4,5},{5,4},{6,7},{7,6},{8,9},{9,8},{10,11... | collective-permute-start | bytes 786440 | tf_op jit(solution)/shard_map/ppermute | solution.py:26
  0.5 13.3 %collective-permute-start = (bf16[128,1024]{1,0:T(8,128)(2,1)}, bf16[128,1024]{1,0:T(8,128)(2,1)S(1)}, u32[]{:S(2)}, u32[]{:S(2)}) collective-permute-start(bf16[128,1024]{1,0:T(8,128)(2,1)} %bitcast.7), channel_id=1, source_target_pairs={{2,4},{4,2},{6,8},{8,6},{10,12},{12,10},{3,5},{5,3},{7,9},{9,7},{1... | collective-permute-start | bytes 786440 | tf_op jit(solution)/shard_map/ppermute | solution.py:26
  1.1 16.8 %collective-permute-start.6 = (bf16[128,1024]{1,0:T(8,128)(2,1)}, bf16[128,1024]{1,0:T(8,128)(2,1)S(1)}, u32[]{:S(2)}, u32[]{:S(2)}) collective-permute-start(bf16[128,1024]{1,0:T(8,128)(2,1)} %bitcast.8), channel_id=1, source_target_pairs={{0,2},{2,0},{4,6},{6,4},{8,10},{10,8},{12,14},{14,12},{1,3},{3,1},... | collective-permute-start | bytes 786440 | tf_op jit(solution)/shard_map/ppermute | solution.py:26
  6.6 12.3 %collective-permute-start.4 = (bf16[128,1024]{1,0:T(8,128)(2,1)}, bf16[128,1024]{1,0:T(8,128)(2,1)S(1)}, u32[]{:S(2)}, u32[]{:S(2)}) collective-permute-start(bf16[128,1024]{1,0:T(8,128)(2,1)} %bitcast.9), channel_id=1, source_target_pairs={{4,0},{6,2},{8,4},{10,6},{12,8},{14,10},{5,1},{7,3},{9,5},{11,7},{... | collective-permute-start | bytes 786440 | tf_op jit(solution)/shard_map/ppermute | solution.py:26
  7.9 11.0 %collective-permute-start.2 = (bf16[128,1024]{1,0:T(8,128)(2,1)}, bf16[128,1024]{1,0:T(8,128)(2,1)S(1)}, u32[]{:S(2)}, u32[]{:S(2)}) collective-permute-start(bf16[128,1024]{1,0:T(8,128)(2,1)} %bitcast.10), channel_id=1, source_target_pairs={{0,4},{2,6},{4,8},{6,10},{8,12},{10,14},{1,5},{3,7},{5,9},{7,11},{... | collective-permute-start | bytes 786440 | tf_op jit(solution)/shard_map/ppermute | solution.py:26
  13.8 1.0 %copy-start = (bf16[128,1,1024]{2,0,1:T(8,128)(2,1)S(1)}, bf16[128,1,1024]{2,0,1:T(8,128)(2,1)}, u32[]{:S(2)}) copy-start(bf16[128,1,1024]{2,0,1:T(8,128)(2,1)} %param.4) | copy-start | bytes 786436
  14.7 0.7 %copy-start.1 = (s32[4,2]{0,1:T(2,128)S(1)}, s32[4,2]{0,1:T(2,128)}, u32[]{:S(2)}) copy-start(s32[4,2]{0,1:T(2,128)} %param.6) | copy-start | bytes 100
  16.9 2.5 %collective-permute-start.8 = (bf16[128,1024]{1,0:T(8,128)(2,1)S(1)}, bf16[128,1024]{1,0:T(8,128)(2,1)S(1)}, u32[]{:S(2)}, u32[]{:S(2)}) collective-permute-start(bf16[128,1024]{1,0:T(8,128)(2,1)S(1)} %collective-permute-done.refs_2_), channel_id=1, source_target_pairs={{0,1},{1,0},{2,3},{3,2},{4,5},{5,4},{6,7},{7,6},{8,9},{9,8},{10,11... | collective-permute-start | bytes 786440 | tf_op jit(solution)/shard_map/ppermute | solution.py:26
  17.9 2.5 %collective-permute-start.7 = (bf16[128,1024]{1,0:T(8,128)(2,1)S(1)}, bf16[128,1024]{1,0:T(8,128)(2,1)S(1)}, u32[]{:S(2)}, u32[]{:S(2)}) collective-permute-start(bf16[128,1024]{1,0:T(8,128)(2,1)S(1)} %collective-permute-done.6.refs_2_), channel_id=1, source_target_pairs={{0,1},{1,0},{2,3},{3,2},{4,5},{5,4},{6,7},{7,6},{8,9},{9,8},{10,11... | collective-permute-start | bytes 786440 | tf_op jit(solution)/shard_map/ppermute | solution.py:26
  18.9 1.5 %collective-permute-start.5 = (bf16[128,1024]{1,0:T(8,128)(2,1)S(1)}, bf16[128,1024]{1,0:T(8,128)(2,1)S(1)}, u32[]{:S(2)}, u32[]{:S(2)}) collective-permute-start(bf16[128,1024]{1,0:T(8,128)(2,1)S(1)} %collective-permute-done.4.refs_1_), channel_id=1, source_target_pairs={{0,1},{1,0},{2,3},{3,2},{4,5},{5,4},{6,7},{7,6},{8,9},{9,8},{10,11... | collective-permute-start | bytes 786440 | tf_op jit(solution)/shard_map/ppermute | solution.py:26
  18.9 1.9 %collective-permute-start.3 = (bf16[128,1024]{1,0:T(8,128)(2,1)S(1)}, bf16[128,1024]{1,0:T(8,128)(2,1)S(1)}, u32[]{:S(2)}, u32[]{:S(2)}) collective-permute-start(bf16[128,1024]{1,0:T(8,128)(2,1)S(1)} %collective-permute-done.2.refs_0_), channel_id=1, source_target_pairs={{0,1},{1,0},{2,3},{3,2},{4,5},{5,4},{6,7},{7,6},{8,9},{9,8},{10,11... | collective-permute-start | bytes 786440 | tf_op jit(solution)/shard_map/ppermute | solution.py:26

commit v12 on v10

--- a/solution.py
+++ b/solution.py
@@ -165,45 +165,48 @@
     slots, lags, half_rows, _ = out_ref.shape
     owner = lax.axis_index("chan")
 
-    def ready(slot):
+    def ready(slot, side, sign):
         if slot < slots:
             source = place_of(pairs_ref[0, slot], owner)
+            prepare(source, sign, unit_ref, left_ref.at[slot % 2, side], half_rows)
+
+    def piece(slot, side):
+        span = pl.ds(LAG, lags - LAG) if side == 0 else pl.ds(0, LAG)
+        return pltpu.make_async_copy(
+            stage_ref.at[slot, span], out_ref.at[slot, span], sems.at[slot, side]
+        )
+
+    for side, sign in enumerate((1, -1)):
+        ready(0, side, sign)
+    for slot in range(slots):
+
+        @pl.when(slot < count_ref[0])
+        def _():
+            source = place_of(pairs_ref[0, slot], owner)
+            partner = place_of(pairs_ref[1, slot], owner)
             for side, sign in enumerate((1, -1)):
-                prepare(source, sign, unit_ref, left_ref.at[slot % 2, side], half_rows)
-
-    copies = []
-
-    def send(slot, first, count):
-        span = pl.ds(first, count)
-        copy = pltpu.make_async_copy(
-            stage_ref.at[slot, span], out_ref.at[slot, span], sems.at[len(copies)]
-        )
-        copy.start()
-        copies.append(copy)
-
-    ready(0)
+                ready(slot + 1, side, sign)
+                correlate(
+                    sign, scale, partner, left_ref.at[slot % 2, side], tall_ref,
+                    stage_ref.at[slot],
+                )
+                if sign > 0:
+                    stage_ref[slot, LAG] = scale * jnp.dot(
+                        own_rows(source, unit_ref, half_rows, slice(None)),
+                        coarse_columns(tall_ref, partner, [0]),
+                        preferred_element_type=jnp.float32,
+                    )
+                piece(slot, side).start()
+
+        @pl.when(slot >= count_ref[0])
+        def _():
+            stage_ref[slot] = jnp.zeros(stage_ref.shape[1:], jnp.float32)
+            for side in range(2):
+                piece(slot, side).start()
+
     for slot in range(slots):
-        ready(slot + 1)
-        factor = jnp.where(slot < count_ref[0], scale, 0.0)
-        source = place_of(pairs_ref[0, slot], owner)
-        partner = place_of(pairs_ref[1, slot], owner)
-        for side, sign in enumerate((1, -1)):
-            correlate(
-                sign, factor, partner, left_ref.at[slot % 2, side], tall_ref, stage_ref.at[slot]
-            )
-            if sign > 0:
-                stage_ref[slot, LAG] = factor * jnp.dot(
-                    own_rows(source, unit_ref, half_rows, slice(None)),
-                    coarse_columns(tall_ref, partner, [0]), preferred_element_type=jnp.float32,
-                )
-                if slot == slots - 1:
-                    send(slot, LAG, lags - LAG)
-        if slot == slots - 1:
-            send(slot, 0, LAG)
-        else:
-            send(slot, 0, lags)
-    for copy in copies:
-        copy.wait()
+        for side in range(2):
+            piece(slot, side).wait()
 
 
 def body(traces, fir_taps, pair_blocks, pair_count):
@@ -276,7 +279,7 @@
         scratch_shapes=[
             pltpu.VMEM((2, 2, FINE * half_rows, halves * length), jnp.bfloat16),
             pltpu.VMEM((cap, lags, half_rows, rows), jnp.float32),
-            pltpu.SemaphoreType.DMA((cap + 1,)),
+            pltpu.SemaphoreType.DMA((cap, 2)),
         ],
         compiler_params=params,
         cost_estimate=heavy,

time: 33 us -> 33.5 us (1.015)
  the two profiles are of different devices: /device:TPU:0 before, /device:TPU:25 now
where the time goes in v12:
time: 33.5 us; the launch traced here: 33.3 us
  Pallas kernels  15.8 us (47%)
  starting transfers between devices  10.6 us (32%)
  waiting for transfers between devices  3.86 us (12%)
  local copies, waits for them, and re-layouts  1.63 us (5%)
  between operations  0.72 us (2%)
  other arithmetic  0.66 us (2%)
    pallas_call x1, Pallas kernels, body(): pl.pallas_call(functools.partial(stack_kernel, scale, units), out_shape=(...  13.4 us
    ppermute x9, starting transfers between devices, passed(): return lax.ppermute(block, axis, route)  10.6 us
    ppermute x9, waiting for transfers between devices, passed(): return lax.ppermute(block, axis, route)  3.86 us
    unnamed x6, local copies, waits for them, and re-layouts  1.63 us
    pallas_call x1, Pallas kernels, body(): pl.pallas_call(early_kernel, out_shape=(band_shape, unit_shape, tall_shap...  1.45 us
    pallas_call x1, Pallas kernels, more(): pl.pallas_call(functools.partial(filter_kernel, units), out_shape=(unit_s...  1 us
  transfers between devices with their start and end apart: 9, of which 3 were waited for; matrix products, arithmetic and copies ran while one was open for 2% of the time, Pallas kernels for 7%

profile of v12, /device:TPU:25, one launch (start us, length us, event | category | flops | bytes accessed | tf_op | source)
XLA Modules:
  0.0 33.3 jit_solution(7410568993533275600)
XLA Ops:
  0.0 0.0 copy-start.2
  0.0 0.7 %collective-permute-start.1 = (bf16[128,1024]{1,0:T(8,128)(2,1)}, bf16[128,1024]{1,0:T(8,128)(2,1)S(1)}, u32[]{:S(2)}, u32[]{:S(2)}) collective-permute-start(bf16[128,1024]{1,0:T(8,128)(2,1)} %bitcast.6), channel_id=1, source_target_pairs={{0,1},{1,0},{2,3},{3,2},{4,5},{5,4},{6,7},{7,6},{8,9},{9,8},{10,11... | collective-permute-start | bytes 786440 | tf_op jit(solution)/shard_map/ppermute | solution.py:24
  0.7 3.0 %collective-permute-start = (bf16[128,1024]{1,0:T(8,128)(2,1)}, bf16[128,1024]{1,0:T(8,128)(2,1)S(1)}, u32[]{:S(2)}, u32[]{:S(2)}) collective-permute-start(bf16[128,1024]{1,0:T(8,128)(2,1)} %bitcast.7), channel_id=1, source_target_pairs={{2,4},{4,2},{6,8},{8,6},{10,12},{12,10},{3,5},{5,3},{7,9},{9,7},{1... | collective-permute-start | bytes 786440 | tf_op jit(solution)/shard_map/ppermute | solution.py:24
  3.7 0.1 collective-permute-start.6
  3.8 3.4 %collective-permute-start.4 = (bf16[128,1024]{1,0:T(8,128)(2,1)}, bf16[128,1024]{1,0:T(8,128)(2,1)S(1)}, u32[]{:S(2)}, u32[]{:S(2)}) collective-permute-start(bf16[128,1024]{1,0:T(8,128)(2,1)} %bitcast.9), channel_id=1, source_target_pairs={{4,0},{6,2},{8,4},{10,6},{12,8},{14,10},{5,1},{7,3},{9,5},{11,7},{... | collective-permute-start | bytes 786440 | tf_op jit(solution)/shard_map/ppermute | solution.py:24
  7.2 1.3 %collective-permute-start.2 = (bf16[128,1024]{1,0:T(8,128)(2,1)}, bf16[128,1024]{1,0:T(8,128)(2,1)S(1)}, u32[]{:S(2)}, u32[]{:S(2)}) collective-permute-start(bf16[128,1024]{1,0:T(8,128)(2,1)} %bitcast.10), channel_id=1, source_target_pairs={{0,4},{2,6},{4,8},{6,10},{8,12},{10,14},{1,5},{3,7},{5,9},{7,11},{... | collective-permute-start | bytes 786440 | tf_op jit(solution)/shard_map/ppermute | solution.py:24
  9.2 0.7 %bitcast_convert_fusion.taps_ref = f32[1,64]{1,0:T(1,128)S(1)} fusion(bf16[64]{0:T(256)(128)(2,1)} %param.5), kind=kLoop, calls=%fused_computation | loop fusion | flops 64 | bytes 384 | tf_op jit(solution)/shard_map/broadcast_in_dim | solution.py:227
  9.8 0.0 collective-permute-done.1.refs_1_
  9.8 1.7 %collective-permute-done.refs_2_ = bf16[128,1024]{1,0:T(8,128)(2,1)S(1)} collective-permute-done((bf16[128,1024]{1,0:T(8,128)(2,1)}, bf16[128,1024]{1,0:T(8,128)(2,1)S(1)}, u32[]{:S(2)}, u32[]{:S(2)}) %collective-permute-start) | collective-permute-done | bytes 262176 | tf_op jit(solution)/shard_map/ppermute | solution.py:24
  11.5 0.0 copy-start
  11.5 0.9 %copy-done = bf16[128,1,1024]{2,0,1:T(8,128)(2,1)S(1)} copy-done((bf16[128,1,1024]{2,0,1:T(8,128)(2,1)S(1)}, bf16[128,1,1024]{2,0,1:T(8,128)(2,1)}, u32[]{:S(2)}) %copy-start) | copy-done | bytes 262168
  12.4 0.0 copy-start.1
  12.4 0.7 %copy-done.1 = s32[4,2]{0,1:T(2,128)S(1)} copy-done((s32[4,2]{0,1:T(2,128)S(1)}, s32[4,2]{0,1:T(2,128)}, u32[]{:S(2)}) %copy-start.1) | copy-done | bytes 56
  13.1 1.5 %shard_map.46 = (bf16[2,256,256]{2,1,0:T(8,128)(2,1)S(1)}, bf16[5,128,2048]{2,1,0:T(8,128)(2,1)S(1)}, bf16[5,2,2,1088,128]{4,3,2,1,0:T(8,128)(2,1)S(1)}) custom-call(s32[2,4]{1,0:T(2,128)S(1)} %bitcast.12, s32[1]{0:T(128)S(6)} %copy.13.count_ref, f32[1,64]{1,0:T(1,128)S(1)} %bitcast_convert_fusion.taps_ref, bf16[128,1024]{1,0:T(8,128)(2,1)S(1)} %bitcast.11, ...), custom_call_target="tpu_custom_call" | custom-call | flops 1 | bytes 1 | tf_op jit(solution)/shard_map/pallas_call | solution.py:246
  14.6 1.1 %collective-permute-start.8 = (bf16[128,1024]{1,0:T(8,128)(2,1)S(1)}, bf16[128,1024]{1,0:T(8,128)(2,1)S(1)}, u32[]{:S(2)}, u32[]{:S(2)}) collective-permute-start(bf16[128,1024]{1,0:T(8,128)(2,1)S(1)} %collective-permute-done.refs_2_), channel_id=1, source_target_pairs={{0,1},{1,0},{2,3},{3,2},{4,5},{5,4},{6,7},{7,6},{8,9},{9,8},{10,11... | collective-permute-start | bytes 786440 | tf_op jit(solution)/shard_map/ppermute | solution.py:24
  15.7 1.8 %collective-permute-done.6.refs_2_ = bf16[128,1024]{1,0:T(8,128)(2,1)S(1)} collective-permute-done((bf16[128,1024]{1,0:T(8,128)(2,1)}, bf16[128,1024]{1,0:T(8,128)(2,1)S(1)}, u32[]{:S(2)}, u32[]{:S(2)}) %collective-permute-start.6) | collective-permute-done | bytes 262176 | tf_op jit(solution)/shard_map/ppermute | solution.py:24
  17.5 0.5 %collective-permute-start.7 = (bf16[128,1024]{1,0:T(8,128)(2,1)S(1)}, bf16[128,1024]{1,0:T(8,128)(2,1)S(1)}, u32[]{:S(2)}, u32[]{:S(2)}) collective-permute-start(bf16[128,1024]{1,0:T(8,128)(2,1)S(1)} %collective-permute-done.6.refs_2_), channel_id=1, source_target_pairs={{0,1},{1,0},{2,3},{3,2},{4,5},{5,4},{6,7},{7,6},{8,9},{9,8},{10,11... | collective-permute-start | bytes 786440 | tf_op jit(solution)/shard_map/ppermute | solution.py:24
  18.0 0.0 collective-permute-done.4.refs_1_
  18.0 0.0 collective-permute-start.5
  18.0 0.0 collective-permute-done.2.refs_0_
  18.0 0.5 %collective-permute-start.3 = (bf16[128,1024]{1,0:T(8,128)(2,1)S(1)}, bf16[128,1024]{1,0:T(8,128)(2,1)S(1)}, u32[]{:S(2)}, u32[]{:S(2)}) collective-permute-start(bf16[128,1024]{1,0:T(8,128)(2,1)S(1)} %collective-permute-done.2.refs_0_), channel_id=1, source_target_pairs={{0,1},{1,0},{2,3},{3,2},{4,5},{5,4},{6,7},{7,6},{8,9},{9,8},{10,11... | collective-permute-start | bytes 786440 | tf_op jit(solution)/shard_map/ppermute | solution.py:24
  18.5 0.0 collective-permute-done.8.refs_3_
  18.5 1.0 %shard_map.47 = (bf16[5,128,2048]{2,1,0:T(8,128)(2,1)S(1)}, bf16[5,2,2,1088,128]{4,3,2,1,0:T(8,128)(2,1)S(1)}) custom-call(bf16[2,256,256]{2,1,0:T(8,128)(2,1)S(1)} %get-tuple-element.14.band_ref, bf16[128,1024]{1,0:T(8,128)(2,1)S(1)} %collective-permute-done.2.refs_0_, ...), custom_call_target="tpu_custom_call", output_to_operand_aliasing={{0}: (5, {}), {1}: (6, {})} | custom-call | flops 1 | bytes 1 | tf_op jit(solution)/shard_map/pallas_call | solution.py:256
  19.5 0.0 collective-permute-done.7.refs_2_
  19.6 0.0 collective-permute-done.5.refs_1_
  19.6 0.4 %collective-permute-done.3.refs_0_ = bf16[128,1024]{1,0:T(8,128)(2,1)S(1)} collective-permute-done((bf16[128,1024]{1,0:T(8,128)(2,1)S(1)}, bf16[128,1024]{1,0:T(8,128)(2,1)S(1)}, u32[]{:S(2)}, u32[]{:S(2)}) %collective-permute-start.3) | collective-permute-done | bytes 262176 | tf_op jit(solution)/shard_map/ppermute | solution.py:24
  19.9 0.0 copy-done.2
  19.9 13.4 %shard_map.48 = (bf16[5,128,2048]{2,1,0:T(8,128)(2,1)S(1)}, bf16[5,2,2,1088,128]{4,3,2,1,0:T(8,128)(2,1)S(1)}, f32[4,65,64,128]{3,2,1,0:T(8,128)}) custom-call(s32[2,4]{1,0:T(2,128)S(1)} %bitcast.13, s32[1]{0:T(128)S(6)} %copy.13.count_ref, bf16[2,256,256]{2,1,0:T(8,128)(2,1)S(1)} %get-tuple-element.14.band_ref, ...), custom_call_target="tpu_custom_call", output_to_operand_aliasing={{0}: (6, {}), {1}: (7, {})} | custom-call | flops 8724152320 | bytes 8519680 | tf_op jit(solution)/shard_map/pallas_call | solution.py:273
Async XLA Ops:
  0.0 19.9 %copy-start.2 = (s32[4,2]{0,1:T(2,128)S(1)}, s32[4,2]{0,1:T(2,128)}, u32[]{:S(2)}) copy-start(s32[4,2]{0,1:T(2,128)} %param.6) | copy-start | bytes 100
  0.0 9.8 %collective-permute-start.1 = (bf16[128,1024]{1,0:T(8,128)(2,1)}, bf16[128,1024]{1,0:T(8,128)(2,1)S(1)}, u32[]{:S(2)}, u32[]{:S(2)}) collective-permute-start(bf16[128,1024]{1,0:T(8,128)(2,1)} %bitcast.6), channel_id=1, source_target_pairs={{0,1},{1,0},{2,3},{3,2},{4,5},{5,4},{6,7},{7,6},{8,9},{9,8},{10,11... | collective-permute-start | bytes 786440 | tf_op jit(solution)/shard_map/ppermute | solution.py:24
  0.7 10.8 %collective-permute-start = (bf16[128,1024]{1,0:T(8,128)(2,1)}, bf16[128,1024]{1,0:T(8,128)(2,1)S(1)}, u32[]{:S(2)}, u32[]{:S(2)}) collective-permute-start(bf16[128,1024]{1,0:T(8,128)(2,1)} %bitcast.7), channel_id=1, source_target_pairs={{2,4},{4,2},{6,8},{8,6},{10,12},{12,10},{3,5},{5,3},{7,9},{9,7},{1... | collective-permute-start | bytes 786440 | tf_op jit(solution)/shard_map/ppermute | solution.py:24
  3.7 13.8 %collective-permute-start.6 = (bf16[128,1024]{1,0:T(8,128)(2,1)}, bf16[128,1024]{1,0:T(8,128)(2,1)S(1)}, u32[]{:S(2)}, u32[]{:S(2)}) collective-permute-start(bf16[128,1024]{1,0:T(8,128)(2,1)} %bitcast.8), channel_id=1, source_target_pairs={{0,2},{2,0},{4,6},{6,4},{8,10},{10,8},{12,14},{14,12},{1,3},{3,1},... | collective-permute-start | bytes 786440 | tf_op jit(solution)/shard_map/ppermute | solution.py:24
  3.8 14.2 %collective-permute-start.4 = (bf16[128,1024]{1,0:T(8,128)(2,1)}, bf16[128,1024]{1,0:T(8,128)(2,1)S(1)}, u32[]{:S(2)}, u32[]{:S(2)}) collective-permute-start(bf16[128,1024]{1,0:T(8,128)(2,1)} %bitcast.9), channel_id=1, source_target_pairs={{4,0},{6,2},{8,4},{10,6},{12,8},{14,10},{5,1},{7,3},{9,5},{11,7},{... | collective-permute-start | bytes 786440 | tf_op jit(solution)/shard_map/ppermute | solution.py:24
  7.2 10.8 %collective-permute-start.2 = (bf16[128,1024]{1,0:T(8,128)(2,1)}, bf16[128,1024]{1,0:T(8,128)(2,1)S(1)}, u32[]{:S(2)}, u32[]{:S(2)}) collective-permute-start(bf16[128,1024]{1,0:T(8,128)(2,1)} %bitcast.10), channel_id=1, source_target_pairs={{0,4},{2,6},{4,8},{6,10},{8,12},{10,14},{1,5},{3,7},{5,9},{7,11},{... | collective-permute-start | bytes 786440 | tf_op jit(solution)/shard_map/ppermute | solution.py:24
  11.5 1.0 %copy-start = (bf16[128,1,1024]{2,0,1:T(8,128)(2,1)S(1)}, bf16[128,1,1024]{2,0,1:T(8,128)(2,1)}, u32[]{:S(2)}) copy-start(bf16[128,1,1024]{2,0,1:T(8,128)(2,1)} %param.4) | copy-start | bytes 786436
  12.4 0.7 %copy-start.1 = (s32[4,2]{0,1:T(2,128)S(1)}, s32[4,2]{0,1:T(2,128)}, u32[]{:S(2)}) copy-start(s32[4,2]{0,1:T(2,128)} %param.6) | copy-start | bytes 100
  14.6 4.0 %collective-permute-start.8 = (bf16[128,1024]{1,0:T(8,128)(2,1)S(1)}, bf16[128,1024]{1,0:T(8,128)(2,1)S(1)}, u32[]{:S(2)}, u32[]{:S(2)}) collective-permute-start(bf16[128,1024]{1,0:T(8,128)(2,1)S(1)} %collective-permute-done.refs_2_), channel_id=1, source_target_pairs={{0,1},{1,0},{2,3},{3,2},{4,5},{5,4},{6,7},{7,6},{8,9},{9,8},{10,11... | collective-permute-start | bytes 786440 | tf_op jit(solution)/shard_map/ppermute | solution.py:24
  17.5 2.0 %collective-permute-start.7 = (bf16[128,1024]{1,0:T(8,128)(2,1)S(1)}, bf16[128,1024]{1,0:T(8,128)(2,1)S(1)}, u32[]{:S(2)}, u32[]{:S(2)}) collective-permute-start(bf16[128,1024]{1,0:T(8,128)(2,1)S(1)} %collective-permute-done.6.refs_2_), channel_id=1, source_target_pairs={{0,1},{1,0},{2,3},{3,2},{4,5},{5,4},{6,7},{7,6},{8,9},{9,8},{10,11... | collective-permute-start | bytes 786440 | tf_op jit(solution)/shard_map/ppermute | solution.py:24
  18.0 1.5 %collective-permute-start.5 = (bf16[128,1024]{1,0:T(8,128)(2,1)S(1)}, bf16[128,1024]{1,0:T(8,128)(2,1)S(1)}, u32[]{:S(2)}, u32[]{:S(2)}) collective-permute-start(bf16[128,1024]{1,0:T(8,128)(2,1)S(1)} %collective-permute-done.4.refs_1_), channel_id=1, source_target_pairs={{0,1},{1,0},{2,3},{3,2},{4,5},{5,4},{6,7},{7,6},{8,9},{9,8},{10,11... | collective-permute-start | bytes 786440 | tf_op jit(solution)/shard_map/ppermute | solution.py:24
  18.0 1.9 %collective-permute-start.3 = (bf16[128,1024]{1,0:T(8,128)(2,1)S(1)}, bf16[128,1024]{1,0:T(8,128)(2,1)S(1)}, u32[]{:S(2)}, u32[]{:S(2)}) collective-permute-start(bf16[128,1024]{1,0:T(8,128)(2,1)S(1)} %collective-permute-done.2.refs_0_), channel_id=1, source_target_pairs={{0,1},{1,0},{2,3},{3,2},{4,5},{5,4},{6,7},{7,6},{8,9},{9,8},{10,11... | collective-permute-start | bytes 786440 | tf_op jit(solution)/shard_map/ppermute | solution.py:24

commit v13 on v10

--- a/solution.py
+++ b/solution.py
@@ -129,9 +129,9 @@
     )
 
 
-def correlate(sign, factor, partner, left_ref, tall_ref, stage_ref):
+def correlate(sign, places, factor, partner, left_ref, tall_ref, stage_ref):
     half_rows, channels = stage_ref.shape[1:]
-    amounts = [sign * FINE * place for place in range(COARSE)]
+    amounts = [sign * FINE * place for place in places]
     result = jnp.dot(
         left_ref[...], coarse_columns(tall_ref, partner, amounts),
         preferred_element_type=jnp.float32,
@@ -187,20 +187,25 @@
         factor = jnp.where(slot < count_ref[0], scale, 0.0)
         source = place_of(pairs_ref[0, slot], owner)
         partner = place_of(pairs_ref[1, slot], owner)
-        for side, sign in enumerate((1, -1)):
+        last = slot == slots - 1
+        whole = range(COARSE)
+        correlate(
+            1, whole, factor, partner, left_ref.at[slot % 2, 0], tall_ref, stage_ref.at[slot]
+        )
+        stage_ref[slot, LAG] = factor * jnp.dot(
+            own_rows(source, unit_ref, half_rows, slice(None)),
+            coarse_columns(tall_ref, partner, [0]), preferred_element_type=jnp.float32,
+        )
+        if last:
+            send(slot, LAG, lags - LAG)
+        for places in (whole[: COARSE // 2], whole[COARSE // 2 :]) if last else (whole,):
             correlate(
-                sign, factor, partner, left_ref.at[slot % 2, side], tall_ref, stage_ref.at[slot]
+                -1, places, factor, partner, left_ref.at[slot % 2, 1], tall_ref,
+                stage_ref.at[slot],
             )
-            if sign > 0:
-                stage_ref[slot, LAG] = factor * jnp.dot(
-                    own_rows(source, unit_ref, half_rows, slice(None)),
-                    coarse_columns(tall_ref, partner, [0]), preferred_element_type=jnp.float32,
-                )
-                if slot == slots - 1:
-                    send(slot, LAG, lags - LAG)
-        if slot == slots - 1:
-            send(slot, 0, LAG)
-        else:
+            if last:
+                send(slot, LAG - FINE * (places[-1] + 1), FINE * len(places))
+        if not last:
             send(slot, 0, lags)
     for copy in copies:
         copy.wait()
@@ -276,7 +281,7 @@
         scratch_shapes=[
             pltpu.VMEM((2, 2, FINE * half_rows, halves * length), jnp.bfloat16),
             pltpu.VMEM((cap, lags, half_rows, rows), jnp.float32),
-            pltpu.SemaphoreType.DMA((cap + 1,)),
+            pltpu.SemaphoreType.DMA((cap + 2,)),
         ],
         compiler_params=params,
         cost_estimate=heavy,

time: 33 us -> 33 us (level)
  no operation moved by 1% of the time
where the time goes in v13:
time: 33 us; the launch traced here: 32.8 us
  Pallas kernels  14.4 us (44%)
  starting transfers between devices  13.1 us (40%)
  waiting for transfers between devices  2.27 us (7%)
  local copies, waits for them, and re-layouts  1.63 us (5%)
  between operations  0.72 us (2%)
  other arithmetic  0.66 us (2%)
    ppermute x9, starting transfers between devices, passed(): return lax.ppermute(block, axis, route)  13.1 us
    pallas_call x1, Pallas kernels, body(): pl.pallas_call(functools.partial(stack_kernel, scale, units), out_shape=(...  12 us
    ppermute x9, waiting for transfers between devices, passed(): return lax.ppermute(block, axis, route)  2.27 us
    unnamed x6, local copies, waits for them, and re-layouts  1.63 us
    pallas_call x1, Pallas kernels, body(): pl.pallas_call(early_kernel, out_shape=(band_shape, unit_shape, tall_shap...  1.46 us
    pallas_call x1, Pallas kernels, more(): pl.pallas_call(functools.partial(filter_kernel, units), out_shape=(unit_s...  1 us
  transfers between devices with their start and end apart: 9, of which 3 were waited for; matrix products, arithmetic and copies ran while one was open for 2% of the time, Pallas kernels for 7%

profile of v13, /device:TPU:0, one launch (start us, length us, event | category | flops | bytes accessed | tf_op | source)
XLA Modules:
  0.0 32.8 jit_solution(10378281608445577002)
XLA Ops:
  0.0 0.0 copy-start.2
  0.0 0.5 %collective-permute-start.1 = (bf16[128,1024]{1,0:T(8,128)(2,1)}, bf16[128,1024]{1,0:T(8,128)(2,1)S(1)}, u32[]{:S(2)}, u32[]{:S(2)}) collective-permute-start(bf16[128,1024]{1,0:T(8,128)(2,1)} %bitcast.6), channel_id=1, source_target_pairs={{0,1},{1,0},{2,3},{3,2},{4,5},{5,4},{6,7},{7,6},{8,9},{9,8},{10,11... | collective-permute-start | bytes 786440 | tf_op jit(solution)/shard_map/ppermute | solution.py:24
  0.5 0.7 %collective-permute-start = (bf16[128,1024]{1,0:T(8,128)(2,1)}, bf16[128,1024]{1,0:T(8,128)(2,1)S(1)}, u32[]{:S(2)}, u32[]{:S(2)}) collective-permute-start(bf16[128,1024]{1,0:T(8,128)(2,1)} %bitcast.7), channel_id=1, source_target_pairs={{2,4},{4,2},{6,8},{8,6},{10,12},{12,10},{3,5},{5,3},{7,9},{9,7},{1... | collective-permute-start | bytes 786440 | tf_op jit(solution)/shard_map/ppermute | solution.py:24
  1.1 5.5 %collective-permute-start.6 = (bf16[128,1024]{1,0:T(8,128)(2,1)}, bf16[128,1024]{1,0:T(8,128)(2,1)S(1)}, u32[]{:S(2)}, u32[]{:S(2)}) collective-permute-start(bf16[128,1024]{1,0:T(8,128)(2,1)} %bitcast.8), channel_id=1, source_target_pairs={{0,2},{2,0},{4,6},{6,4},{8,10},{10,8},{12,14},{14,12},{1,3},{3,1},... | collective-permute-start | bytes 786440 | tf_op jit(solution)/shard_map/ppermute | solution.py:24
  6.6 1.3 %collective-permute-start.4 = (bf16[128,1024]{1,0:T(8,128)(2,1)}, bf16[128,1024]{1,0:T(8,128)(2,1)S(1)}, u32[]{:S(2)}, u32[]{:S(2)}) collective-permute-start(bf16[128,1024]{1,0:T(8,128)(2,1)} %bitcast.9), channel_id=1, source_target_pairs={{4,0},{6,2},{8,4},{10,6},{12,8},{14,10},{5,1},{7,3},{9,5},{11,7},{... | collective-permute-start | bytes 786440 | tf_op jit(solution)/shard_map/ppermute | solution.py:24
  7.9 4.6 %collective-permute-start.2 = (bf16[128,1024]{1,0:T(8,128)(2,1)}, bf16[128,1024]{1,0:T(8,128)(2,1)S(1)}, u32[]{:S(2)}, u32[]{:S(2)}) collective-permute-start(bf16[128,1024]{1,0:T(8,128)(2,1)} %bitcast.10), channel_id=1, source_target_pairs={{0,4},{2,6},{4,8},{6,10},{8,12},{10,14},{1,5},{3,7},{5,9},{7,11},{... | collective-permute-start | bytes 786440 | tf_op jit(solution)/shard_map/ppermute | solution.py:24
  13.1 0.7 %bitcast_convert_fusion.taps_ref = f32[1,64]{1,0:T(1,128)S(1)} fusion(bf16[64]{0:T(256)(128)(2,1)} %param.5), kind=kLoop, calls=%fused_computation | loop fusion | flops 64 | bytes 384 | tf_op jit(solution)/shard_map/broadcast_in_dim | solution.py:229
  13.8 0.0 collective-permute-done.1.refs_1_
  13.8 0.0 collective-permute-done.refs_2_
  13.8 0.0 copy-start
  13.8 0.9 %copy-done = bf16[128,1,1024]{2,0,1:T(8,128)(2,1)S(1)} copy-done((bf16[128,1,1024]{2,0,1:T(8,128)(2,1)S(1)}, bf16[128,1,1024]{2,0,1:T(8,128)(2,1)}, u32[]{:S(2)}) %copy-start) | copy-done | bytes 262168
  14.7 0.0 copy-start.1
  14.7 0.7 %copy-done.1 = s32[4,2]{0,1:T(2,128)S(1)} copy-done((s32[4,2]{0,1:T(2,128)S(1)}, s32[4,2]{0,1:T(2,128)}, u32[]{:S(2)}) %copy-start.1) | copy-done | bytes 56
  15.4 1.5 %shard_map.46 = (bf16[2,256,256]{2,1,0:T(8,128)(2,1)S(1)}, bf16[5,128,2048]{2,1,0:T(8,128)(2,1)S(1)}, bf16[5,2,2,1088,128]{4,3,2,1,0:T(8,128)(2,1)S(1)}) custom-call(s32[2,4]{1,0:T(2,128)S(1)} %bitcast.12, s32[1]{0:T(128)S(6)} %copy.13.count_ref, f32[1,64]{1,0:T(1,128)S(1)} %bitcast_convert_fusion.taps_ref, bf16[128,1024]{1,0:T(8,128)(2,1)S(1)} %bitcast.11, ...), custom_call_target="tpu_custom_call" | custom-call | flops 1 | bytes 1 | tf_op jit(solution)/shard_map/pallas_call | solution.py:248
  16.9 0.1 collective-permute-start.8
  17.0 1.0 %collective-permute-done.6.refs_2_ = bf16[128,1024]{1,0:T(8,128)(2,1)S(1)} collective-permute-done((bf16[128,1024]{1,0:T(8,128)(2,1)}, bf16[128,1024]{1,0:T(8,128)(2,1)S(1)}, u32[]{:S(2)}, u32[]{:S(2)}) %collective-permute-start.6) | collective-permute-done | bytes 262176 | tf_op jit(solution)/shard_map/ppermute | solution.py:24
  17.9 0.0 collective-permute-start.7
  18.0 0.9 %collective-permute-done.4.refs_1_ = bf16[128,1024]{1,0:T(8,128)(2,1)S(1)} collective-permute-done((bf16[128,1024]{1,0:T(8,128)(2,1)}, bf16[128,1024]{1,0:T(8,128)(2,1)S(1)}, u32[]{:S(2)}, u32[]{:S(2)}) %collective-permute-start.4) | collective-permute-done | bytes 262176 | tf_op jit(solution)/shard_map/ppermute | solution.py:24
  18.9 0.0 collective-permute-start.5
  18.9 0.0 collective-permute-done.2.refs_0_
  18.9 0.5 %collective-permute-start.3 = (bf16[128,1024]{1,0:T(8,128)(2,1)S(1)}, bf16[128,1024]{1,0:T(8,128)(2,1)S(1)}, u32[]{:S(2)}, u32[]{:S(2)}) collective-permute-start(bf16[128,1024]{1,0:T(8,128)(2,1)S(1)} %collective-permute-done.2.refs_0_), channel_id=1, source_target_pairs={{0,1},{1,0},{2,3},{3,2},{4,5},{5,4},{6,7},{7,6},{8,9},{9,8},{10,11... | collective-permute-start | bytes 786440 | tf_op jit(solution)/shard_map/ppermute | solution.py:24
  19.4 0.0 collective-permute-done.8.refs_3_
  19.4 1.0 %shard_map.47 = (bf16[5,128,2048]{2,1,0:T(8,128)(2,1)S(1)}, bf16[5,2,2,1088,128]{4,3,2,1,0:T(8,128)(2,1)S(1)}) custom-call(bf16[2,256,256]{2,1,0:T(8,128)(2,1)S(1)} %get-tuple-element.14.band_ref, bf16[128,1024]{1,0:T(8,128)(2,1)S(1)} %collective-permute-done.2.refs_0_, ...), custom_call_target="tpu_custom_call", output_to_operand_aliasing={{0}: (5, {}), {1}: (6, {})} | custom-call | flops 1 | bytes 1 | tf_op jit(solution)/shard_map/pallas_call | solution.py:258
  20.4 0.0 collective-permute-done.7.refs_2_
  20.4 0.0 collective-permute-done.5.refs_1_
  20.4 0.4 %collective-permute-done.3.refs_0_ = bf16[128,1024]{1,0:T(8,128)(2,1)S(1)} collective-permute-done((bf16[128,1024]{1,0:T(8,128)(2,1)S(1)}, bf16[128,1024]{1,0:T(8,128)(2,1)S(1)}, u32[]{:S(2)}, u32[]{:S(2)}) %collective-permute-start.3) | collective-permute-done | bytes 262176 | tf_op jit(solution)/shard_map/ppermute | solution.py:24
  20.8 0.0 copy-done.2
  20.8 12.0 %shard_map.48 = (bf16[5,128,2048]{2,1,0:T(8,128)(2,1)S(1)}, bf16[5,2,2,1088,128]{4,3,2,1,0:T(8,128)(2,1)S(1)}, f32[4,65,64,128]{3,2,1,0:T(8,128)}) custom-call(s32[2,4]{1,0:T(2,128)S(1)} %bitcast.13, s32[1]{0:T(128)S(6)} %copy.13.count_ref, bf16[2,256,256]{2,1,0:T(8,128)(2,1)S(1)} %get-tuple-element.14.band_ref, ...), custom_call_target="tpu_custom_call", output_to_operand_aliasing={{0}: (6, {}), {1}: (7, {})} | custom-call | flops 8724152320 | bytes 8519680 | tf_op jit(solution)/shard_map/pallas_call | solution.py:275
Async XLA Ops:
  0.0 20.8 %copy-start.2 = (s32[4,2]{0,1:T(2,128)S(1)}, s32[4,2]{0,1:T(2,128)}, u32[]{:S(2)}) copy-start(s32[4,2]{0,1:T(2,128)} %param.6) | copy-start | bytes 100
  0.0 13.8 %collective-permute-start.1 = (bf16[128,1024]{1,0:T(8,128)(2,1)}, bf16[128,1024]{1,0:T(8,128)(2,1)S(1)}, u32[]{:S(2)}, u32[]{:S(2)}) collective-permute-start(bf16[128,1024]{1,0:T(8,128)(2,1)} %bitcast.6), channel_id=1, source_target_pairs={{0,1},{1,0},{2,3},{3,2},{4,5},{5,4},{6,7},{7,6},{8,9},{9,8},{10,11... | collective-permute-start | bytes 786440 | tf_op jit(solution)/shard_map/ppermute | solution.py:24
  0.5 13.3 %collective-permute-start = (bf16[128,1024]{1,0:T(8,128)(2,1)}, bf16[128,1024]{1,0:T(8,128)(2,1)S(1)}, u32[]{:S(2)}, u32[]{:S(2)}) collective-permute-start(bf16[128,1024]{1,0:T(8,128)(2,1)} %bitcast.7), channel_id=1, source_target_pairs={{2,4},{4,2},{6,8},{8,6},{10,12},{12,10},{3,5},{5,3},{7,9},{9,7},{1... | collective-permute-start | bytes 786440 | tf_op jit(solution)/shard_map/ppermute | solution.py:24
  1.1 16.8 %collective-permute-start.6 = (bf16[128,1024]{1,0:T(8,128)(2,1)}, bf16[128,1024]{1,0:T(8,128)(2,1)S(1)}, u32[]{:S(2)}, u32[]{:S(2)}) collective-permute-start(bf16[128,1024]{1,0:T(8,128)(2,1)} %bitcast.8), channel_id=1, source_target_pairs={{0,2},{2,0},{4,6},{6,4},{8,10},{10,8},{12,14},{14,12},{1,3},{3,1},... | collective-permute-start | bytes 786440 | tf_op jit(solution)/shard_map/ppermute | solution.py:24
  6.6 12.3 %collective-permute-start.4 = (bf16[128,1024]{1,0:T(8,128)(2,1)}, bf16[128,1024]{1,0:T(8,128)(2,1)S(1)}, u32[]{:S(2)}, u32[]{:S(2)}) collective-permute-start(bf16[128,1024]{1,0:T(8,128)(2,1)} %bitcast.9), channel_id=1, source_target_pairs={{4,0},{6,2},{8,4},{10,6},{12,8},{14,10},{5,1},{7,3},{9,5},{11,7},{... | collective-permute-start | bytes 786440 | tf_op jit(solution)/shard_map/ppermute | solution.py:24
  7.9 11.0 %collective-permute-start.2 = (bf16[128,1024]{1,0:T(8,128)(2,1)}, bf16[128,1024]{1,0:T(8,128)(2,1)S(1)}, u32[]{:S(2)}, u32[]{:S(2)}) collective-permute-start(bf16[128,1024]{1,0:T(8,128)(2,1)} %bitcast.10), channel_id=1, source_target_pairs={{0,4},{2,6},{4,8},{6,10},{8,12},{10,14},{1,5},{3,7},{5,9},{7,11},{... | collective-permute-start | bytes 786440 | tf_op jit(solution)/shard_map/ppermute | solution.py:24
  13.8 1.0 %copy-start = (bf16[128,1,1024]{2,0,1:T(8,128)(2,1)S(1)}, bf16[128,1,1024]{2,0,1:T(8,128)(2,1)}, u32[]{:S(2)}) copy-start(bf16[128,1,1024]{2,0,1:T(8,128)(2,1)} %param.4) | copy-start | bytes 786436
  14.7 0.7 %copy-start.1 = (s32[4,2]{0,1:T(2,128)S(1)}, s32[4,2]{0,1:T(2,128)}, u32[]{:S(2)}) copy-start(s32[4,2]{0,1:T(2,128)} %param.6) | copy-start | bytes 100
  16.9 2.5 %collective-permute-start.8 = (bf16[128,1024]{1,0:T(8,128)(2,1)S(1)}, bf16[128,1024]{1,0:T(8,128)(2,1)S(1)}, u32[]{:S(2)}, u32[]{:S(2)}) collective-permute-start(bf16[128,1024]{1,0:T(8,128)(2,1)S(1)} %collective-permute-done.refs_2_), channel_id=1, source_target_pairs={{0,1},{1,0},{2,3},{3,2},{4,5},{5,4},{6,7},{7,6},{8,9},{9,8},{10,11... | collective-permute-start | bytes 786440 | tf_op jit(solution)/shard_map/ppermute | solution.py:24
  17.9 2.5 %collective-permute-start.7 = (bf16[128,1024]{1,0:T(8,128)(2,1)S(1)}, bf16[128,1024]{1,0:T(8,128)(2,1)S(1)}, u32[]{:S(2)}, u32[]{:S(2)}) collective-permute-start(bf16[128,1024]{1,0:T(8,128)(2,1)S(1)} %collective-permute-done.6.refs_2_), channel_id=1, source_target_pairs={{0,1},{1,0},{2,3},{3,2},{4,5},{5,4},{6,7},{7,6},{8,9},{9,8},{10,11... | collective-permute-start | bytes 786440 | tf_op jit(solution)/shard_map/ppermute | solution.py:24
  18.9 1.5 %collective-permute-start.5 = (bf16[128,1024]{1,0:T(8,128)(2,1)S(1)}, bf16[128,1024]{1,0:T(8,128)(2,1)S(1)}, u32[]{:S(2)}, u32[]{:S(2)}) collective-permute-start(bf16[128,1024]{1,0:T(8,128)(2,1)S(1)} %collective-permute-done.4.refs_1_), channel_id=1, source_target_pairs={{0,1},{1,0},{2,3},{3,2},{4,5},{5,4},{6,7},{7,6},{8,9},{9,8},{10,11... | collective-permute-start | bytes 786440 | tf_op jit(solution)/shard_map/ppermute | solution.py:24
  18.9 1.9 %collective-permute-start.3 = (bf16[128,1024]{1,0:T(8,128)(2,1)S(1)}, bf16[128,1024]{1,0:T(8,128)(2,1)S(1)}, u32[]{:S(2)}, u32[]{:S(2)}) collective-permute-start(bf16[128,1024]{1,0:T(8,128)(2,1)S(1)} %collective-permute-done.2.refs_0_), channel_id=1, source_target_pairs={{0,1},{1,0},{2,3},{3,2},{4,5},{5,4},{6,7},{7,6},{8,9},{9,8},{10,11... | collective-permute-start | bytes 786440 | tf_op jit(solution)/shard_map/ppermute | solution.py:24
